TPU v7x, 32 devices: a whole 2x2x4 slice. The times are simulated.
32 devices in a mesh: row: 2 (over x), col: 16 (over z, y, core).
Axes of the slice: x: 2, y: 2, z: 4, core: 2. Of those that a mesh axis runs over, the one named last changes fastest.
Arguments:
- layer_input: bfloat16 [5120, 3072], P(('row', 'col')), may hold values from -0.119628906 to 0.119628906
- queries: bfloat16 [5120, 128], P(('row', 'col')), may hold values from -7 to 7
- key_states: bfloat16 [5120, 128], P(('row', 'col')), may hold values from -7 to 7
- value_states: bfloat16 [5120, 128], P(('row', 'col')), may hold values from -6 to 6
- forward_out: bfloat16 [5120, 128], P(('row', 'col')), may hold values from -1.5 to 1.5
- out_grad: bfloat16 [5120, 128], P(('row', 'col')), may hold values from -12 to 12
- token_pos: int32 [5120], replicated, may hold values from 0 to 5119, as said below
- block_sample: int32 [40], replicated, may hold values from 0 to 4, never falling along the last dimension, each value on 1 to 20 neighbouring positions
Outputs:
- query_grad: bfloat16 [5120, 128], P(('row', 'col'))
- key_grad: bfloat16 [5120, 128], P(('row', 'col'))
- value_grad: bfloat16 [5120, 128], P(('row', 'col'))
- weight_grad: float32 [3072, 384], P('col')
Inputs may be any that keep to these rules, and one draw needn't show every extreme that they name: `token_pos`: each packed position appears in exactly one slot. `block_sample`: never falling along the blocks; every sample spans 1 to 20 blocks and one spans exactly 20.
All inputs are finite; a program needn't handle non-finite values.
Results may differ from a plain program's by a relative error of at most 0.019.
Values may be sent and summed in bfloat16 or wider, within the bound.
No kernel may reach another device: no remote copies, remote signals or barrier semaphores. Data moves between devices by JAX's collectives and lax.ppermute only.
A program may use at most 64 MiB of HBM per device.

v0:
```python
import math

import jax
import jax.numpy as jnp
from jax import lax
from jax.sharding import PartitionSpec as P

BLK = 128


NEG_FILL = -1e30


def joined(part, axis, combine):
    gathered = jax.tree.map(lambda a: lax.all_gather(a, axis), part)

    def take(source):
        return jax.tree.map(lambda a: lax.dynamic_index_in_dim(a, source, 0, False), gathered)

    return lax.fori_loop(
        1, lax.axis_size(axis), lambda source, state: combine(state, take(source)), take(0)
    )


def sample_of(positions, block_sample):
    block_index = positions // BLK
    block_ids = jnp.arange(block_sample.shape[0], dtype=jnp.int32)
    matches = block_index[:, None] == block_ids[None, :]
    return jnp.sum(jnp.where(matches, block_sample[None, :], 0), axis=1)


def local(
    layer_input, queries, key_states, value_states, forward_out, out_grad, token_pos, block_sample
):
    token_count = queries.shape[0]
    head_width = queries.shape[1]
    score_scale = 1.0 / math.sqrt(head_width)
    col_count = lax.axis_size("col")
    row_count = lax.axis_size("row")
    row_id = lax.axis_index("row")
    col_id = lax.axis_index("col")
    query_rows, grad_rows, output_rows = (
        lax.all_gather(queries, "col", axis=0, tiled=True),
        lax.all_gather(out_grad, "col", axis=0, tiled=True),
        lax.all_gather(forward_out, "col", axis=0, tiled=True),
    )
    key_rows, value_rows = (
        lax.all_gather(key_states, "row", axis=0, tiled=True),
        lax.all_gather(value_states, "row", axis=0, tiled=True),
    )
    query_count = query_rows.shape[0]
    block_rows = math.gcd(query_count, 512)
    block_count = query_count // block_rows
    query_pos = lax.dynamic_slice_in_dim(token_pos, row_id * query_count, query_count)
    key_pos = lax.dynamic_index_in_dim(
        token_pos.reshape(row_count, col_count, token_count), col_id, axis=1, keepdims=False
    ).reshape(-1)
    key_sample = sample_of(key_pos, block_sample)
    query_blocks = query_rows.reshape(block_count, block_rows, head_width)
    grad_blocks = grad_rows.reshape(block_count, block_rows, head_width)
    output_blocks = output_rows.reshape(block_count, block_rows, head_width)
    query_samples = lax.map(
        lambda pos_block: sample_of(pos_block, block_sample),
        query_pos.reshape(block_count, block_rows),
    )

    def masked_scores(query_block, sample_block):
        scores = (
            lax.dot_general(
                query_block, key_rows, (((1,), (1,)), ((), ())), preferred_element_type=jnp.float32
            )
            * score_scale
        )
        live_pairs = sample_block[:, None] == key_sample[None, :]
        return (jnp.where(live_pairs, scores, NEG_FILL), live_pairs)

    def local_stats(running, inputs):
        scores, live_pairs = masked_scores(inputs[0], inputs[1])
        peak_rows = jnp.max(scores, axis=1)
        row_sum = jnp.sum(jnp.where(live_pairs, jnp.exp(scores - peak_rows[:, None]), 0.0), axis=1)
        return (running, (peak_rows, row_sum))

    unused, (peak_local, total_local) = lax.scan(
        local_stats, jnp.zeros((), jnp.float32), (query_blocks, query_samples)
    )
    peak_local = peak_local.reshape(-1)
    total_local = total_local.reshape(-1)

    def combine_stats(left_stats, right_stats):
        joint_peak = jnp.maximum(left_stats[0], right_stats[0])
        joint_sum = left_stats[1] * jnp.exp(left_stats[0] - joint_peak) + right_stats[1] * jnp.exp(
            right_stats[0] - joint_peak
        )
        return (joint_peak, joint_sum)

    row_peak, row_total = joined((peak_local, total_local), "col", combine_stats)

    def backward_block(running, inputs):
        key_acc, value_acc = running
        query_block, grad_block, output_block, sample_block, peak_block, total_block = inputs
        scores, live_pairs = masked_scores(query_block, sample_block)
        prob_rows = (
            jnp.where(live_pairs, jnp.exp(scores - peak_block[:, None]), 0.0) / total_block[:, None]
        )
        prob_low = prob_rows.astype(jnp.bfloat16)
        value_acc = value_acc + lax.dot_general(
            prob_low, grad_block, (((0,), (0,)), ((), ())), preferred_element_type=jnp.float32
        )
        prob_grad = lax.dot_general(
            grad_block, value_rows, (((1,), (1,)), ((), ())), preferred_element_type=jnp.float32
        )
        row_delta = jnp.sum(
            grad_block.astype(jnp.float32) * output_block.astype(jnp.float32), axis=1
        )
        score_grad = (prob_rows * (prob_grad - row_delta[:, None])).astype(jnp.bfloat16)
        query_part = jnp.dot(score_grad, key_rows, preferred_element_type=jnp.float32) * score_scale
        key_step = (
            lax.dot_general(
                score_grad,
                query_block,
                (((0,), (0,)), ((), ())),
                preferred_element_type=jnp.float32,
            )
            * score_scale
        )
        return ((key_acc + key_step, value_acc), query_part)

    zero_keys = jnp.zeros((key_rows.shape[0], head_width), jnp.float32)
    (key_part, value_part), query_parts = lax.scan(
        backward_block,
        (zero_keys, zero_keys),
        (
            query_blocks,
            grad_blocks,
            output_blocks,
            query_samples,
            row_peak.reshape(block_count, block_rows),
            row_total.reshape(block_count, block_rows),
        ),
    )
    query_grad = lax.psum_scatter(
        query_parts.reshape(query_count, head_width).astype(jnp.bfloat16),
        "col",
        scatter_dimension=0,
        tiled=True,
    )
    key_sum, value_sum = (
        lax.psum_scatter(
            key_part.astype(jnp.bfloat16), "row", scatter_dimension=0, tiled=True
        ).astype(jnp.float32),
        lax.psum_scatter(
            value_part.astype(jnp.bfloat16), "row", scatter_dimension=0, tiled=True
        ).astype(jnp.float32),
    )
    key_grad = key_sum.astype(jnp.bfloat16)
    value_grad = value_sum.astype(jnp.bfloat16)
    all_grads = jnp.concatenate([query_grad, key_grad, value_grad], axis=1)
    model_width = layer_input.shape[1]
    piece_rows = model_width // (row_count * col_count)
    split_input = layer_input.reshape(token_count, col_count, row_count, piece_rows)
    partial_value = jnp.einsum(
        "tcrp,tk->rcpk", split_input, all_grads, preferred_element_type=jnp.float32
    )
    partial_value = partial_value.reshape(row_count * col_count, piece_rows, 3 * head_width)
    own_piece = lax.psum_scatter(partial_value, ("row", "col"), scatter_dimension=0, tiled=True)
    weight_grad = lax.all_gather(own_piece, "row", axis=0, tiled=True).reshape(
        row_count * piece_rows, 3 * head_width
    )
    return (query_grad, key_grad, value_grad, weight_grad)


def solution(mesh):
    return jax.shard_map(
        local,
        mesh=mesh,
        in_specs=(
            P(("row", "col"), None),
            P(("row", "col"), None),
            P(("row", "col"), None),
            P(("row", "col"), None),
            P(("row", "col"), None),
            P(("row", "col"), None),
            P(),
            P(),
        ),
        out_specs=(
            P(("row", "col"), None),
            P(("row", "col"), None),
            P(("row", "col"), None),
            P("col", None),
        ),
        check_vma=False,
    )
```

profile of v0, /device:TPU:0, one launch (start us, length us, event | category | flops | bytes accessed | tf_op | source)
XLA Modules:
  0.0 349.0 jit_solution(12475567057849155152)
XLA Ops:
  7.3 0.8 reshape.126
  8.1 0.8 dynamic_slice.67
  8.9 4.3 %while.56 = (s32[]{:T(128)}, s32[5,512]{1,0:T(8,128)S(1)}, s32[5,512]{1,0:T(8,128)S(1)}, s32[40]{0:T(128)}, s32[]{:T(128)}, /*index=5*/s32[]{:T(128)}) while((s32[]{:T(128)}, s32[5,512]{1,0:T(8,128)S(1)}, s32[5,512]{1,0:T(8,128)S(1)}, s32[40]{0:T(128)}, s32[]{:T(128)}, /*index=5*/s32[]{:T(128)}) %tuple.103), condition=%wide.region_2.3_spmd, body=%wide.region_0.2_spmd.sunk | while | flops 68610 | bytes 16629 | solution.py:62
  8.9 0.7 select_reduce_fusion.3
  9.8 0.7 select_reduce_fusion.3
  10.6 0.7 select_reduce_fusion.3
  11.5 0.7 select_reduce_fusion.3
  12.3 0.7 select_reduce_fusion.3
  13.3 0.7 select_reduce_fusion.1
  14.0 5.8 %all_gather.25 = bf16[320,128]{1,0:T(8,128)(2,1)S(1)} all-gather(bf16[160,128]{1,0:T(8,128)(2,1)} %param.18), channel_id=1, replica_groups=mesh['row'=2,'col'=16] {'row'}, dimensions={0}, use_global_device_ids=true | all-gather | bytes 122880 | tf_op jit(solution)/shard_map/all_gather | solution.py:48
  19.9 24.4 %all_gather.24 = bf16[2560,128]{1,0:T(8,128)(2,1)S(1)} all-gather(bf16[160,128]{1,0:T(8,128)(2,1)} %param.17), channel_id=1, replica_groups=mesh['row'=2,'col'=16] {'col'}, dimensions={0}, use_global_device_ids=true | all-gather | bytes 696320 | tf_op jit(solution)/shard_map/all_gather | solution.py:43
  44.3 3.0 while.57
  47.3 17.9 %all-gather = f32[16,1,2560]{2,1,0:T(1,128)S(1)} all-gather(f32[1,1,2560]{2,1,0:T(1,128)S(1)} %reshape.137), channel_id=1, replica_groups=mesh['row'=2,'col'=16] {'col'}, dimensions={0}, use_global_device_ids=true | all-gather | bytes 174080 | tf_op jit(solution)/shard_map/all_gather | solution.py:15
  65.3 19.2 %all-gather.1 = f32[16,1,2560]{2,1,0:T(1,128)S(1)} all-gather(f32[1,1,2560]{2,1,0:T(1,128)S(1)} %reshape.139), channel_id=1, replica_groups=mesh['row'=2,'col'=16] {'col'}, dimensions={0}, use_global_device_ids=true | all-gather | bytes 174080 | tf_op jit(solution)/shard_map/all_gather | solution.py:15
  84.5 4.7 %all_gather.29 = bf16[320,128]{1,0:T(8,128)(2,1)S(1)} all-gather(bf16[160,128]{1,0:T(8,128)(2,1)S(1)} %copy-done.1), channel_id=1, replica_groups=mesh['row'=2,'col'=16] {'row'}, dimensions={0}, use_global_device_ids=true | all-gather | bytes 122880 | tf_op jit(solution)/shard_map/all_gather | solution.py:49
  89.2 1.7 while.58
  90.9 19.3 %all_gather.30 = bf16[2560,128]{1,0:T(8,128)(2,1)S(1)} all-gather(bf16[160,128]{1,0:T(8,128)(2,1)S(1)} %copy-done.2), channel_id=1, replica_groups=mesh['row'=2,'col'=16] {'col'}, dimensions={0}, use_global_device_ids=true | all-gather | bytes 696320 | tf_op jit(solution)/shard_map/all_gather | solution.py:45
  110.2 20.6 %all_gather.28 = bf16[2560,128]{1,0:T(8,128)(2,1)S(1)} all-gather(bf16[160,128]{1,0:T(8,128)(2,1)S(1)} %copy-done.3), channel_id=1, replica_groups=mesh['row'=2,'col'=16] {'col'}, dimensions={0}, use_global_device_ids=true | all-gather | bytes 696320 | tf_op jit(solution)/shard_map/all_gather | solution.py:44
  130.8 11.6 %while.59 = (s32[]{:T(128)}, f32[320,128]{1,0:T(8,128)S(1)}, f32[320,128]{1,0:T(8,128)S(1)}, bf16[5,512,128]{2,1,0:T(8,128)(2,1)}, s32[5,512]{1,0:T(8,128)S(1)},...) while((s32[]{:T(128)}, f32[320,128]{1,0:T(8,128)S(1)}, ...), condition=%wide.region_12.13_spmd.clone, body=%wide.region_10.12_spmd.clone.sunk | while | flops 211885568 | bytes 4923584 | solution.py:129
  131.0 0.3 fusion.77
  131.9 0.3 fusion.80
  132.2 0.9 fusion.81
  133.3 0.3 fusion.77
  133.7 0.3 convolution_add_fusion.2
  134.2 0.3 fusion.80
  134.5 1.0 fusion.81
  135.6 0.3 fusion.77
  136.5 0.3 fusion.80
  136.8 1.0 fusion.81
  138.0 0.3 fusion.77
  138.3 0.3 convolution_add_fusion.2
  138.9 0.3 fusion.80
  139.2 1.0 fusion.81
  140.3 0.3 fusion.77
  141.2 0.3 fusion.80
  141.5 1.0 fusion.81
  142.4 0.6 convert_element_type.33
  143.2 0.6 convert_element_type.34
  143.9 0.7 reduce-scatter.5.cloned.1.call-update
  144.6 1.3 reshape.133
  146.0 4.5 %reduce-scatter.7.cloned.1.call-done = bf16[160,128]{1,0:T(8,128)(2,1)} async-done(((bf16[320,128]{1,0:T(8,128)(2,1)}), bf16[160,128]{1,0:T(8,128)(2,1)}) %reduce-scatter.7.cloned.1.call-update) | async-done | bytes 40976 | tf_op jit(solution)/shard_map/reduce_scatter | solution.py:148
  150.4 12.7 %reduce-scatter.9.cloned.1.call-done = bf16[160,128]{1,0:T(8,128)(2,1)} async-done(((bf16[320,128]{1,0:T(8,128)(2,1)}), bf16[160,128]{1,0:T(8,128)(2,1)}) %reduce-scatter.9.cloned.1.call-update) | async-done | bytes 40976 | tf_op jit(solution)/shard_map/reduce_scatter | solution.py:151
  163.2 60.3 %reduce-scatter.5.cloned.1.call-done = bf16[160,128]{1,0:T(8,128)(2,1)} async-done(((bf16[2560,128]{1,0:T(8,128)(2,1)}), bf16[160,128]{1,0:T(8,128)(2,1)}) %reduce-scatter.5.cloned.1.call-update) | async-done | bytes 40976 | tf_op jit(solution)/shard_map/reduce_scatter | solution.py:141
  223.5 1.9 convolution_bitcast_fusion
  225.3 2.5 copy.18
  227.8 107.9 %reduce-scatter.11.cloned.1.call-done = f32[1,96,384]{2,1,0:T(8,128)} async-done(((f32[32,96,384]{2,1,0:T(8,128)}), f32[1,96,384]{2,1,0:T(8,128)}) %reduce-scatter.11.cloned.1.call-update) | async-done | bytes 147472 | tf_op jit(solution)/shard_map/reduce_scatter | solution.py:165
  335.8 6.0 %all_gather.31 = f32[2,96,384]{2,1,0:T(8,128)S(1)} all-gather(f32[1,96,384]{2,1,0:T(8,128)} %reduce-scatter.11.cloned.1.call-done), channel_id=1, replica_groups=mesh['row'=2,'col'=16] {'row'}, dimensions={0}, use_global_device_ids=true | all-gather | bytes 442368 | tf_op jit(solution)/shard_map/all_gather | solution.py:166
  341.8 0.7 copy.69
  (126 shorter events, 7.8 us)
Async XLA Ops:
  7.2 143.3 %reduce-scatter.7.cloned.1.call-start = ((), (), s32[]{:S(2)}) async-start(), calls=%async_computation.5 | async-start | bytes 122880 | tf_op jit(solution)/shard_map/reduce_scatter | solution.py:148
  44.3 40.3 %copy-start.1 = (bf16[160,128]{1,0:T(8,128)(2,1)S(1)}, bf16[160,128]{1,0:T(8,128)(2,1)}, u32[]{:S(2)}) copy-start(bf16[160,128]{1,0:T(8,128)(2,1)} %param.19) | copy-start | bytes 122884
  47.3 43.7 %copy-start.2 = (bf16[160,128]{1,0:T(8,128)(2,1)S(1)}, bf16[160,128]{1,0:T(8,128)(2,1)}, u32[]{:S(2)}) copy-start(bf16[160,128]{1,0:T(8,128)(2,1)} %param.20) | copy-start | bytes 122884
  65.2 45.0 %copy-start.3 = (bf16[160,128]{1,0:T(8,128)(2,1)S(1)}, bf16[160,128]{1,0:T(8,128)(2,1)}, u32[]{:S(2)}) copy-start(bf16[160,128]{1,0:T(8,128)(2,1)} %param.21) | copy-start | bytes 122884
  142.4 2.2 copy-start
  143.1 20.1 %reduce-scatter.9.cloned.1.call-start = ((), (), s32[]{:S(2)}) async-start(), calls=%async_computation.6 | async-start | bytes 122880 | tf_op jit(solution)/shard_map/reduce_scatter | solution.py:151
  143.9 79.6 %reduce-scatter.5.cloned.1.call-start = ((), (), s32[]{:S(2)}) async-start(), calls=%async_computation.4 | async-start | bytes 696320 | tf_op jit(solution)/shard_map/reduce_scatter | solution.py:141
  144.6 191.2 %reduce-scatter.11.cloned.1.call-start = ((), (), s32[]{:S(2)}) async-start(), calls=%async_computation.7 | async-start | bytes 4866048 | tf_op jit(solution)/shard_map/reduce_scatter | solution.py:165
Sparse Core Ops, SparseCore 0:
  143.2 7.1 reduce-scatter.6
  153.2 9.9 reduce-scatter.8
  167.3 56.1 reduce-scatter.4
  229.7 106.0 reduce-scatter.10
where the time goes:
time: 350 us; the launch traced here: 349 us
  waiting for transfers between devices  186 us (53%)
  blocking collectives  118 us (34%)
  between operations  13.9 us (4%)
  matrix products  13.7 us (4%)
  local copies, waits for them, and re-layouts  8.42 us (2%)
  other arithmetic  7.61 us (2%)
    reduce_scatter x1, waiting for transfers between devices, local(): lax.psum_scatter(partial_value, ('row', 'col'), scatter_dimension=0, tile...  108 us
    reduce_scatter x1, waiting for transfers between devices, local(): lax.psum_scatter(query_parts.reshape(query_count, head_width).astype(jnp....  60.3 us
    all_gather x2, blocking collectives, joined(): gathered = jax.tree.map(lambda a: lax.all_gather(a, axis), part)  37.1 us
    all_gather x1, blocking collectives, local(): lax.all_gather(queries, 'col', axis=0, tiled=True)  24.4 us
    all_gather x1, blocking collectives, local(): lax.all_gather(out_grad, 'col', axis=0, tiled=True)  20.6 us
    all_gather x1, blocking collectives, local(): lax.all_gather(forward_out, 'col', axis=0, tiled=True)  19.3 us
    reduce_scatter x1, waiting for transfers between devices, local(): lax.psum_scatter(value_part.astype(jnp.bfloat16), 'row', scatter_dimensio...  12.7 us
  transfers between devices with their start and end apart: 4, of which 4 were waited for; matrix products, arithmetic and copies ran while one was open for 1% of the time, Pallas kernels for 0%

commit v1 on v0

v1 whole, which is shorter than its diff:
```python
import functools
import math

import jax
import jax.numpy as jnp
from jax import lax
from jax.experimental import pallas as pl
from jax.experimental.pallas import tpu as pltpu
from jax.sharding import Mesh
from jax.sharding import PartitionSpec as P

BLK = 128
LANES = 128
PAD_ROWS = 16
NEG_FILL = -1e30
LOG2E = math.log2(math.e)
MIB = 1 << 20
F32 = jnp.float32
BF16 = jnp.bfloat16
VMEM = pl.BlockSpec(memory_space=pltpu.VMEM)
SMEM = pl.BlockSpec(memory_space=pltpu.SMEM)


def dot_nt(left, right, precision=None):
    return lax.dot_general(
        left, right, (((1,), (1,)), ((), ())), preferred_element_type=F32, precision=precision
    )


def dot_tn(left, right):
    return lax.dot_general(left, right, (((0,), (0,)), ((), ())), preferred_element_type=F32)


def params(nbytes):
    return pltpu.CompilerParams(vmem_limit_bytes=nbytes)


def split_three(values):
    high = values.astype(BF16).astype(F32)
    rest = values - high
    middle = rest.astype(BF16).astype(F32)
    return high, middle, rest - middle


def pack_kernel(axes, q_ref, k_ref, v_ref, o_ref, g_ref, pos_ref, ids_ref, qg_ref, kv_ref, prod, extra):
    count, width = q_ref.shape
    me = jnp.int32(0)
    for name, size in axes:
        me = me * size + lax.axis_index(name)
    qg_ref[:count, :width] = q_ref[...]
    qg_ref[:count, width:] = g_ref[...]
    kv_ref[:count, :width] = k_ref[...]
    kv_ref[:count, width:] = v_ref[...]
    prod[...] = jnp.zeros_like(prod)
    prod[:count, :] = g_ref[...].astype(F32) * o_ref[...].astype(F32)
    delta = dot_nt(
        jnp.ones((PAD_ROWS, width), F32), prod[...], precision=lax.Precision.HIGHEST
    )
    high, middle, low = split_three(delta)
    row = lax.broadcasted_iota(jnp.int32, delta.shape, 0)
    extra[...] = jnp.where(row == 0, high, jnp.where(row == 1, middle, jnp.where(row == 2, low, 0.0)))
    block = pos_ref[pl.ds(me, 1), :] // BLK

    def add_id(index, found):
        return jnp.where(block == index, ids_ref[index], found)

    found = lax.fori_loop(0, ids_ref.shape[0], add_id, jnp.zeros_like(block))
    extra[3:4, :count] = found.astype(F32)
    tail = extra[...].astype(BF16)
    qg_ref[count:, :] = tail
    kv_ref[count:, :] = tail


def forward_kernel(count, width, n_q, n_kv, *refs):
    qg_refs, refs = refs[:n_q], refs[n_q:]
    kv_refs, refs = refs[:n_kv], refs[n_kv:]
    w_ref, u_ref, stat_ref, own_ref, refs = *refs[:4], refs[4:]
    send_refs, (queries, grads, keys, rows) = refs[: n_q - 1], refs[n_q - 1 :]
    total = n_q * count
    factor = LOG2E / math.sqrt(width)
    for slot, ref in enumerate(qg_refs):
        queries[slot * count : (slot + 1) * count, :] = ref[:count, :width]
        grads[slot * count : (slot + 1) * count, :] = ref[:count, width:]
        tail = ref[count:, :].astype(F32)
        rows[0:1, slot * count : (slot + 1) * count] = (tail[0:1] + tail[1:2] + tail[2:3])[:, :count]
        rows[1:2, slot * count : (slot + 1) * count] = tail[3:4, :count]
    delta = rows[0:1, :]
    query_ids = rows[1:2, :]

    def over_pieces(body, state):
        base = 0
        for ref in kv_refs:
            depth = ref.shape[0]
            if depth == 1:
                state = body(ref.at[0], base, state)
            else:
                state = lax.fori_loop(
                    0, depth, lambda i, s, ref=ref, base=base: body(ref.at[i], base + i, s), state
                )
            base += depth
        return state

    def scores_of(ref):
        key_ids = jnp.transpose(ref[count:, :].astype(F32))[:count, 3:4]
        scores = dot_nt(ref[:count, :width], queries[...]) * factor
        return jnp.where(key_ids == query_ids, scores, NEG_FILL)

    def fold(values, combine):
        out = values[0:8]
        for start in range(8, count, 8):
            out = combine(out, values[start : start + 8])
        return out

    def peak_step(ref, index, peak):
        return jnp.maximum(peak, fold(scores_of(ref), jnp.maximum))

    peak8 = over_pieces(peak_step, jnp.full((8, total), NEG_FILL, F32))
    peak = jnp.max(peak8, axis=0, keepdims=True)

    def grad_step(ref, index, mass):
        weight = jnp.exp2(scores_of(ref) - peak)
        w_ref[index] = weight.astype(BF16)
        prob_grad = dot_nt(ref[:count, width:], grads[...])
        u_ref[index] = (weight * (prob_grad - delta)).astype(BF16)
        keys[index] = ref[:count, :width]
        return mass + fold(weight, jnp.add)

    mass8 = over_pieces(grad_step, jnp.zeros((8, total), F32))
    mass = jnp.sum(mass8, axis=0, keepdims=True)
    level = peak + jnp.log2(mass)
    stat_ref[...] = jnp.zeros_like(stat_ref)
    stat_ref[0:1, :] = peak
    stat_ref[1:2, :] = level

    n_pieces = keys.shape[0]
    if n_pieces <= 8:
        joined = dot_tn(
            keys[...].reshape(n_pieces * count, width), u_ref[...].reshape(n_pieces * count, total)
        )
    else:
        joined = lax.fori_loop(
            0,
            n_pieces,
            lambda i, s: s + dot_tn(keys[i], u_ref[i]),
            jnp.zeros((width, total), F32),
        )
    query_part = jnp.transpose(joined / mass)
    own_ref[...] = query_part[:count]
    chunks = total // LANES
    parts = split_three(level)
    tail_rows = send_refs[0].shape[0] - count
    lines = [part[:, c * LANES : (c + 1) * LANES] for part in parts for c in range(chunks)]
    row = lax.broadcasted_iota(jnp.int32, (tail_rows, LANES), 0)
    tail = jnp.zeros((tail_rows, LANES), F32)
    for place, line in enumerate(lines):
        tail = jnp.where(row == place, line, tail)
    tail = tail.astype(BF16)
    for slot, ref in enumerate(send_refs, 1):
        ref[:count, :] = query_part[slot * count : (slot + 1) * count].astype(BF16)
        ref[count:, :] = tail


def backward_kernel(count, width, n_q, *refs):
    w_ref, u_ref, stat_ref, own_ref, refs = *refs[:4], refs[4:]
    qg_refs, refs = refs[:n_q], refs[n_q:]
    got_refs, refs = refs[: n_q - 1], refs[n_q - 1 :]
    mine_ref, other_ref, dq_ref, queries, grads = refs
    total = n_q * count
    chunks = total // LANES
    scale = 1.0 / math.sqrt(width)
    stat = jnp.transpose(stat_ref[...])
    peak, level = stat[:, 0:1], stat[:, 1:2]
    levels = [[level[s * count : (s + 1) * count] for s in range(n_q)]]
    for offset, ref in enumerate(got_refs, 1):
        tail = ref[count:, :].astype(F32)
        summed = tail[:chunks] + tail[chunks : 2 * chunks] + tail[2 * chunks : 3 * chunks]
        summed = jnp.concatenate([summed, jnp.zeros((-chunks % 8, LANES), F32)], axis=0)
        across = jnp.transpose(summed)
        column = jnp.concatenate([across[:, c : c + 1] for c in range(chunks)], axis=0)
        levels.append(
            [column[(s ^ offset) * count : ((s ^ offset) + 1) * count] for s in range(n_q)]
        )
    for slot in range(n_q):
        here = [one[slot] for one in levels]
        top = functools.reduce(jnp.maximum, here)
        shares = [jnp.exp2(one - top) for one in here]
        mass = functools.reduce(jnp.add, shares)
        rows = slice(slot * count, (slot + 1) * count)
        share = jnp.exp2(peak[rows] - top) / mass
        queries[rows, :] = (qg_refs[slot][:count, :width].astype(F32) * share).astype(BF16)
        grads[rows, :] = (qg_refs[slot][:count, width:].astype(F32) * share).astype(BF16)
        if slot == 0:
            query_grad = own_ref[...] * shares[0]
            for one, ref in zip(shares[1:], got_refs):
                query_grad = query_grad + ref[:count, :].astype(F32) * one
            dq_ref[...] = (query_grad * (scale / mass)).astype(BF16)

    n_pieces = w_ref.shape[0]
    half = n_pieces // 2

    def emit(first, size, ref, place):
        many = (size * count, total)
        value_part = jnp.dot(
            w_ref[pl.ds(first, size)].reshape(many), grads[...], preferred_element_type=F32
        )
        key_part = jnp.dot(
            u_ref[pl.ds(first, size)].reshape(many), queries[...], preferred_element_type=F32
        )
        shape = (size, count, width)
        ref[pl.ds(place, size), :, :width] = (key_part * scale).reshape(shape).astype(ref.dtype)
        ref[pl.ds(place, size), :, width:] = value_part.reshape(shape).astype(ref.dtype)

    if half <= 4:
        emit(half, half, other_ref, 0)
        emit(0, half, mine_ref, 0)
    else:

        @pl.loop(0, half)
        def _(i):
            emit(half + i, 1, other_ref, i)
            emit(i, 1, mine_ref, i)


def weight_kernel(n_pairs, *refs):
    x_refs, refs = refs[:n_pairs], refs[n_pairs:]
    g_refs, refs = refs[:n_pairs], refs[n_pairs:]
    mine_ref, other_ref, sums = refs
    total = None
    for x_ref, g_ref in zip(x_refs, g_refs):
        part = dot_tn(x_ref[...], g_ref[...])
        total = part if total is None else total + part
    sums[...] = total.reshape(sums.shape)
    z_id, core_id = lax.axis_index("z"), lax.axis_index("core")
    for slot in range(sums.shape[1]):
        mine_ref[slot] = sums[core_id, z_id ^ slot]
        other_ref[slot] = sums[core_id ^ 1, z_id ^ slot].astype(other_ref.dtype)


def xor_permute(value, names, offsets):
    sizes = [lax.axis_size(name) for name in names]
    pairs = []
    for source in range(math.prod(sizes)):
        rest, digits = source, []
        for size in reversed(sizes):
            digits.append(rest % size)
            rest //= size
        target = 0
        for digit, size, offset in zip(reversed(digits), sizes, offsets):
            target = target * size + (digit ^ offset)
        pairs.append((source, target))
    return lax.ppermute(value, tuple(names), pairs)


def local(axes, layer_input, queries, keys, values, forward_out, out_grad, token_pos, block_sample):
    sizes = dict(axes)
    n_row, n_z, n_y, n_core = (sizes[name] for name in ("row", "z", "y", "core"))
    count, width = queries.shape
    model_width = layer_input.shape[1]
    total = n_z * count
    plane = [(a, b) for a in range(n_row) for b in range(n_y)]
    n_plane = len(plane)
    n_pieces = n_core * n_plane

    def over_plane(value, where):
        return xor_permute(value, ("row", "y"), where)

    def over_z(value, offset):
        return xor_permute(value, ("z",), (offset,))

    def over_core(value):
        return xor_permute(value, ("core",), (1,))

    packed = jax.ShapeDtypeStruct((count + PAD_ROWS, 2 * width), BF16)
    qg, kv = pl.pallas_call(
        functools.partial(pack_kernel, axes),
        out_shape=(packed, packed),
        in_specs=[VMEM] * 6 + [SMEM],
        out_specs=(VMEM, VMEM),
        scratch_shapes=[
            pltpu.VMEM((2 * width, width), F32),
            pltpu.VMEM((PAD_ROWS, 2 * width), F32),
        ],
        compiler_params=params(8 * MIB),
        name="pack",
    )(queries, keys, values, forward_out, out_grad, token_pos.reshape(-1, count), block_sample)

    kv_near = [kv] + [over_plane(kv, where) for where in plane[1:]]
    qg_all = [qg] + [over_z(qg, offset) for offset in range(1, n_z)]
    kv_all = kv_near + [over_core(piece) for piece in kv_near]
    if n_pieces <= 8:
        kv_all = [piece[None] for piece in kv_all]
    else:
        kv_all = [jnp.stack(kv_all)]

    blk = model_width // (n_z * n_y * n_core * n_row)
    row_id, y_id = lax.axis_index("row"), lax.axis_index("y")
    split_input = layer_input.reshape(count, n_z, n_y, n_core, n_row, blk)
    split_input = split_input.transpose(4, 2, 0, 3, 1, 5).reshape(n_plane, count, -1)
    x_send = [
        lax.dynamic_index_in_dim(split_input, (row_id ^ a) * n_y + (y_id ^ b), 0, False)
        for a, b in plane
    ]
    x_all = [x_send[0]] + [over_plane(x, where) for x, where in zip(x_send[1:], plane[1:])]

    mass_rows = 3 * total // LANES
    tail_rows = -(-mass_rows // PAD_ROWS) * PAD_ROWS
    big = jax.ShapeDtypeStruct((n_pieces, count, total), BF16)
    w, u, stat, own_part, *send = pl.pallas_call(
        functools.partial(forward_kernel, count, width, n_z, len(kv_all)),
        out_shape=[
            big,
            big,
            jax.ShapeDtypeStruct((8, total), F32),
            jax.ShapeDtypeStruct((count, width), F32),
        ]
        + [jax.ShapeDtypeStruct((count + tail_rows, width), BF16)] * (n_z - 1),
        in_specs=[VMEM] * (n_z + len(kv_all)),
        out_specs=[VMEM] * (4 + n_z - 1),
        scratch_shapes=[
            pltpu.VMEM((total, width), BF16),
            pltpu.VMEM((total, width), BF16),
            pltpu.VMEM((n_pieces, count, width), BF16),
            pltpu.VMEM((8, total), F32),
        ],
        compiler_params=params(16 * MIB if n_pieces <= 8 else 56 * MIB),
        name="forward",
    )(*qg_all, *kv_all)
    got = [over_z(piece, offset) for offset, piece in enumerate(send, 1)]

    mine, other, query_grad = pl.pallas_call(
        functools.partial(backward_kernel, count, width, n_z),
        out_shape=[
            jax.ShapeDtypeStruct((n_pieces // 2, count, 2 * width), F32),
            jax.ShapeDtypeStruct((n_pieces // 2, count, 2 * width), BF16),
            jax.ShapeDtypeStruct((count, width), BF16),
        ],
        in_specs=[VMEM] * (4 + n_z + n_z - 1),
        out_specs=[VMEM] * 3,
        scratch_shapes=[pltpu.VMEM((total, width), BF16), pltpu.VMEM((total, width), BF16)],
        compiler_params=params(16 * MIB if n_pieces <= 8 else 56 * MIB),
        name="backward",
    )(w, u, stat, own_part, *qg_all, *got)

    both = mine + over_core(other).astype(F32)
    kv_sum = both[0]
    for index, where in enumerate(plane[1:], 1):
        kv_sum = kv_sum + over_plane(both[index].astype(BF16), where).astype(F32)
    kv_grad = kv_sum.astype(BF16)
    all_grads = jnp.concatenate([query_grad, kv_grad], axis=1)
    g_all = [all_grads] + [over_plane(all_grads, where) for where in plane[1:]]

    block = (n_z, blk, 3 * width)
    mine, other = pl.pallas_call(
        functools.partial(weight_kernel, n_plane),
        out_shape=[jax.ShapeDtypeStruct(block, F32), jax.ShapeDtypeStruct(block, BF16)],
        in_specs=[VMEM] * (2 * n_plane),
        out_specs=[VMEM] * 2,
        scratch_shapes=[pltpu.VMEM((n_core,) + block, F32)],
        compiler_params=params(24 * MIB),
        name="weights",
    )(*x_all, *g_all)
    both = mine + over_core(other).astype(F32)
    piece = both[0]
    for offset in range(1, n_z):
        piece = piece + over_z(both[offset].astype(BF16), offset).astype(F32)
    low = piece.astype(BF16)
    parts = [piece] + [xor_permute(low, ("row",), (a,)).astype(F32) for a in range(1, n_row)]
    stacked = jnp.stack(parts)
    stacked = stacked[row_id ^ jnp.arange(n_row)]
    weight_grad = stacked.reshape(n_row * blk, 3 * width)
    return query_grad, kv_grad[:, :width], kv_grad[:, width:], weight_grad


def solution(mesh):
    n_row, n_col = mesh.shape["row"], mesh.shape["col"]
    n_core = 2
    n_z = 1 << ((n_col.bit_length() - 1) // 2)
    n_y = n_col // (n_core * n_z)
    axes = (("row", n_row), ("z", n_z), ("y", n_y), ("core", n_core))
    split = Mesh(
        mesh.devices.reshape(tuple(size for _, size in axes)), tuple(name for name, _ in axes)
    )
    tokens = P(("row", "z", "y", "core"), None)
    return jax.shard_map(
        functools.partial(local, axes),
        mesh=split,
        in_specs=(tokens,) * 6 + (P(), P()),
        out_specs=(tokens, tokens, tokens, P(("z", "y", "core"), None)),
        check_vma=False,
    )
```

time: 350 us -> 86.6 us (0.25)
  waiting for transfers between devices: 186 us -> 32.5 us
  blocking collectives: 118 us -> 0 us
  starting transfers between devices: 0.16 us -> 31.9 us
  matrix products: 13.7 us -> 0 us
  between operations: 13.9 us -> 0.86 us
  Pallas kernels: 0 us -> 7.01 us
  other arithmetic: 7.61 us -> 1.28 us
  local copies, waits for them, and re-layouts: 8.42 us -> 12.4 us
    reduce_scatter x4 -> x0, waiting for transfers between devices: 185 us -> none  [the longest x1 108 us: local(): lax.psum_scatter(partial_value, ('row', 'col'), scatter_dimension=0, tile...]
    all_gather x8 -> x0, blocking collectives: 118 us -> none  [the longest x2 37.1 us: joined(): gathered = jax.tree.map(lambda a: lax.all_gather(a, axis), part)]
    ppermute x0 -> x28, waiting for transfers between devices: none -> 32.5 us  [xor_permute(): return lax.ppermute(value, tuple(names), pairs)]
    ppermute x0 -> x28, starting transfers between devices: none -> 31.9 us  [xor_permute(): return lax.ppermute(value, tuple(names), pairs)]
    dot_general x31 -> x0, matrix products: 13.7 us -> none  [the longest x5 4.79 us: backward_block(): jnp.dot(score_grad, key_rows, preferred_element_type=jnp.float32)]
    pallas_call x0 -> x4, Pallas kernels: none -> 7.01 us  [the longest x1 2.64 us: local(): pl.pallas_call(functools.partial(forward_kernel, count, width, n_z, len(k...]
    reduce_sum x16 -> x0, other arithmetic: 6.03 us -> none  [the longest x6 4.48 us: sample_of(): return jnp.sum(jnp.where(matches, block_sample[None, :], 0), axis=1)]
    unnamed x13 -> x16, local copies, waits for them, and re-layouts: 0.79 us -> 4.55 us
  transfers between devices with their start and end apart: 4 -> 28, of which waited for: 4 -> 15; matrix products, arithmetic and copies ran while one was open for 1% -> 7% of each run, Pallas kernels for 0% -> 0%
where the time goes in v1:
time: 86.6 us; the launch traced here: 86.1 us
  waiting for transfers between devices  32.5 us (38%)
  starting transfers between devices  31.9 us (37%)
  local copies, waits for them, and re-layouts  12.4 us (14%)
  Pallas kernels  7.01 us (8%)
  other arithmetic  1.28 us (1%)
    ppermute x28, waiting for transfers between devices, xor_permute(): return lax.ppermute(value, tuple(names), pairs)  32.5 us
    ppermute x28, starting transfers between devices, xor_permute(): return lax.ppermute(value, tuple(names), pairs)  31.9 us
    unnamed x16, local copies, waits for them, and re-layouts  4.55 us
    pallas_call x1, Pallas kernels, local(): pl.pallas_call(functools.partial(forward_kernel, count, width, n_z, len(k...  2.64 us
    pallas_call x1, Pallas kernels, local(): pl.pallas_call(functools.partial(backward_kernel, count, width, n_z), out...  2.25 us
    reshape x1, local copies, waits for them, and re-layouts, local(): split_input = layer_input.reshape(count, n_z, n_y, n_core, n_row, blk)  2.19 us
    transpose x1, local copies, waits for them, and re-layouts, local(): split_input.transpose(4, 2, 0, 3, 1, 5).reshape(n_plane, count, -1)  1.82 us
  transfers between devices with their start and end apart: 28, of which 15 were waited for; matrix products, arithmetic and copies ran while one was open for 7% of the time, Pallas kernels for 0%

profile of v1, /device:TPU:0, one launch (start us, length us, event | category | flops | bytes accessed | tf_op | source)
XLA Modules:
  0.0 86.1 jit_solution(152253551830768420)
XLA Ops:
  0.6 0.8 reshape.42.pos_ref
  1.4 0.8 copy-done
  2.2 0.8 copy-done.1
  3.0 0.8 copy-done.2
  3.8 0.8 copy-done.3
  4.6 0.8 copy-done.4
  5.3 0.7 copy-done.5
  6.0 1.0 %pack.1 = (bf16[176,256]{1,0:T(8,128)(2,1)S(1)}, bf16[176,256]{1,0:T(8,128)(2,1)S(1)}) custom-call(bf16[160,128]{1,0:T(8,128)(2,1)S(1)} %copy-done, bf16[160,128]{1,0:T(8,128)(2,1)S(1)} %copy-done.1, bf16[160,128]{1,0:T(8,128)(2,1)S(1)} %copy-done.2, bf16[160,128]{1,0:T(8,128)(2,1)S(1)} %copy-done.3, bf16[160,128]{1,0:T(8,128)(2,1)S(1)} %copy-done.4, ...), custom_call_target="tpu_custom_call" | custom-call | tf_op jit(solution)/shard_map/pack/pallas_call | solution.py:274
  7.0 3.0 %collective-permute-start.3 = (bf16[176,256]{1,0:T(8,128)(2,1)S(1)}, bf16[176,256]{1,0:T(8,128)(2,1)S(1)}, u32[]{:S(2)}, u32[]{:S(2)}) collective-permute-start(bf16[176,256]{1,0:T(8,128)(2,1)S(1)} %get-tuple-element.19), channel_id=1, source_target_pairs={{0,2},{2,0},{16,18},{18,16},{1,3},{3,1},{17,19},{19,17},{4,6},{6,4... | collective-permute-start | bytes 270344 | tf_op jit(solution)/shard_map/ppermute | solution.py:251
  10.1 1.5 %collective-permute-start.4 = (bf16[176,256]{1,0:T(8,128)(2,1)S(1)}, bf16[176,256]{1,0:T(8,128)(2,1)S(1)}, u32[]{:S(2)}, u32[]{:S(2)}) collective-permute-start(bf16[176,256]{1,0:T(8,128)(2,1)S(1)} %get-tuple-element.19), channel_id=1, source_target_pairs={{0,16},{2,18},{16,0},{18,2},{1,17},{3,19},{17,1},{19,3},{4,20},{6,... | collective-permute-start | bytes 270344 | tf_op jit(solution)/shard_map/ppermute | solution.py:251
  11.6 2.0 %collective-permute-start = (bf16[176,256]{1,0:T(8,128)(2,1)S(1)}, bf16[176,256]{1,0:T(8,128)(2,1)S(1)}, u32[]{:S(2)}, u32[]{:S(2)}) collective-permute-start(bf16[176,256]{1,0:T(8,128)(2,1)S(1)} %get-tuple-element.18.refs_0_.refs_4_), channel_id=1, source_target_pairs={{0,4},{4,0},{8,12},{12,8},{1,5},{5,1},{9,13},{13,9},{2,6},{6,2},{1... | collective-permute-start | bytes 270344 | tf_op jit(solution)/shard_map/ppermute | solution.py:251
  13.6 2.6 %collective-permute-start.1 = (bf16[176,256]{1,0:T(8,128)(2,1)S(1)}, bf16[176,256]{1,0:T(8,128)(2,1)S(1)}, u32[]{:S(2)}, u32[]{:S(2)}) collective-permute-start(bf16[176,256]{1,0:T(8,128)(2,1)S(1)} %get-tuple-element.18.refs_0_.refs_4_), channel_id=1, source_target_pairs={{0,8},{4,12},{8,0},{12,4},{1,9},{5,13},{9,1},{13,5},{2,10},{6,14},... | collective-permute-start | bytes 270344 | tf_op jit(solution)/shard_map/ppermute | solution.py:251
  16.2 0.5 collective-permute-start.2
  17.5 4.1 %collective-permute-done.1.refs_2_.refs_6_ = bf16[176,256]{1,0:T(8,128)(2,1)S(1)} collective-permute-done((bf16[176,256]{1,0:T(8,128)(2,1)S(1)}, bf16[176,256]{1,0:T(8,128)(2,1)S(1)}, u32[]{:S(2)}, u32[]{:S(2)}) %collective-permute-start.1) | collective-permute-done | bytes 90144 | tf_op jit(solution)/shard_map/ppermute | solution.py:251
  21.6 1.0 %collective-permute-done.2.refs_3_.refs_7_ = bf16[176,256]{1,0:T(8,128)(2,1)S(1)} collective-permute-done((bf16[176,256]{1,0:T(8,128)(2,1)S(1)}, bf16[176,256]{1,0:T(8,128)(2,1)S(1)}, u32[]{:S(2)}, u32[]{:S(2)}) %collective-permute-start.2) | collective-permute-done | bytes 90144 | tf_op jit(solution)/shard_map/ppermute | solution.py:251
  22.9 2.6 %forward.1 = (bf16[8,160,640]{2,1,0:T(8,128)(2,1)S(1)}, bf16[8,160,640]{2,1,0:T(8,128)(2,1)S(1)}, f32[8,640]{1,0:T(8,128)S(1)}, f32[160,128]{1,0:T(8,128)S(1)}, ...) custom-call(bf16[176,256]{1,0:T(8,128)(2,1)S(1)} %get-tuple-element.18.refs_0_.refs_4_, ...), custom_call_target="tpu_custom_call" | custom-call | tf_op jit(solution)/shard_map/forward/pallas_call | solution.py:308
  25.5 1.3 %collective-permute-start.10 = (bf16[176,128]{1,0:T(8,128)(2,1)S(1)}, bf16[176,128]{1,0:T(8,128)(2,1)S(1)}, u32[]{:S(2)}, u32[]{:S(2)}) collective-permute-start(bf16[176,128]{1,0:T(8,128)(2,1)S(1)} %get-tuple-element.24), channel_id=1, source_target_pairs={{0,4},{4,0},{8,12},{12,8},{1,5},{5,1},{9,13},{13,9},{2,6},{6,2},{1... | collective-permute-start | bytes 135176 | tf_op jit(solution)/shard_map/ppermute | solution.py:251
  26.8 2.8 %collective-permute-start.11 = (bf16[176,128]{1,0:T(8,128)(2,1)S(1)}, bf16[176,128]{1,0:T(8,128)(2,1)S(1)}, u32[]{:S(2)}, u32[]{:S(2)}) collective-permute-start(bf16[176,128]{1,0:T(8,128)(2,1)S(1)} %get-tuple-element.25), channel_id=1, source_target_pairs={{0,8},{4,12},{8,0},{12,4},{1,9},{5,13},{9,1},{13,5},{2,10},{6,14},... | collective-permute-start | bytes 135176 | tf_op jit(solution)/shard_map/ppermute | solution.py:251
  30.0 2.5 %collective-permute-done.11.refs_9_ = bf16[176,128]{1,0:T(8,128)(2,1)S(1)} collective-permute-done((bf16[176,128]{1,0:T(8,128)(2,1)S(1)}, bf16[176,128]{1,0:T(8,128)(2,1)S(1)}, u32[]{:S(2)}, u32[]{:S(2)}) %collective-permute-start.11) | collective-permute-done | bytes 45088 | tf_op jit(solution)/shard_map/ppermute | solution.py:251
  32.5 2.9 %collective-permute-done.12.refs_10_ = bf16[176,128]{1,0:T(8,128)(2,1)S(1)} collective-permute-done((bf16[176,128]{1,0:T(8,128)(2,1)S(1)}, bf16[176,128]{1,0:T(8,128)(2,1)S(1)}, u32[]{:S(2)}, u32[]{:S(2)}) %collective-permute-start.12) | collective-permute-done | bytes 45088 | tf_op jit(solution)/shard_map/ppermute | solution.py:251
  35.5 2.2 %backward.1 = (f32[4,160,256]{2,1,0:T(8,128)S(1)}, bf16[4,160,256]{2,1,0:T(8,128)(2,1)S(1)}, bf16[160,128]{1,0:T(8,128)(2,1)}) custom-call(bf16[8,160,640]{2,1,0:T(8,128)(2,1)S(1)} %get-tuple-element.20.refs_0_, bf16[8,160,640]{2,1,0:T(8,128)(2,1)S(1)} %get-tuple-element.21.refs_1_, f32[8,640]{1,0:T(8,128)S(1)} %get-tuple-element.22.refs_2_, ...), custom_call_target="tpu_custom_call" | custom-call | tf_op jit(solution)/shard_map/backward/pallas_call | solution.py:330
  37.8 2.2 %reshape.43 = bf16[160,4,2,2,2,96]{5,4,3,2,1,0:T(2,128)(2,1)} reshape(bf16[160,3072]{1,0:T(8,128)(2,1)S(1)} %copy-done.6) | data formatting | bytes 1966080 | tf_op jit(solution)/shard_map/reshape | solution.py:297
  40.0 1.8 %copy.12 = bf16[2,2,160,2,4,96]{5,4,3,2,1,0:T(4,128)(2,1)S(1)} copy(bf16[2,2,160,2,4,96]{5,0,3,1,4,2:T(2,128)(2,1)} %bitcast.67) | data formatting | bytes 1966080 | tf_op jit(solution)/shard_map/transpose | solution.py:298
  41.8 1.1 %reshape.44 = bf16[4,160,768]{2,1,0:T(8,128)(2,1)S(1)} reshape(bf16[2,2,160,2,4,96]{5,4,3,2,1,0:T(4,128)(2,1)S(1)} %copy.12) | data formatting | bytes 1966080 | tf_op jit(solution)/shard_map/reshape | solution.py:298
  42.9 1.1 %fusion.11 = (bf16[4,160,256]{2,1,0:T(8,128)(2,1)S(1)}, f32[4,160,256]{2,1,0:T(8,128)S(1)}) fusion(f32[4,160,256]{2,1,0:T(8,128)S(1)} %get-tuple-element.28, bf16[4,160,256]{2,1,0:T(8,128)(2,1)} %collective-permute-done.13), kind=kLoop, calls=%fused_computation.31 | loop fusion | flops 491520 | bytes 1966080 | tf_op jit(solution)/shard_map/convert.6
  44.0 1.6 %collective-permute-start.14 = (bf16[160,256]{1,0:T(8,128)(2,1)S(1)}, bf16[160,256]{1,0:T(8,128)(2,1)S(1)}, u32[]{:S(2)}, u32[]{:S(2)}) collective-permute-start(bf16[160,256]{1,0:T(8,128)(2,1)S(1)} %get-tuple-element.42), channel_id=1, source_target_pairs={{0,2},{2,0},{16,18},{18,16},{1,3},{3,1},{17,19},{19,17},{4,6},{6,4... | collective-permute-start | bytes 245768 | tf_op jit(solution)/shard_map/ppermute | solution.py:251
  45.6 1.5 %collective-permute-start.15 = (bf16[160,256]{1,0:T(8,128)(2,1)S(1)}, bf16[160,256]{1,0:T(8,128)(2,1)S(1)}, u32[]{:S(2)}, u32[]{:S(2)}) collective-permute-start(bf16[160,256]{1,0:T(8,128)(2,1)S(1)} %get-tuple-element.44), channel_id=1, source_target_pairs={{0,16},{2,18},{16,0},{18,2},{1,17},{3,19},{17,1},{19,3},{4,20},{6,... | collective-permute-start | bytes 245768 | tf_op jit(solution)/shard_map/ppermute | solution.py:251
  47.6 1.6 %collective-permute-start.17 = (bf16[160,768]{1,0:T(8,128)(2,1)S(1)}, bf16[160,768]{1,0:T(8,128)(2,1)S(1)}, u32[]{:S(2)}, u32[]{:S(2)}) collective-permute-start(bf16[160,768]{1,0:T(8,128)(2,1)S(1)} %get-tuple-element.38), channel_id=1, source_target_pairs={{0,2},{2,0},{16,18},{18,16},{1,3},{3,1},{17,19},{19,17},{4,6},{6,4... | collective-permute-start | bytes 737288 | tf_op jit(solution)/shard_map/ppermute | solution.py:251
  49.2 1.5 %collective-permute-start.18 = (bf16[160,768]{1,0:T(8,128)(2,1)S(1)}, bf16[160,768]{1,0:T(8,128)(2,1)S(1)}, u32[]{:S(2)}, u32[]{:S(2)}) collective-permute-start(bf16[160,768]{1,0:T(8,128)(2,1)S(1)} %get-tuple-element.37), channel_id=1, source_target_pairs={{0,16},{2,18},{16,0},{18,2},{1,17},{3,19},{17,1},{19,3},{4,20},{6,... | collective-permute-start | bytes 737288 | tf_op jit(solution)/shard_map/ppermute | solution.py:251
  50.7 0.6 collective-permute-start.19
  51.4 2.0 %collective-permute-done.16 = bf16[160,256]{1,0:T(8,128)(2,1)S(1)} collective-permute-done((bf16[160,256]{1,0:T(8,128)(2,1)S(1)}, bf16[160,256]{1,0:T(8,128)(2,1)S(1)}, u32[]{:S(2)}, u32[]{:S(2)}) %collective-permute-start.16) | collective-permute-done | bytes 81952 | tf_op jit(solution)/shard_map/ppermute | solution.py:251
  53.4 0.7 collective-permute-start.20
  54.1 1.6 %collective-permute-start.21 = (bf16[160,384]{1,0:T(8,128)(2,1)S(1)}, bf16[160,384]{1,0:T(8,128)(2,1)S(1)}, u32[]{:S(2)}, u32[]{:S(2)}) collective-permute-start(bf16[160,384]{1,0:T(8,128)(2,1)S(1)} %pad_maximum_fusion.1.refs_4_), channel_id=1, source_target_pairs={{0,16},{2,18},{16,0},{18,2},{1,17},{3,19},{17,1},{19,3},{4,20},{6,... | collective-permute-start | bytes 368648 | tf_op jit(solution)/shard_map/ppermute | solution.py:251
  55.7 6.3 %collective-permute-done.17.refs_1_ = bf16[160,768]{1,0:T(8,128)(2,1)S(1)} collective-permute-done((bf16[160,768]{1,0:T(8,128)(2,1)S(1)}, bf16[160,768]{1,0:T(8,128)(2,1)S(1)}, u32[]{:S(2)}, u32[]{:S(2)}) %collective-permute-start.17) | collective-permute-done | bytes 245792 | tf_op jit(solution)/shard_map/ppermute | solution.py:251
  61.9 2.1 %collective-permute-start.22 = (bf16[160,384]{1,0:T(8,128)(2,1)S(1)}, bf16[160,384]{1,0:T(8,128)(2,1)S(1)}, u32[]{:S(2)}, u32[]{:S(2)}) collective-permute-start(bf16[160,384]{1,0:T(8,128)(2,1)S(1)} %pad_maximum_fusion.1.refs_4_), channel_id=1, source_target_pairs={{0,18},{2,16},{16,2},{18,0},{1,19},{3,17},{17,3},{19,1},{4,22},{6,... | collective-permute-start | bytes 368648 | tf_op jit(solution)/shard_map/ppermute | solution.py:251
  64.1 1.2 %collective-permute-done.20.refs_5_ = bf16[160,384]{1,0:T(8,128)(2,1)S(1)} collective-permute-done((bf16[160,384]{1,0:T(8,128)(2,1)S(1)}, bf16[160,384]{1,0:T(8,128)(2,1)S(1)}, u32[]{:S(2)}, u32[]{:S(2)}) %collective-permute-start.20) | collective-permute-done | bytes 122912 | tf_op jit(solution)/shard_map/ppermute | solution.py:251
  65.3 0.8 collective-permute-done.21.refs_6_
  66.1 2.0 %collective-permute-done.22.refs_7_ = bf16[160,384]{1,0:T(8,128)(2,1)S(1)} collective-permute-done((bf16[160,384]{1,0:T(8,128)(2,1)S(1)}, bf16[160,384]{1,0:T(8,128)(2,1)S(1)}, u32[]{:S(2)}, u32[]{:S(2)}) %collective-permute-start.22) | collective-permute-done | bytes 122912 | tf_op jit(solution)/shard_map/ppermute | solution.py:251
  68.1 1.1 %weights.1 = (f32[4,96,384]{2,1,0:T(8,128)S(1)}, bf16[4,96,384]{2,1,0:T(8,128)(2,1)S(1)}) custom-call(bf16[160,768]{1,0:T(8,128)(2,1)S(1)} %get-tuple-element.39.refs_0_, bf16[160,768]{1,0:T(8,128)(2,1)S(1)} %collective-permute-done.17.refs_1_, bf16[160,768]{1,0:T(8,128)(2,1)S(1)} %collective-permute-done.18.refs_2_, ...), custom_call_target="tpu_custom_call" | custom-call | tf_op jit(solution)/shard_map/weights/pallas_call | solution.py:353
  69.3 1.6 %collective-permute-done.23 = bf16[4,96,384]{2,1,0:T(8,128)(2,1)S(1)} collective-permute-done((bf16[4,96,384]{2,1,0:T(8,128)(2,1)S(1)}, bf16[4,96,384]{2,1,0:T(8,128)(2,1)S(1)}, u32[]{:S(2)}, u32[]{:S(2)}) %collective-permute-start.23) | collective-permute-done | bytes 294944 | tf_op jit(solution)/shard_map/ppermute | solution.py:251
  71.0 1.3 %collective-permute-start.25 = (bf16[96,384]{1,0:T(8,128)(2,1)S(1)}, bf16[96,384]{1,0:T(8,128)(2,1)S(1)}, u32[]{:S(2)}, u32[]{:S(2)}) collective-permute-start(bf16[96,384]{1,0:T(8,128)(2,1)S(1)} %get-tuple-element.47), channel_id=1, source_target_pairs={{0,8},{4,12},{8,0},{12,4},{1,9},{5,13},{9,1},{13,5},{2,10},{6,14},... | collective-permute-start | bytes 221192 | tf_op jit(solution)/shard_map/ppermute | solution.py:251
  72.3 3.1 %collective-permute-start.26 = (bf16[96,384]{1,0:T(8,128)(2,1)S(1)}, bf16[96,384]{1,0:T(8,128)(2,1)S(1)}, u32[]{:S(2)}, u32[]{:S(2)}) collective-permute-start(bf16[96,384]{1,0:T(8,128)(2,1)S(1)} %get-tuple-element.46), channel_id=1, source_target_pairs={{0,12},{4,8},{8,4},{12,0},{1,13},{5,9},{9,5},{13,1},{2,14},{6,10},... | collective-permute-start | bytes 221192 | tf_op jit(solution)/shard_map/ppermute | solution.py:251
  75.4 1.0 %collective-permute-done.24 = bf16[96,384]{1,0:T(8,128)(2,1)S(1)} collective-permute-done((bf16[96,384]{1,0:T(8,128)(2,1)S(1)}, bf16[96,384]{1,0:T(8,128)(2,1)S(1)}, u32[]{:S(2)}, u32[]{:S(2)}) %collective-permute-start.24) | collective-permute-done | bytes 73760 | tf_op jit(solution)/shard_map/ppermute | solution.py:251
  76.4 3.9 %collective-permute-done.25 = bf16[96,384]{1,0:T(8,128)(2,1)S(1)} collective-permute-done((bf16[96,384]{1,0:T(8,128)(2,1)S(1)}, bf16[96,384]{1,0:T(8,128)(2,1)S(1)}, u32[]{:S(2)}, u32[]{:S(2)}) %collective-permute-start.25) | collective-permute-done | bytes 73760 | tf_op jit(solution)/shard_map/ppermute | solution.py:251
  80.3 1.1 %collective-permute-start.27 = (bf16[96,384]{1,0:T(8,128)(2,1)S(1)}, bf16[96,384]{1,0:T(8,128)(2,1)S(1)}, u32[]{:S(2)}, u32[]{:S(2)}) collective-permute-start(bf16[96,384]{1,0:T(8,128)(2,1)S(1)} %get-tuple-element.41), channel_id=1, source_target_pairs={{0,16},{16,0},{1,17},{17,1},{2,18},{18,2},{3,19},{19,3},{4,20},{20... | collective-permute-start | bytes 221192 | tf_op jit(solution)/shard_map/ppermute | solution.py:251
  81.4 0.6 fusion.12
  82.1 2.7 %collective-permute-done.27 = bf16[96,384]{1,0:T(8,128)(2,1)S(1)} collective-permute-done((bf16[96,384]{1,0:T(8,128)(2,1)S(1)}, bf16[96,384]{1,0:T(8,128)(2,1)S(1)}, u32[]{:S(2)}, u32[]{:S(2)}) %collective-permute-start.27) | collective-permute-done | bytes 73760 | tf_op jit(solution)/shard_map/ppermute | solution.py:251
  84.8 1.3 %gather_fusion = f32[2,96,384]{2,1,0:T(8,128)} fusion(f32[2,96,384]{2,1,0:T(8,128)S(1)} %pad_maximum_fusion, s32[1024]{0:T(1024)S(1)} %pad_clamp_fusion), kind=kCustom, calls=%fused_computation | custom fusion | bytes 589832 | tf_op jit(solution)/shard_map/gather | solution.py:369
  (46 shorter events, 2.6 us)
Async XLA Ops:
  1.4 0.8 copy-start
  2.2 0.8 copy-start.1
  3.0 0.8 copy-start.2
  3.8 0.8 copy-start.3
  4.6 0.8 copy-start.4
  5.3 0.7 copy-start.5
  7.0 9.2 %collective-permute-start.3 = (bf16[176,256]{1,0:T(8,128)(2,1)S(1)}, bf16[176,256]{1,0:T(8,128)(2,1)S(1)}, u32[]{:S(2)}, u32[]{:S(2)}) collective-permute-start(bf16[176,256]{1,0:T(8,128)(2,1)S(1)} %get-tuple-element.19), channel_id=1, source_target_pairs={{0,2},{2,0},{16,18},{18,16},{1,3},{3,1},{17,19},{19,17},{4,6},{6,4... | collective-permute-start | bytes 270344 | tf_op jit(solution)/shard_map/ppermute | solution.py:251
  10.1 6.6 %collective-permute-start.4 = (bf16[176,256]{1,0:T(8,128)(2,1)S(1)}, bf16[176,256]{1,0:T(8,128)(2,1)S(1)}, u32[]{:S(2)}, u32[]{:S(2)}) collective-permute-start(bf16[176,256]{1,0:T(8,128)(2,1)S(1)} %get-tuple-element.19), channel_id=1, source_target_pairs={{0,16},{2,18},{16,0},{18,2},{1,17},{3,19},{17,1},{19,3},{4,20},{6,... | collective-permute-start | bytes 270344 | tf_op jit(solution)/shard_map/ppermute | solution.py:251
  11.5 5.4 %collective-permute-start.5 = (bf16[176,256]{1,0:T(8,128)(2,1)S(1)}, bf16[176,256]{1,0:T(8,128)(2,1)S(1)}, u32[]{:S(2)}, u32[]{:S(2)}) collective-permute-start(bf16[176,256]{1,0:T(8,128)(2,1)S(1)} %get-tuple-element.19), channel_id=1, source_target_pairs={{0,18},{2,16},{16,2},{18,0},{1,19},{3,17},{17,3},{19,1},{4,22},{6,... | collective-permute-start | bytes 270344 | tf_op jit(solution)/shard_map/ppermute | solution.py:251
  11.6 5.6 %collective-permute-start = (bf16[176,256]{1,0:T(8,128)(2,1)S(1)}, bf16[176,256]{1,0:T(8,128)(2,1)S(1)}, u32[]{:S(2)}, u32[]{:S(2)}) collective-permute-start(bf16[176,256]{1,0:T(8,128)(2,1)S(1)} %get-tuple-element.18.refs_0_.refs_4_), channel_id=1, source_target_pairs={{0,4},{4,0},{8,12},{12,8},{1,5},{5,1},{9,13},{13,9},{2,6},{6,2},{1... | collective-permute-start | bytes 270344 | tf_op jit(solution)/shard_map/ppermute | solution.py:251
  13.6 8.0 %collective-permute-start.1 = (bf16[176,256]{1,0:T(8,128)(2,1)S(1)}, bf16[176,256]{1,0:T(8,128)(2,1)S(1)}, u32[]{:S(2)}, u32[]{:S(2)}) collective-permute-start(bf16[176,256]{1,0:T(8,128)(2,1)S(1)} %get-tuple-element.18.refs_0_.refs_4_), channel_id=1, source_target_pairs={{0,8},{4,12},{8,0},{12,4},{1,9},{5,13},{9,1},{13,5},{2,10},{6,14},... | collective-permute-start | bytes 270344 | tf_op jit(solution)/shard_map/ppermute | solution.py:251
  16.2 6.4 %collective-permute-start.2 = (bf16[176,256]{1,0:T(8,128)(2,1)S(1)}, bf16[176,256]{1,0:T(8,128)(2,1)S(1)}, u32[]{:S(2)}, u32[]{:S(2)}) collective-permute-start(bf16[176,256]{1,0:T(8,128)(2,1)S(1)} %get-tuple-element.18.refs_0_.refs_4_), channel_id=1, source_target_pairs={{0,12},{4,8},{8,4},{12,0},{1,13},{5,9},{9,5},{13,1},{2,14},{6,10},... | collective-permute-start | bytes 270344 | tf_op jit(solution)/shard_map/ppermute | solution.py:251
  16.7 6.0 %collective-permute-start.6 = (bf16[176,256]{1,0:T(8,128)(2,1)S(1)}, bf16[176,256]{1,0:T(8,128)(2,1)S(1)}, u32[]{:S(2)}, u32[]{:S(2)}) collective-permute-start(bf16[176,256]{1,0:T(8,128)(2,1)S(1)} %get-tuple-element.19), channel_id=1, source_target_pairs={{0,1},{1,0},{2,3},{3,2},{4,5},{5,4},{6,7},{7,6},{8,9},{9,8},{10,11... | collective-permute-start | bytes 270344 | tf_op jit(solution)/shard_map/ppermute | solution.py:251
  17.0 5.7 %collective-permute-start.7 = (bf16[176,256]{1,0:T(8,128)(2,1)S(1)}, bf16[176,256]{1,0:T(8,128)(2,1)S(1)}, u32[]{:S(2)}, u32[]{:S(2)}) collective-permute-start(bf16[176,256]{1,0:T(8,128)(2,1)S(1)} %collective-permute-done.3), channel_id=1, source_target_pairs={{0,1},{1,0},{2,3},{3,2},{4,5},{5,4},{6,7},{7,6},{8,9},{9,8},{10,11... | collective-permute-start | bytes 270344 | tf_op jit(solution)/shard_map/ppermute | solution.py:251
  17.2 5.4 %collective-permute-start.8 = (bf16[176,256]{1,0:T(8,128)(2,1)S(1)}, bf16[176,256]{1,0:T(8,128)(2,1)S(1)}, u32[]{:S(2)}, u32[]{:S(2)}) collective-permute-start(bf16[176,256]{1,0:T(8,128)(2,1)S(1)} %collective-permute-done.4), channel_id=1, source_target_pairs={{0,1},{1,0},{2,3},{3,2},{4,5},{5,4},{6,7},{7,6},{8,9},{9,8},{10,11... | collective-permute-start | bytes 270344 | tf_op jit(solution)/shard_map/ppermute | solution.py:251
  21.6 1.3 %collective-permute-start.9 = (bf16[176,256]{1,0:T(8,128)(2,1)S(1)}, bf16[176,256]{1,0:T(8,128)(2,1)S(1)}, u32[]{:S(2)}, u32[]{:S(2)}) collective-permute-start(bf16[176,256]{1,0:T(8,128)(2,1)S(1)} %collective-permute-done.5), channel_id=1, source_target_pairs={{0,1},{1,0},{2,3},{3,2},{4,5},{5,4},{6,7},{7,6},{8,9},{9,8},{10,11... | collective-permute-start | bytes 270344 | tf_op jit(solution)/shard_map/ppermute | solution.py:251
  25.5 4.5 %collective-permute-start.10 = (bf16[176,128]{1,0:T(8,128)(2,1)S(1)}, bf16[176,128]{1,0:T(8,128)(2,1)S(1)}, u32[]{:S(2)}, u32[]{:S(2)}) collective-permute-start(bf16[176,128]{1,0:T(8,128)(2,1)S(1)} %get-tuple-element.24), channel_id=1, source_target_pairs={{0,4},{4,0},{8,12},{12,8},{1,5},{5,1},{9,13},{13,9},{2,6},{6,2},{1... | collective-permute-start | bytes 135176 | tf_op jit(solution)/shard_map/ppermute | solution.py:251
  26.8 5.7 %collective-permute-start.11 = (bf16[176,128]{1,0:T(8,128)(2,1)S(1)}, bf16[176,128]{1,0:T(8,128)(2,1)S(1)}, u32[]{:S(2)}, u32[]{:S(2)}) collective-permute-start(bf16[176,128]{1,0:T(8,128)(2,1)S(1)} %get-tuple-element.25), channel_id=1, source_target_pairs={{0,8},{4,12},{8,0},{12,4},{1,9},{5,13},{9,1},{13,5},{2,10},{6,14},... | collective-permute-start | bytes 135176 | tf_op jit(solution)/shard_map/ppermute | solution.py:251
  29.6 5.8 %collective-permute-start.12 = (bf16[176,128]{1,0:T(8,128)(2,1)S(1)}, bf16[176,128]{1,0:T(8,128)(2,1)S(1)}, u32[]{:S(2)}, u32[]{:S(2)}) collective-permute-start(bf16[176,128]{1,0:T(8,128)(2,1)S(1)} %get-tuple-element.26), channel_id=1, source_target_pairs={{0,12},{4,8},{8,4},{12,0},{1,13},{5,9},{9,5},{13,1},{2,14},{6,10},... | collective-permute-start | bytes 135176 | tf_op jit(solution)/shard_map/ppermute | solution.py:251
  35.4 2.4 %copy-start.6 = (bf16[160,3072]{1,0:T(8,128)(2,1)S(1)}, bf16[160,3072]{1,0:T(8,128)(2,1)}, u32[]{:S(2)}) copy-start(bf16[160,3072]{1,0:T(8,128)(2,1)} %param.8) | copy-start | bytes 2949124
  37.7 5.2 %collective-permute-start.13 = (bf16[4,160,256]{2,1,0:T(8,128)(2,1)S(1)}, bf16[4,160,256]{2,1,0:T(8,128)(2,1)}, u32[]{:S(2)}, u32[]{:S(2)}) collective-permute-start(bf16[4,160,256]{2,1,0:T(8,128)(2,1)S(1)} %get-tuple-element.29), channel_id=1, source_target_pairs={{0,1},{1,0},{2,3},{3,2},{4,5},{5,4},{6,7},{7,6},{8,9},{9,8},{10,11... | collective-permute-start | bytes 983048 | tf_op jit(solution)/shard_map/ppermute | solution.py:251
  44.0 9.4 %copy-start.7 = (bf16[160,128]{1,0:T(8,128)(2,1)S(1)}, bf16[160,128]{1,0:T(8,128)(2,1)}, u32[]{:S(2)}) copy-start(bf16[160,128]{1,0:T(8,128)(2,1)} %get-tuple-element.14) | copy-start | bytes 122884
  44.0 6.7 %collective-permute-start.14 = (bf16[160,256]{1,0:T(8,128)(2,1)S(1)}, bf16[160,256]{1,0:T(8,128)(2,1)S(1)}, u32[]{:S(2)}, u32[]{:S(2)}) collective-permute-start(bf16[160,256]{1,0:T(8,128)(2,1)S(1)} %get-tuple-element.42), channel_id=1, source_target_pairs={{0,2},{2,0},{16,18},{18,16},{1,3},{3,1},{17,19},{19,17},{4,6},{6,4... | collective-permute-start | bytes 245768 | tf_op jit(solution)/shard_map/ppermute | solution.py:251
  45.6 5.7 %collective-permute-start.15 = (bf16[160,256]{1,0:T(8,128)(2,1)S(1)}, bf16[160,256]{1,0:T(8,128)(2,1)S(1)}, u32[]{:S(2)}, u32[]{:S(2)}) collective-permute-start(bf16[160,256]{1,0:T(8,128)(2,1)S(1)} %get-tuple-element.44), channel_id=1, source_target_pairs={{0,16},{2,18},{16,0},{18,2},{1,17},{3,19},{17,1},{19,3},{4,20},{6,... | collective-permute-start | bytes 245768 | tf_op jit(solution)/shard_map/ppermute | solution.py:251
  47.1 6.2 %collective-permute-start.16 = (bf16[160,256]{1,0:T(8,128)(2,1)S(1)}, bf16[160,256]{1,0:T(8,128)(2,1)S(1)}, u32[]{:S(2)}, u32[]{:S(2)}) collective-permute-start(bf16[160,256]{1,0:T(8,128)(2,1)S(1)} %get-tuple-element.43), channel_id=1, source_target_pairs={{0,18},{2,16},{16,2},{18,0},{1,19},{3,17},{17,3},{19,1},{4,22},{6,... | collective-permute-start | bytes 245768 | tf_op jit(solution)/shard_map/ppermute | solution.py:251
  47.6 14.3 %collective-permute-start.17 = (bf16[160,768]{1,0:T(8,128)(2,1)S(1)}, bf16[160,768]{1,0:T(8,128)(2,1)S(1)}, u32[]{:S(2)}, u32[]{:S(2)}) collective-permute-start(bf16[160,768]{1,0:T(8,128)(2,1)S(1)} %get-tuple-element.38), channel_id=1, source_target_pairs={{0,2},{2,0},{16,18},{18,16},{1,3},{3,1},{17,19},{19,17},{4,6},{6,4... | collective-permute-start | bytes 737288 | tf_op jit(solution)/shard_map/ppermute | solution.py:251
  49.2 14.8 %collective-permute-start.18 = (bf16[160,768]{1,0:T(8,128)(2,1)S(1)}, bf16[160,768]{1,0:T(8,128)(2,1)S(1)}, u32[]{:S(2)}, u32[]{:S(2)}) collective-permute-start(bf16[160,768]{1,0:T(8,128)(2,1)S(1)} %get-tuple-element.37), channel_id=1, source_target_pairs={{0,16},{2,18},{16,0},{18,2},{1,17},{3,19},{17,1},{19,3},{4,20},{6,... | collective-permute-start | bytes 737288 | tf_op jit(solution)/shard_map/ppermute | solution.py:251
  50.7 13.3 %collective-permute-start.19 = (bf16[160,768]{1,0:T(8,128)(2,1)S(1)}, bf16[160,768]{1,0:T(8,128)(2,1)S(1)}, u32[]{:S(2)}, u32[]{:S(2)}) collective-permute-start(bf16[160,768]{1,0:T(8,128)(2,1)S(1)} %get-tuple-element.36), channel_id=1, source_target_pairs={{0,18},{2,16},{16,2},{18,0},{1,19},{3,17},{17,3},{19,1},{4,22},{6,... | collective-permute-start | bytes 737288 | tf_op jit(solution)/shard_map/ppermute | solution.py:251
  53.4 11.9 %collective-permute-start.20 = (bf16[160,384]{1,0:T(8,128)(2,1)S(1)}, bf16[160,384]{1,0:T(8,128)(2,1)S(1)}, u32[]{:S(2)}, u32[]{:S(2)}) collective-permute-start(bf16[160,384]{1,0:T(8,128)(2,1)S(1)} %pad_maximum_fusion.1.refs_4_), channel_id=1, source_target_pairs={{0,2},{2,0},{16,18},{18,16},{1,3},{3,1},{17,19},{19,17},{4,6},{6,4... | collective-permute-start | bytes 368648 | tf_op jit(solution)/shard_map/ppermute | solution.py:251
  54.1 12.0 %collective-permute-start.21 = (bf16[160,384]{1,0:T(8,128)(2,1)S(1)}, bf16[160,384]{1,0:T(8,128)(2,1)S(1)}, u32[]{:S(2)}, u32[]{:S(2)}) collective-permute-start(bf16[160,384]{1,0:T(8,128)(2,1)S(1)} %pad_maximum_fusion.1.refs_4_), channel_id=1, source_target_pairs={{0,16},{2,18},{16,0},{18,2},{1,17},{3,19},{17,1},{19,3},{4,20},{6,... | collective-permute-start | bytes 368648 | tf_op jit(solution)/shard_map/ppermute | solution.py:251
  61.9 6.2 %collective-permute-start.22 = (bf16[160,384]{1,0:T(8,128)(2,1)S(1)}, bf16[160,384]{1,0:T(8,128)(2,1)S(1)}, u32[]{:S(2)}, u32[]{:S(2)}) collective-permute-start(bf16[160,384]{1,0:T(8,128)(2,1)S(1)} %pad_maximum_fusion.1.refs_4_), channel_id=1, source_target_pairs={{0,18},{2,16},{16,2},{18,0},{1,19},{3,17},{17,3},{19,1},{4,22},{6,... | collective-permute-start | bytes 368648 | tf_op jit(solution)/shard_map/ppermute | solution.py:251
  69.2 1.6 %collective-permute-start.23 = (bf16[4,96,384]{2,1,0:T(8,128)(2,1)S(1)}, bf16[4,96,384]{2,1,0:T(8,128)(2,1)S(1)}, u32[]{:S(2)}, u32[]{:S(2)}) collective-permute-start(bf16[4,96,384]{2,1,0:T(8,128)(2,1)S(1)} %get-tuple-element.31), channel_id=1, source_target_pairs={{0,1},{1,0},{2,3},{3,2},{4,5},{5,4},{6,7},{7,6},{8,9},{9,8},{10,11... | collective-permute-start | bytes 884744 | tf_op jit(solution)/shard_map/ppermute | solution.py:251
  71.0 5.4 %collective-permute-start.24 = (bf16[96,384]{1,0:T(8,128)(2,1)S(1)}, bf16[96,384]{1,0:T(8,128)(2,1)S(1)}, u32[]{:S(2)}, u32[]{:S(2)}) collective-permute-start(bf16[96,384]{1,0:T(8,128)(2,1)S(1)} %get-tuple-element.45), channel_id=1, source_target_pairs={{0,4},{4,0},{8,12},{12,8},{1,5},{5,1},{9,13},{13,9},{2,6},{6,2},{1... | collective-permute-start | bytes 221192 | tf_op jit(solution)/shard_map/ppermute | solution.py:251
  71.0 9.2 %collective-permute-start.25 = (bf16[96,384]{1,0:T(8,128)(2,1)S(1)}, bf16[96,384]{1,0:T(8,128)(2,1)S(1)}, u32[]{:S(2)}, u32[]{:S(2)}) collective-permute-start(bf16[96,384]{1,0:T(8,128)(2,1)S(1)} %get-tuple-element.47), channel_id=1, source_target_pairs={{0,8},{4,12},{8,0},{12,4},{1,9},{5,13},{9,1},{13,5},{2,10},{6,14},... | collective-permute-start | bytes 221192 | tf_op jit(solution)/shard_map/ppermute | solution.py:251
  72.3 7.9 %collective-permute-start.26 = (bf16[96,384]{1,0:T(8,128)(2,1)S(1)}, bf16[96,384]{1,0:T(8,128)(2,1)S(1)}, u32[]{:S(2)}, u32[]{:S(2)}) collective-permute-start(bf16[96,384]{1,0:T(8,128)(2,1)S(1)} %get-tuple-element.46), channel_id=1, source_target_pairs={{0,12},{4,8},{8,4},{12,0},{1,13},{5,9},{9,5},{13,1},{2,14},{6,10},... | collective-permute-start | bytes 221192 | tf_op jit(solution)/shard_map/ppermute | solution.py:251
  80.3 4.4 %collective-permute-start.27 = (bf16[96,384]{1,0:T(8,128)(2,1)S(1)}, bf16[96,384]{1,0:T(8,128)(2,1)S(1)}, u32[]{:S(2)}, u32[]{:S(2)}) collective-permute-start(bf16[96,384]{1,0:T(8,128)(2,1)S(1)} %get-tuple-element.41), channel_id=1, source_target_pairs={{0,16},{16,0},{1,17},{17,1},{2,18},{18,2},{3,19},{19,3},{4,20},{20... | collective-permute-start | bytes 221192 | tf_op jit(solution)/shard_map/ppermute | solution.py:251

commit v2 on v1

--- a/solution.py
+++ b/solution.py
@@ -18,7 +18,7 @@
 F32 = jnp.float32
 BF16 = jnp.bfloat16
 VMEM = pl.BlockSpec(memory_space=pltpu.VMEM)
-SMEM = pl.BlockSpec(memory_space=pltpu.SMEM)
+HBM = pl.BlockSpec(memory_space=pltpu.HBM)
 
 
 def dot_nt(left, right, precision=None):
@@ -42,33 +42,84 @@
     return high, middle, rest - middle
 
 
-def pack_kernel(axes, q_ref, k_ref, v_ref, o_ref, g_ref, pos_ref, ids_ref, qg_ref, kv_ref, prod, extra):
-    count, width = q_ref.shape
+def pack_kernel(
+    axes, q_hbm, k_hbm, v_hbm, o_hbm, g_hbm, x_hbm, pos_hbm, ids_hbm, qg_ref, kv_ref, x_ref, *scratch
+):
+    outs, prod, extra, pos, ids, sems = scratch
+    count, width = outs.shape
+    copies = [
+        pltpu.make_async_copy(source, target, sems.at[place])
+        for place, (source, target) in enumerate(
+            (
+                (pos_hbm, pos),
+                (ids_hbm, ids),
+                (g_hbm, qg_ref.at[:count, width:]),
+                (o_hbm, outs),
+                (q_hbm, qg_ref.at[:count, :width]),
+                (k_hbm, kv_ref.at[:count, :width]),
+                (v_hbm, kv_ref.at[:count, width:]),
+                (x_hbm, x_ref),
+            )
+        )
+    ]
+    for copy in copies:
+        copy.start()
     me = jnp.int32(0)
     for name, size in axes:
         me = me * size + lax.axis_index(name)
-    qg_ref[:count, :width] = q_ref[...]
-    qg_ref[:count, width:] = g_ref[...]
-    kv_ref[:count, :width] = k_ref[...]
-    kv_ref[:count, width:] = v_ref[...]
     prod[...] = jnp.zeros_like(prod)
-    prod[:count, :] = g_ref[...].astype(F32) * o_ref[...].astype(F32)
+    copies[0].wait()
+    copies[1].wait()
+    lines = min(pos.shape[0], (count + LANES - 2) // LANES + 1)
+    first = jnp.minimum(me * count // LANES, pos.shape[0] - lines)
+    shift = me * count - first * LANES
+    block = jnp.concatenate([pos[pl.ds(first + i, 1), :] for i in range(lines)], axis=1) // BLK
+
+    def add_id(index, found):
+        return jnp.where(block == index, ids[index], found)
+
+    found = lax.fori_loop(0, ids.shape[0], add_id, jnp.zeros_like(block), unroll=8)
+    found = jnp.broadcast_to(found.astype(F32), (8, lines * LANES))
+    found = pltpu.roll(found, lines * LANES - shift, 1)
+    copies[2].wait()
+    copies[3].wait()
+    prod[:count, :] = qg_ref[:count, width:].astype(F32) * outs[...].astype(F32)
     delta = dot_nt(
         jnp.ones((PAD_ROWS, width), F32), prod[...], precision=lax.Precision.HIGHEST
     )
     high, middle, low = split_three(delta)
     row = lax.broadcasted_iota(jnp.int32, delta.shape, 0)
     extra[...] = jnp.where(row == 0, high, jnp.where(row == 1, middle, jnp.where(row == 2, low, 0.0)))
-    block = pos_ref[pl.ds(me, 1), :] // BLK
-
-    def add_id(index, found):
-        return jnp.where(block == index, ids_ref[index], found)
-
-    found = lax.fori_loop(0, ids_ref.shape[0], add_id, jnp.zeros_like(block))
-    extra[3:4, :count] = found.astype(F32)
+    extra[3:4, :count] = found[0:1, :count]
     tail = extra[...].astype(BF16)
     qg_ref[count:, :] = tail
     kv_ref[count:, :] = tail
+    for copy in copies[4:]:
+        copy.wait()
+
+
+def deal_kernel(sizes, x_ref, *refs):
+    *out_refs, dealt = refs
+    n_row, n_z, n_y, n_core = sizes
+    blk = x_ref.shape[1] // (n_row * n_z * n_y * n_core)
+    for a in range(n_row):
+        for b in range(n_y):
+            for core in range(n_core):
+                for z in range(n_z):
+                    first = (((z * n_y + b) * n_core + core) * n_row + a) * blk
+                    dealt[a * n_y + b, core, :, z * blk : (z + 1) * blk] = x_ref[:, first : first + blk]
+    me_row, me_y = lax.axis_index("row"), lax.axis_index("y")
+    for a in range(n_row):
+        for b in range(n_y):
+            out_refs[a * n_y + b][...] = dealt[(me_row ^ a) * n_y + (me_y ^ b)]
+
+
+def assemble_kernel(own_ref, *refs):
+    *got_refs, out_ref = refs
+    me_row = lax.axis_index("row")
+    out_ref[me_row] = own_ref[...]
+    for offset, ref in enumerate(got_refs, 1):
+        out_ref[me_row ^ offset] = ref[...].astype(F32)
 
 
 def forward_kernel(count, width, n_q, n_kv, *refs):
@@ -221,19 +272,19 @@
             emit(i, 1, mine_ref, i)
 
 
-def weight_kernel(n_pairs, *refs):
+def weight_kernel(n_pairs, n_z, *refs):
     x_refs, refs = refs[:n_pairs], refs[n_pairs:]
     g_refs, refs = refs[:n_pairs], refs[n_pairs:]
-    mine_ref, other_ref, sums = refs
+    out_refs, sums = refs[:n_z], refs[n_z]
+    core_id = lax.axis_index("core")
     total = None
     for x_ref, g_ref in zip(x_refs, g_refs):
-        part = dot_tn(x_ref[...], g_ref[...])
+        part = dot_tn(x_ref[core_id], g_ref[...])
         total = part if total is None else total + part
     sums[...] = total.reshape(sums.shape)
-    z_id, core_id = lax.axis_index("z"), lax.axis_index("core")
-    for slot in range(sums.shape[1]):
-        mine_ref[slot] = sums[core_id, z_id ^ slot]
-        other_ref[slot] = sums[core_id ^ 1, z_id ^ slot].astype(other_ref.dtype)
+    z_id = lax.axis_index("z")
+    for slot, ref in enumerate(out_refs):
+        ref[...] = sums[z_id ^ slot].astype(ref.dtype)
 
 
 def xor_permute(value, names, offsets):
@@ -271,36 +322,55 @@
         return xor_permute(value, ("core",), (1,))
 
     packed = jax.ShapeDtypeStruct((count + PAD_ROWS, 2 * width), BF16)
-    qg, kv = pl.pallas_call(
+    qg, kv, x_here = pl.pallas_call(
         functools.partial(pack_kernel, axes),
-        out_shape=(packed, packed),
-        in_specs=[VMEM] * 6 + [SMEM],
-        out_specs=(VMEM, VMEM),
+        out_shape=(packed, packed, jax.ShapeDtypeStruct(layer_input.shape, BF16)),
+        in_specs=[HBM] * 8,
+        out_specs=(VMEM, VMEM, VMEM),
         scratch_shapes=[
+            pltpu.VMEM((count, width), BF16),
             pltpu.VMEM((2 * width, width), F32),
             pltpu.VMEM((PAD_ROWS, 2 * width), F32),
+            pltpu.VMEM((token_pos.shape[0] // LANES, LANES), jnp.int32),
+            pltpu.SMEM(block_sample.shape, jnp.int32),
+            pltpu.SemaphoreType.DMA((8,)),
         ],
         compiler_params=params(8 * MIB),
         name="pack",
-    )(queries, keys, values, forward_out, out_grad, token_pos.reshape(-1, count), block_sample)
-
+    )(
+        *(
+            pltpu.with_memory_space_constraint(value, pltpu.HBM)
+            for value in (
+                queries,
+                keys,
+                values,
+                forward_out,
+                out_grad,
+                layer_input,
+                token_pos.reshape(-1, LANES),
+                block_sample,
+            )
+        )
+    )
+
+    blk = model_width // (n_z * n_y * n_core * n_row)
     kv_near = [kv] + [over_plane(kv, where) for where in plane[1:]]
     qg_all = [qg] + [over_z(qg, offset) for offset in range(1, n_z)]
+    x_send = pl.pallas_call(
+        functools.partial(deal_kernel, (n_row, n_z, n_y, n_core)),
+        out_shape=[jax.ShapeDtypeStruct((n_core, count, n_z * blk), BF16)] * n_plane,
+        in_specs=[VMEM],
+        out_specs=[VMEM] * n_plane,
+        scratch_shapes=[pltpu.VMEM((n_plane, n_core, count, n_z * blk), BF16)],
+        compiler_params=params(16 * MIB),
+        name="deal",
+    )(x_here)
+    kv_near[1:], x_send = lax.optimization_barrier((kv_near[1:], x_send))
     kv_all = kv_near + [over_core(piece) for piece in kv_near]
     if n_pieces <= 8:
         kv_all = [piece[None] for piece in kv_all]
     else:
         kv_all = [jnp.stack(kv_all)]
-
-    blk = model_width // (n_z * n_y * n_core * n_row)
-    row_id, y_id = lax.axis_index("row"), lax.axis_index("y")
-    split_input = layer_input.reshape(count, n_z, n_y, n_core, n_row, blk)
-    split_input = split_input.transpose(4, 2, 0, 3, 1, 5).reshape(n_plane, count, -1)
-    x_send = [
-        lax.dynamic_index_in_dim(split_input, (row_id ^ a) * n_y + (y_id ^ b), 0, False)
-        for a, b in plane
-    ]
-    x_all = [x_send[0]] + [over_plane(x, where) for x, where in zip(x_send[1:], plane[1:])]
 
     mass_rows = 3 * total // LANES
     tail_rows = -(-mass_rows // PAD_ROWS) * PAD_ROWS
@@ -326,6 +396,18 @@
         name="forward",
     )(*qg_all, *kv_all)
     got = [over_z(piece, offset) for offset, piece in enumerate(send, 1)]
+    x_send, stat = lax.optimization_barrier((x_send, stat))
+    x_all = [x_send[0]] + [over_plane(x, where) for x, where in zip(x_send[1:], plane[1:])]
+    far = [index for index, (a, b) in enumerate(plane) if a and b]
+    near = [index for index, (a, b) in enumerate(plane) if (a or b) and not (a and b)]
+
+    def together(values, indices):
+        values, some = lax.optimization_barrier((values, [x_all[index] for index in indices]))
+        for index, value in zip(indices, some):
+            x_all[index] = value
+        return values
+
+    got = together(got, far)
 
     mine, other, query_grad = pl.pallas_call(
         functools.partial(backward_kernel, count, width, n_z),
@@ -338,36 +420,49 @@
         out_specs=[VMEM] * 3,
         scratch_shapes=[pltpu.VMEM((total, width), BF16), pltpu.VMEM((total, width), BF16)],
         compiler_params=params(16 * MIB if n_pieces <= 8 else 56 * MIB),
+        cost_estimate=pl.CostEstimate(flops=int(3e10), bytes_accessed=0, transcendentals=0),
         name="backward",
     )(w, u, stat, own_part, *qg_all, *got)
 
+    other = together(other, near)
     both = mine + over_core(other).astype(F32)
+
+    x_pair = [over_core(x) for x in x_all]
+    arrived = [
+        over_plane(both[index].astype(BF16), where) for index, where in enumerate(plane[1:], 1)
+    ]
     kv_sum = both[0]
-    for index, where in enumerate(plane[1:], 1):
-        kv_sum = kv_sum + over_plane(both[index].astype(BF16), where).astype(F32)
+    for part in arrived:
+        kv_sum = kv_sum + part.astype(F32)
     kv_grad = kv_sum.astype(BF16)
     all_grads = jnp.concatenate([query_grad, kv_grad], axis=1)
     g_all = [all_grads] + [over_plane(all_grads, where) for where in plane[1:]]
-
-    block = (n_z, blk, 3 * width)
-    mine, other = pl.pallas_call(
-        functools.partial(weight_kernel, n_plane),
-        out_shape=[jax.ShapeDtypeStruct(block, F32), jax.ShapeDtypeStruct(block, BF16)],
-        in_specs=[VMEM] * (2 * n_plane),
-        out_specs=[VMEM] * 2,
-        scratch_shapes=[pltpu.VMEM((n_core,) + block, F32)],
+    g_all = g_all + [over_core(g) for g in g_all]
+    x_all = x_all + x_pair
+    mine, *send = pl.pallas_call(
+        functools.partial(weight_kernel, len(x_all), n_z),
+        out_shape=[jax.ShapeDtypeStruct((blk, 3 * width), F32)]
+        + [jax.ShapeDtypeStruct((blk, 3 * width), BF16)] * (n_z - 1),
+        in_specs=[VMEM] * (2 * len(x_all)),
+        out_specs=[VMEM] * n_z,
+        scratch_shapes=[pltpu.VMEM((n_z, blk, 3 * width), F32)],
         compiler_params=params(24 * MIB),
         name="weights",
     )(*x_all, *g_all)
-    both = mine + over_core(other).astype(F32)
+    both = [mine] + send
     piece = both[0]
     for offset in range(1, n_z):
-        piece = piece + over_z(both[offset].astype(BF16), offset).astype(F32)
+        piece = piece + over_z(both[offset], offset).astype(F32)
     low = piece.astype(BF16)
-    parts = [piece] + [xor_permute(low, ("row",), (a,)).astype(F32) for a in range(1, n_row)]
-    stacked = jnp.stack(parts)
-    stacked = stacked[row_id ^ jnp.arange(n_row)]
-    weight_grad = stacked.reshape(n_row * blk, 3 * width)
+    parts = [piece] + [xor_permute(low, ("row",), (a,)) for a in range(1, n_row)]
+    weight_grad = pl.pallas_call(
+        assemble_kernel,
+        out_shape=jax.ShapeDtypeStruct((n_row, blk, 3 * width), F32),
+        in_specs=[VMEM] * n_row,
+        out_specs=VMEM,
+        compiler_params=params(8 * MIB),
+        name="assemble",
+    )(*parts).reshape(n_row * blk, 3 * width)
     return query_grad, kv_grad[:, :width], kv_grad[:, width:], weight_grad
 
 

time: 86.6 us -> 71.7 us (0.83)
  local copies, waits for them, and re-layouts: 12.4 us -> 0.66 us
  waiting for transfers between devices: 32.5 us -> 29.9 us
  Pallas kernels: 7.01 us -> 8.77 us
  other arithmetic: 1.28 us -> 0.21 us
    unnamed x16 -> x2, local copies, waits for them, and re-layouts: 4.55 us -> 0.01 us
    reshape x3 -> x0, local copies, waits for them, and re-layouts: 4.05 us -> none  [the longest x1 2.19 us: local(): split_input = layer_input.reshape(count, n_z, n_y, n_core, n_row, blk)]
    ppermute x28 -> x35, waiting for transfers between devices: 32.5 us -> 29.9 us  [xor_permute(): return lax.ppermute(value, tuple(names), pairs)]
    transpose x1 -> x0, local copies, waits for them, and re-layouts: 1.82 us -> none  [local(): split_input.transpose(4, 2, 0, 3, 1, 5).reshape(n_plane, count, -1)]
    pallas_call x1 -> x3, Pallas kernels: 1.09 us -> 2.47 us  [the longest x1 1.07 us: local(): pl.pallas_call(functools.partial(weight_kernel, len(x_all), n_z), out_sha...]
    gather x1 -> x0, local copies, waits for them, and re-layouts: 1.28 us -> none  [local(): stacked = stacked[row_id ^ jnp.arange(n_row)]]
    another operation x5 -> x1, other arithmetic: 1.21 us -> 0.11 us
    ppermute x28 -> x35, starting transfers between devices: 31.9 us -> 31.2 us  [xor_permute(): return lax.ppermute(value, tuple(names), pairs)]
  transfers between devices with their start and end apart: 28 -> 35, of which waited for: 15 -> 21; matrix products, arithmetic and copies ran while one was open for 7% -> 1% of each run, Pallas kernels for 0% -> 4%
where the time goes in v2:
time: 71.7 us; the launch traced here: 71.5 us
  starting transfers between devices  31.2 us (44%)
  waiting for transfers between devices  29.9 us (42%)
  Pallas kernels  8.77 us (12%)
  between operations  0.77 us (1%)
    ppermute x35, starting transfers between devices, xor_permute(): return lax.ppermute(value, tuple(names), pairs)  31.2 us
    ppermute x35, waiting for transfers between devices, xor_permute(): return lax.ppermute(value, tuple(names), pairs)  29.9 us
    pallas_call x1, Pallas kernels, local(): pl.pallas_call(functools.partial(forward_kernel, count, width, n_z, len(k...  2.64 us
    pallas_call x1, Pallas kernels, local(): pl.pallas_call(functools.partial(backward_kernel, count, width, n_z), out...  2.25 us
  transfers between devices with their start and end apart: 35, of which 21 were waited for; matrix products, arithmetic and copies ran while one was open for 1% of the time, Pallas kernels for 4%

profile of v2, /device:TPU:0, one launch (start us, length us, event | category | flops | bytes accessed | tf_op | source)
XLA Modules:
  0.0 71.5 jit_solution(11214699836183818954)
XLA Ops:
  0.6 1.4 %pack.1 = (bf16[176,256]{1,0:T(8,128)(2,1)S(1)}, bf16[176,256]{1,0:T(8,128)(2,1)S(1)}, bf16[160,3072]{1,0:T(8,128)(2,1)S(1)}) custom-call(bf16[160,128]{1,0:T(8,128)(2,1)} %q_hbm.1, bf16[160,128]{1,0:T(8,128)(2,1)} %k_hbm.1, bf16[160,128]{1,0:T(8,128)(2,1)} %v_hbm.1, bf16[160,128]{1,0:T(8,128)(2,1)} %o_hbm.1, bf16[160,128]{1,0:T(8,128)(2,1)} %g_hbm.1, ...), custom_call_target="tpu_custom_call" | custom-call | tf_op jit(solution)/shard_map/pack/pallas_call | solution.py:325
  2.1 4.0 %collective-permute-start.5 = (bf16[176,256]{1,0:T(8,128)(2,1)S(1)}, bf16[176,256]{1,0:T(8,128)(2,1)S(1)}, u32[]{:S(2)}, u32[]{:S(2)}) collective-permute-start(bf16[176,256]{1,0:T(8,128)(2,1)S(1)} %get-tuple-element.45), channel_id=1, source_target_pairs={{0,18},{2,16},{16,2},{18,0},{1,19},{3,17},{17,3},{19,1},{4,22},{6,... | collective-permute-start | bytes 270344 | tf_op jit(solution)/shard_map/ppermute | solution.py:302
  6.0 0.5 collective-permute-start.4
  6.6 0.1 collective-permute-start.3
  6.7 4.0 %collective-permute-start.2 = (bf16[176,256]{1,0:T(8,128)(2,1)S(1)}, bf16[176,256]{1,0:T(8,128)(2,1)S(1)}, u32[]{:S(2)}, u32[]{:S(2)}) collective-permute-start(bf16[176,256]{1,0:T(8,128)(2,1)S(1)} %get-tuple-element.44.refs_0_.refs_4_), channel_id=1, source_target_pairs={{0,12},{4,8},{8,4},{12,0},{1,13},{5,9},{9,5},{13,1},{2,14},{6,10},... | collective-permute-start | bytes 270344 | tf_op jit(solution)/shard_map/ppermute | solution.py:302
  10.7 0.7 deal.1
  11.3 0.6 collective-permute-start
  12.0 0.5 collective-permute-start.7
  12.5 1.5 %collective-permute-done.2.refs_3_.refs_7_ = bf16[176,256]{1,0:T(8,128)(2,1)S(1)} collective-permute-done((bf16[176,256]{1,0:T(8,128)(2,1)S(1)}, bf16[176,256]{1,0:T(8,128)(2,1)S(1)}, u32[]{:S(2)}, u32[]{:S(2)}) %collective-permute-start.2) | collective-permute-done | bytes 90144 | tf_op jit(solution)/shard_map/ppermute | solution.py:302
  13.9 3.6 %collective-permute-done.1.refs_2_.refs_6_ = bf16[176,256]{1,0:T(8,128)(2,1)S(1)} collective-permute-done((bf16[176,256]{1,0:T(8,128)(2,1)S(1)}, bf16[176,256]{1,0:T(8,128)(2,1)S(1)}, u32[]{:S(2)}, u32[]{:S(2)}) %collective-permute-start.1) | collective-permute-done | bytes 90144 | tf_op jit(solution)/shard_map/ppermute | solution.py:302
  17.5 0.1 collective-permute-done.refs_1_.refs_5_
  17.7 1.1 %collective-permute-done.9 = bf16[176,256]{1,0:T(8,128)(2,1)S(1)} collective-permute-done((bf16[176,256]{1,0:T(8,128)(2,1)S(1)}, bf16[176,256]{1,0:T(8,128)(2,1)S(1)}, u32[]{:S(2)}, u32[]{:S(2)}) %collective-permute-start.9) | collective-permute-done | bytes 90144 | tf_op jit(solution)/shard_map/ppermute | solution.py:302
  18.8 2.6 %forward.1 = (bf16[8,160,640]{2,1,0:T(8,128)(2,1)S(1)}, bf16[8,160,640]{2,1,0:T(8,128)(2,1)S(1)}, f32[8,640]{1,0:T(8,128)S(1)}, f32[160,128]{1,0:T(8,128)S(1)}, ...) custom-call(bf16[176,256]{1,0:T(8,128)(2,1)S(1)} %get-tuple-element.44.refs_0_.refs_4_, ...), custom_call_target="tpu_custom_call" | custom-call | tf_op jit(solution)/shard_map/forward/pallas_call | solution.py:378
  21.5 2.5 %collective-permute-start.13 = (bf16[2,160,384]{2,1,0:T(8,128)(2,1)S(1)}, bf16[2,160,384]{2,1,0:T(8,128)(2,1)S(1)}, u32[]{:S(2)}, u32[]{:S(2)}) collective-permute-start(bf16[2,160,384]{2,1,0:T(8,128)(2,1)S(1)} %get-tuple-element.66), channel_id=1, source_target_pairs={{0,18},{2,16},{16,2},{18,0},{1,19},{3,17},{17,3},{19,1},{4,22},{6,... | collective-permute-start | bytes 737288 | tf_op jit(solution)/shard_map/ppermute | solution.py:302
  24.0 2.9 %collective-permute-start.11 = (bf16[176,128]{1,0:T(8,128)(2,1)S(1)}, bf16[176,128]{1,0:T(8,128)(2,1)S(1)}, u32[]{:S(2)}, u32[]{:S(2)}) collective-permute-start(bf16[176,128]{1,0:T(8,128)(2,1)S(1)} %get-tuple-element.64), channel_id=1, source_target_pairs={{0,8},{4,12},{8,0},{12,4},{1,9},{5,13},{9,1},{13,5},{2,10},{6,14},... | collective-permute-start | bytes 135176 | tf_op jit(solution)/shard_map/ppermute | solution.py:302
  26.9 1.4 %collective-permute-start.12 = (bf16[176,128]{1,0:T(8,128)(2,1)S(1)}, bf16[176,128]{1,0:T(8,128)(2,1)S(1)}, u32[]{:S(2)}, u32[]{:S(2)}) collective-permute-start(bf16[176,128]{1,0:T(8,128)(2,1)S(1)} %get-tuple-element.65), channel_id=1, source_target_pairs={{0,12},{4,8},{8,4},{12,0},{1,13},{5,9},{9,5},{13,1},{2,14},{6,10},... | collective-permute-start | bytes 135176 | tf_op jit(solution)/shard_map/ppermute | solution.py:302
  28.4 0.5 collective-permute-start.14
  28.9 0.5 collective-permute-start.15
  29.4 0.4 collective-permute-done.11.refs_9_
  29.8 2.9 %collective-permute-done.12.refs_10_ = bf16[176,128]{1,0:T(8,128)(2,1)S(1)} collective-permute-done((bf16[176,128]{1,0:T(8,128)(2,1)S(1)}, bf16[176,128]{1,0:T(8,128)(2,1)S(1)}, u32[]{:S(2)}, u32[]{:S(2)}) %collective-permute-start.12) | collective-permute-done | bytes 45088 | tf_op jit(solution)/shard_map/ppermute | solution.py:302
  32.8 2.2 %backward.1 = (f32[4,160,256]{2,1,0:T(8,128)S(1)}, bf16[4,160,256]{2,1,0:T(8,128)(2,1)S(1)}, bf16[160,128]{1,0:T(8,128)(2,1)}) custom-call(bf16[8,160,640]{2,1,0:T(8,128)(2,1)S(1)} %get-tuple-element.54.refs_0_, bf16[8,160,640]{2,1,0:T(8,128)(2,1)S(1)} %get-tuple-element.55.refs_1_, f32[8,640]{1,0:T(8,128)S(1)} %get-tuple-element.61.refs_2_, ...), custom_call_target="tpu_custom_call" | custom-call | flops 30000001024 | tf_op jit(solution)/shard_map/backward/pallas_call | solution.py:412
  35.0 0.7 collective-permute-done.14.refs_1_
  35.8 1.6 %collective-permute-done.16 = bf16[4,160,256]{2,1,0:T(8,128)(2,1)S(1)} collective-permute-done((bf16[4,160,256]{2,1,0:T(8,128)(2,1)S(1)}, bf16[4,160,256]{2,1,0:T(8,128)(2,1)S(1)}, u32[]{:S(2)}, u32[]{:S(2)}) %collective-permute-start.16) | collective-permute-done | bytes 327712 | tf_op jit(solution)/shard_map/ppermute | solution.py:302
  37.4 0.1 fusion.5
  37.5 1.5 %collective-permute-start.17 = (bf16[160,256]{1,0:T(8,128)(2,1)S(1)}, bf16[160,256]{1,0:T(8,128)(2,1)S(1)}, u32[]{:S(2)}, u32[]{:S(2)}) collective-permute-start(bf16[160,256]{1,0:T(8,128)(2,1)S(1)} %get-tuple-element.88), channel_id=1, source_target_pairs={{0,2},{2,0},{16,18},{18,16},{1,3},{3,1},{17,19},{19,17},{4,6},{6,4... | collective-permute-start | bytes 245768 | tf_op jit(solution)/shard_map/ppermute | solution.py:302
  39.1 1.5 %collective-permute-start.19 = (bf16[160,256]{1,0:T(8,128)(2,1)S(1)}, bf16[160,256]{1,0:T(8,128)(2,1)S(1)}, u32[]{:S(2)}, u32[]{:S(2)}) collective-permute-start(bf16[160,256]{1,0:T(8,128)(2,1)S(1)} %get-tuple-element.89), channel_id=1, source_target_pairs={{0,18},{2,16},{16,2},{18,0},{1,19},{3,17},{17,3},{19,1},{4,22},{6,... | collective-permute-start | bytes 245768 | tf_op jit(solution)/shard_map/ppermute | solution.py:302
  40.6 0.5 collective-permute-start.18
  41.1 0.5 collective-permute-start.23
  41.6 0.7 collective-permute-done.17
  42.3 2.9 %collective-permute-done.19 = bf16[160,256]{1,0:T(8,128)(2,1)S(1)} collective-permute-done((bf16[160,256]{1,0:T(8,128)(2,1)S(1)}, bf16[160,256]{1,0:T(8,128)(2,1)S(1)}, u32[]{:S(2)}, u32[]{:S(2)}) %collective-permute-start.19) | collective-permute-done | bytes 81952 | tf_op jit(solution)/shard_map/ppermute | solution.py:302
  45.4 2.2 %collective-permute-start.26 = (bf16[160,384]{1,0:T(8,128)(2,1)S(1)}, bf16[160,384]{1,0:T(8,128)(2,1)S(1)}, u32[]{:S(2)}, u32[]{:S(2)}) collective-permute-start(bf16[160,384]{1,0:T(8,128)(2,1)S(1)} %pad_maximum_fusion.refs_8_), channel_id=1, source_target_pairs={{0,18},{2,16},{16,2},{18,0},{1,19},{3,17},{17,3},{19,1},{4,22},{6,... | collective-permute-start | bytes 368648 | tf_op jit(solution)/shard_map/ppermute | solution.py:302
  47.6 0.8 %collective-permute-start.25 = (bf16[160,384]{1,0:T(8,128)(2,1)S(1)}, bf16[160,384]{1,0:T(8,128)(2,1)S(1)}, u32[]{:S(2)}, u32[]{:S(2)}) collective-permute-start(bf16[160,384]{1,0:T(8,128)(2,1)S(1)} %pad_maximum_fusion.refs_8_), channel_id=1, source_target_pairs={{0,16},{2,18},{16,0},{18,2},{1,17},{3,19},{17,1},{19,3},{4,20},{6,... | collective-permute-start | bytes 368648 | tf_op jit(solution)/shard_map/ppermute | solution.py:302
  48.4 0.6 collective-permute-start.24
  48.9 3.5 %collective-permute-done.26.refs_11_ = bf16[160,384]{1,0:T(8,128)(2,1)S(1)} collective-permute-done((bf16[160,384]{1,0:T(8,128)(2,1)S(1)}, bf16[160,384]{1,0:T(8,128)(2,1)S(1)}, u32[]{:S(2)}, u32[]{:S(2)}) %collective-permute-start.26) | collective-permute-done | bytes 122912 | tf_op jit(solution)/shard_map/ppermute | solution.py:302
  52.5 1.2 %collective-permute-done.25.refs_10_ = bf16[160,384]{1,0:T(8,128)(2,1)S(1)} collective-permute-done((bf16[160,384]{1,0:T(8,128)(2,1)S(1)}, bf16[160,384]{1,0:T(8,128)(2,1)S(1)}, u32[]{:S(2)}, u32[]{:S(2)}) %collective-permute-start.25) | collective-permute-done | bytes 122912 | tf_op jit(solution)/shard_map/ppermute | solution.py:302
  53.7 0.9 %collective-permute-done.24.refs_9_ = bf16[160,384]{1,0:T(8,128)(2,1)S(1)} collective-permute-done((bf16[160,384]{1,0:T(8,128)(2,1)S(1)}, bf16[160,384]{1,0:T(8,128)(2,1)S(1)}, u32[]{:S(2)}, u32[]{:S(2)}) %collective-permute-start.24) | collective-permute-done | bytes 122912 | tf_op jit(solution)/shard_map/ppermute | solution.py:302
  54.6 0.4 collective-permute-done.29.refs_14_
  55.0 0.9 %collective-permute-done.28.refs_13_ = bf16[160,384]{1,0:T(8,128)(2,1)S(1)} collective-permute-done((bf16[160,384]{1,0:T(8,128)(2,1)S(1)}, bf16[160,384]{1,0:T(8,128)(2,1)S(1)}, u32[]{:S(2)}, u32[]{:S(2)}) %collective-permute-start.28) | collective-permute-done | bytes 122912 | tf_op jit(solution)/shard_map/ppermute | solution.py:302
  56.0 1.1 %weights.1 = (f32[96,384]{1,0:T(8,128)S(1)}, bf16[96,384]{1,0:T(8,128)(2,1)S(1)}, bf16[96,384]{1,0:T(8,128)(2,1)S(1)}, bf16[96,384]{1,0:T(8,128)(2,1)S(1)}) custom-call(bf16[2,160,384]{2,1,0:T(8,128)(2,1)S(1)} %get-tuple-element.76.refs_0_, bf16[2,160,384]{2,1,0:T(8,128)(2,1)S(1)} %collective-permute-done.14.refs_1_, ...), custom_call_target="tpu_custom_call" | custom-call | tf_op jit(solution)/shard_map/weights/pallas_call | solution.py:442
  57.1 2.9 %collective-permute-start.32 = (bf16[96,384]{1,0:T(8,128)(2,1)S(1)}, bf16[96,384]{1,0:T(8,128)(2,1)S(1)}, u32[]{:S(2)}, u32[]{:S(2)}) collective-permute-start(bf16[96,384]{1,0:T(8,128)(2,1)S(1)} %get-tuple-element.82), channel_id=1, source_target_pairs={{0,8},{4,12},{8,0},{12,4},{1,9},{5,13},{9,1},{13,5},{2,10},{6,14},... | collective-permute-start | bytes 221192 | tf_op jit(solution)/shard_map/ppermute | solution.py:302
  60.0 1.4 %collective-permute-start.33 = (bf16[96,384]{1,0:T(8,128)(2,1)S(1)}, bf16[96,384]{1,0:T(8,128)(2,1)S(1)}, u32[]{:S(2)}, u32[]{:S(2)}) collective-permute-start(bf16[96,384]{1,0:T(8,128)(2,1)S(1)} %get-tuple-element.83), channel_id=1, source_target_pairs={{0,12},{4,8},{8,4},{12,0},{1,13},{5,9},{9,5},{13,1},{2,14},{6,10},... | collective-permute-start | bytes 221192 | tf_op jit(solution)/shard_map/ppermute | solution.py:302
  61.5 1.1 %collective-permute-done.31 = bf16[96,384]{1,0:T(8,128)(2,1)S(1)} collective-permute-done((bf16[96,384]{1,0:T(8,128)(2,1)S(1)}, bf16[96,384]{1,0:T(8,128)(2,1)S(1)}, u32[]{:S(2)}, u32[]{:S(2)}) %collective-permute-start.31) | collective-permute-done | bytes 73760 | tf_op jit(solution)/shard_map/ppermute | solution.py:302
  62.6 2.7 %collective-permute-done.32 = bf16[96,384]{1,0:T(8,128)(2,1)S(1)} collective-permute-done((bf16[96,384]{1,0:T(8,128)(2,1)S(1)}, bf16[96,384]{1,0:T(8,128)(2,1)S(1)}, u32[]{:S(2)}, u32[]{:S(2)}) %collective-permute-start.32) | collective-permute-done | bytes 73760 | tf_op jit(solution)/shard_map/ppermute | solution.py:302
  65.3 1.0 %collective-permute-done.33 = bf16[96,384]{1,0:T(8,128)(2,1)S(1)} collective-permute-done((bf16[96,384]{1,0:T(8,128)(2,1)S(1)}, bf16[96,384]{1,0:T(8,128)(2,1)S(1)}, u32[]{:S(2)}, u32[]{:S(2)}) %collective-permute-start.33) | collective-permute-done | bytes 73760 | tf_op jit(solution)/shard_map/ppermute | solution.py:302
  66.3 1.4 %collective-permute-start.34 = (bf16[96,384]{1,0:T(8,128)(2,1)S(1)}, bf16[96,384]{1,0:T(8,128)(2,1)S(1)}, u32[]{:S(2)}, u32[]{:S(2)}) collective-permute-start(bf16[96,384]{1,0:T(8,128)(2,1)S(1)} %get-tuple-element.84), channel_id=1, source_target_pairs={{0,16},{16,0},{1,17},{17,1},{2,18},{18,2},{3,19},{19,3},{4,20},{20... | collective-permute-start | bytes 221192 | tf_op jit(solution)/shard_map/ppermute | solution.py:302
  67.8 0.6 fusion.6
  68.4 2.4 %collective-permute-done.34.refs_0_ = bf16[96,384]{1,0:T(8,128)(2,1)S(1)} collective-permute-done((bf16[96,384]{1,0:T(8,128)(2,1)S(1)}, bf16[96,384]{1,0:T(8,128)(2,1)S(1)}, u32[]{:S(2)}, u32[]{:S(2)}) %collective-permute-start.34) | collective-permute-done | bytes 73760 | tf_op jit(solution)/shard_map/ppermute | solution.py:302
  70.8 0.7 %assemble.1 = f32[2,96,384]{2,1,0:T(8,128)} custom-call(f32[96,384]{1,0:T(8,128)S(1)} %get-tuple-element.85.own_ref, bf16[96,384]{1,0:T(8,128)(2,1)S(1)} %collective-permute-done.34.refs_0_), custom_call_target="tpu_custom_call" | custom-call | tf_op jit(solution)/shard_map/assemble/pallas_call | solution.py:458
  (36 shorter events, 0.4 us)
Async XLA Ops:
  2.1 9.3 %collective-permute-start.5 = (bf16[176,256]{1,0:T(8,128)(2,1)S(1)}, bf16[176,256]{1,0:T(8,128)(2,1)S(1)}, u32[]{:S(2)}, u32[]{:S(2)}) collective-permute-start(bf16[176,256]{1,0:T(8,128)(2,1)S(1)} %get-tuple-element.45), channel_id=1, source_target_pairs={{0,18},{2,16},{16,2},{18,0},{1,19},{3,17},{17,3},{19,1},{4,22},{6,... | collective-permute-start | bytes 270344 | tf_op jit(solution)/shard_map/ppermute | solution.py:302
  6.0 6.0 %collective-permute-start.4 = (bf16[176,256]{1,0:T(8,128)(2,1)S(1)}, bf16[176,256]{1,0:T(8,128)(2,1)S(1)}, u32[]{:S(2)}, u32[]{:S(2)}) collective-permute-start(bf16[176,256]{1,0:T(8,128)(2,1)S(1)} %get-tuple-element.45), channel_id=1, source_target_pairs={{0,16},{2,18},{16,0},{18,2},{1,17},{3,19},{17,1},{19,3},{4,20},{6,... | collective-permute-start | bytes 270344 | tf_op jit(solution)/shard_map/ppermute | solution.py:302
  6.6 5.4 %collective-permute-start.3 = (bf16[176,256]{1,0:T(8,128)(2,1)S(1)}, bf16[176,256]{1,0:T(8,128)(2,1)S(1)}, u32[]{:S(2)}, u32[]{:S(2)}) collective-permute-start(bf16[176,256]{1,0:T(8,128)(2,1)S(1)} %get-tuple-element.45), channel_id=1, source_target_pairs={{0,2},{2,0},{16,18},{18,16},{1,3},{3,1},{17,19},{19,17},{4,6},{6,4... | collective-permute-start | bytes 270344 | tf_op jit(solution)/shard_map/ppermute | solution.py:302
  6.7 7.3 %collective-permute-start.2 = (bf16[176,256]{1,0:T(8,128)(2,1)S(1)}, bf16[176,256]{1,0:T(8,128)(2,1)S(1)}, u32[]{:S(2)}, u32[]{:S(2)}) collective-permute-start(bf16[176,256]{1,0:T(8,128)(2,1)S(1)} %get-tuple-element.44.refs_0_.refs_4_), channel_id=1, source_target_pairs={{0,12},{4,8},{8,4},{12,0},{1,13},{5,9},{9,5},{13,1},{2,14},{6,10},... | collective-permute-start | bytes 270344 | tf_op jit(solution)/shard_map/ppermute | solution.py:302
  10.7 6.9 %collective-permute-start.1 = (bf16[176,256]{1,0:T(8,128)(2,1)S(1)}, bf16[176,256]{1,0:T(8,128)(2,1)S(1)}, u32[]{:S(2)}, u32[]{:S(2)}) collective-permute-start(bf16[176,256]{1,0:T(8,128)(2,1)S(1)} %get-tuple-element.44.refs_0_.refs_4_), channel_id=1, source_target_pairs={{0,8},{4,12},{8,0},{12,4},{1,9},{5,13},{9,1},{13,5},{2,10},{6,14},... | collective-permute-start | bytes 270344 | tf_op jit(solution)/shard_map/ppermute | solution.py:302
  11.3 6.3 %collective-permute-start = (bf16[176,256]{1,0:T(8,128)(2,1)S(1)}, bf16[176,256]{1,0:T(8,128)(2,1)S(1)}, u32[]{:S(2)}, u32[]{:S(2)}) collective-permute-start(bf16[176,256]{1,0:T(8,128)(2,1)S(1)} %get-tuple-element.44.refs_0_.refs_4_), channel_id=1, source_target_pairs={{0,4},{4,0},{8,12},{12,8},{1,5},{5,1},{9,13},{13,9},{2,6},{6,2},{1... | collective-permute-start | bytes 270344 | tf_op jit(solution)/shard_map/ppermute | solution.py:302
  12.0 5.7 %collective-permute-start.6 = (bf16[176,256]{1,0:T(8,128)(2,1)S(1)}, bf16[176,256]{1,0:T(8,128)(2,1)S(1)}, u32[]{:S(2)}, u32[]{:S(2)}) collective-permute-start(bf16[176,256]{1,0:T(8,128)(2,1)S(1)} %get-tuple-element.45), channel_id=1, source_target_pairs={{0,1},{1,0},{2,3},{3,2},{4,5},{5,4},{6,7},{7,6},{8,9},{9,8},{10,11... | collective-permute-start | bytes 270344 | tf_op jit(solution)/shard_map/ppermute | solution.py:302
  12.0 5.7 %collective-permute-start.7 = (bf16[176,256]{1,0:T(8,128)(2,1)S(1)}, bf16[176,256]{1,0:T(8,128)(2,1)S(1)}, u32[]{:S(2)}, u32[]{:S(2)}) collective-permute-start(bf16[176,256]{1,0:T(8,128)(2,1)S(1)} %collective-permute-done.3), channel_id=1, source_target_pairs={{0,1},{1,0},{2,3},{3,2},{4,5},{5,4},{6,7},{7,6},{8,9},{9,8},{10,11... | collective-permute-start | bytes 270344 | tf_op jit(solution)/shard_map/ppermute | solution.py:302
  13.9 3.7 %collective-permute-start.8 = (bf16[176,256]{1,0:T(8,128)(2,1)S(1)}, bf16[176,256]{1,0:T(8,128)(2,1)S(1)}, u32[]{:S(2)}, u32[]{:S(2)}) collective-permute-start(bf16[176,256]{1,0:T(8,128)(2,1)S(1)} %collective-permute-done.4), channel_id=1, source_target_pairs={{0,1},{1,0},{2,3},{3,2},{4,5},{5,4},{6,7},{7,6},{8,9},{9,8},{10,11... | collective-permute-start | bytes 270344 | tf_op jit(solution)/shard_map/ppermute | solution.py:302
  17.5 1.3 %collective-permute-start.9 = (bf16[176,256]{1,0:T(8,128)(2,1)S(1)}, bf16[176,256]{1,0:T(8,128)(2,1)S(1)}, u32[]{:S(2)}, u32[]{:S(2)}) collective-permute-start(bf16[176,256]{1,0:T(8,128)(2,1)S(1)} %collective-permute-done.5), channel_id=1, source_target_pairs={{0,1},{1,0},{2,3},{3,2},{4,5},{5,4},{6,7},{7,6},{8,9},{9,8},{10,11... | collective-permute-start | bytes 270344 | tf_op jit(solution)/shard_map/ppermute | solution.py:302
  21.5 11.3 %collective-permute-start.13 = (bf16[2,160,384]{2,1,0:T(8,128)(2,1)S(1)}, bf16[2,160,384]{2,1,0:T(8,128)(2,1)S(1)}, u32[]{:S(2)}, u32[]{:S(2)}) collective-permute-start(bf16[2,160,384]{2,1,0:T(8,128)(2,1)S(1)} %get-tuple-element.66), channel_id=1, source_target_pairs={{0,18},{2,16},{16,2},{18,0},{1,19},{3,17},{17,3},{19,1},{4,22},{6,... | collective-permute-start | bytes 737288 | tf_op jit(solution)/shard_map/ppermute | solution.py:302
  24.0 4.9 %collective-permute-start.10 = (bf16[176,128]{1,0:T(8,128)(2,1)S(1)}, bf16[176,128]{1,0:T(8,128)(2,1)S(1)}, u32[]{:S(2)}, u32[]{:S(2)}) collective-permute-start(bf16[176,128]{1,0:T(8,128)(2,1)S(1)} %get-tuple-element.63), channel_id=1, source_target_pairs={{0,4},{4,0},{8,12},{12,8},{1,5},{5,1},{9,13},{13,9},{2,6},{6,2},{1... | collective-permute-start | bytes 135176 | tf_op jit(solution)/shard_map/ppermute | solution.py:302
  24.0 5.8 %collective-permute-start.11 = (bf16[176,128]{1,0:T(8,128)(2,1)S(1)}, bf16[176,128]{1,0:T(8,128)(2,1)S(1)}, u32[]{:S(2)}, u32[]{:S(2)}) collective-permute-start(bf16[176,128]{1,0:T(8,128)(2,1)S(1)} %get-tuple-element.64), channel_id=1, source_target_pairs={{0,8},{4,12},{8,0},{12,4},{1,9},{5,13},{9,1},{13,5},{2,10},{6,14},... | collective-permute-start | bytes 135176 | tf_op jit(solution)/shard_map/ppermute | solution.py:302
  26.9 5.8 %collective-permute-start.12 = (bf16[176,128]{1,0:T(8,128)(2,1)S(1)}, bf16[176,128]{1,0:T(8,128)(2,1)S(1)}, u32[]{:S(2)}, u32[]{:S(2)}) collective-permute-start(bf16[176,128]{1,0:T(8,128)(2,1)S(1)} %get-tuple-element.65), channel_id=1, source_target_pairs={{0,12},{4,8},{8,4},{12,0},{1,13},{5,9},{9,5},{13,1},{2,14},{6,10},... | collective-permute-start | bytes 135176 | tf_op jit(solution)/shard_map/ppermute | solution.py:302
  28.4 7.3 %collective-permute-start.14 = (bf16[2,160,384]{2,1,0:T(8,128)(2,1)S(1)}, bf16[2,160,384]{2,1,0:T(8,128)(2,1)S(1)}, u32[]{:S(2)}, u32[]{:S(2)}) collective-permute-start(bf16[2,160,384]{2,1,0:T(8,128)(2,1)S(1)} %get-tuple-element.73), channel_id=1, source_target_pairs={{0,2},{2,0},{16,18},{18,16},{1,3},{3,1},{17,19},{19,17},{4,6},{6,4... | collective-permute-start | bytes 737288 | tf_op jit(solution)/shard_map/ppermute | solution.py:302
  28.9 6.9 %collective-permute-start.15 = (bf16[2,160,384]{2,1,0:T(8,128)(2,1)S(1)}, bf16[2,160,384]{2,1,0:T(8,128)(2,1)S(1)}, u32[]{:S(2)}, u32[]{:S(2)}) collective-permute-start(bf16[2,160,384]{2,1,0:T(8,128)(2,1)S(1)} %get-tuple-element.74), channel_id=1, source_target_pairs={{0,16},{2,18},{16,0},{18,2},{1,17},{3,19},{17,1},{19,3},{4,20},{6,... | collective-permute-start | bytes 737288 | tf_op jit(solution)/shard_map/ppermute | solution.py:302
  35.0 10.3 %copy-start = (bf16[160,128]{1,0:T(8,128)(2,1)S(1)}, bf16[160,128]{1,0:T(8,128)(2,1)}, u32[]{:S(2)}) copy-start(bf16[160,128]{1,0:T(8,128)(2,1)} %get-tuple-element.40) | copy-start | bytes 122884
  35.8 1.6 %collective-permute-start.16 = (bf16[4,160,256]{2,1,0:T(8,128)(2,1)S(1)}, bf16[4,160,256]{2,1,0:T(8,128)(2,1)S(1)}, u32[]{:S(2)}, u32[]{:S(2)}) collective-permute-start(bf16[4,160,256]{2,1,0:T(8,128)(2,1)S(1)} %get-tuple-element.75), channel_id=1, source_target_pairs={{0,1},{1,0},{2,3},{3,2},{4,5},{5,4},{6,7},{7,6},{8,9},{9,8},{10,11... | collective-permute-start | bytes 983048 | tf_op jit(solution)/shard_map/ppermute | solution.py:302
  37.5 4.7 %collective-permute-start.17 = (bf16[160,256]{1,0:T(8,128)(2,1)S(1)}, bf16[160,256]{1,0:T(8,128)(2,1)S(1)}, u32[]{:S(2)}, u32[]{:S(2)}) collective-permute-start(bf16[160,256]{1,0:T(8,128)(2,1)S(1)} %get-tuple-element.88), channel_id=1, source_target_pairs={{0,2},{2,0},{16,18},{18,16},{1,3},{3,1},{17,19},{19,17},{4,6},{6,4... | collective-permute-start | bytes 245768 | tf_op jit(solution)/shard_map/ppermute | solution.py:302
  39.1 6.1 %collective-permute-start.19 = (bf16[160,256]{1,0:T(8,128)(2,1)S(1)}, bf16[160,256]{1,0:T(8,128)(2,1)S(1)}, u32[]{:S(2)}, u32[]{:S(2)}) collective-permute-start(bf16[160,256]{1,0:T(8,128)(2,1)S(1)} %get-tuple-element.89), channel_id=1, source_target_pairs={{0,18},{2,16},{16,2},{18,0},{1,19},{3,17},{17,3},{19,1},{4,22},{6,... | collective-permute-start | bytes 245768 | tf_op jit(solution)/shard_map/ppermute | solution.py:302
  40.6 4.7 %collective-permute-start.18 = (bf16[160,256]{1,0:T(8,128)(2,1)S(1)}, bf16[160,256]{1,0:T(8,128)(2,1)S(1)}, u32[]{:S(2)}, u32[]{:S(2)}) collective-permute-start(bf16[160,256]{1,0:T(8,128)(2,1)S(1)} %get-tuple-element.90), channel_id=1, source_target_pairs={{0,16},{2,18},{16,0},{18,2},{1,17},{3,19},{17,1},{19,3},{4,20},{6,... | collective-permute-start | bytes 245768 | tf_op jit(solution)/shard_map/ppermute | solution.py:302
  41.1 6.5 %collective-permute-start.20 = (bf16[2,160,384]{2,1,0:T(8,128)(2,1)S(1)}, bf16[2,160,384]{2,1,0:T(8,128)(2,1)S(1)}, u32[]{:S(2)}, u32[]{:S(2)}) collective-permute-start(bf16[2,160,384]{2,1,0:T(8,128)(2,1)S(1)} %get-tuple-element.76.refs_0_), channel_id=1, source_target_pairs={{0,1},{1,0},{2,3},{3,2},{4,5},{5,4},{6,7},{7,6},{8,9},{9,8},{10,11... | collective-permute-start | bytes 737288 | tf_op jit(solution)/shard_map/ppermute | solution.py:302
  41.1 7.2 %collective-permute-start.23 = (bf16[2,160,384]{2,1,0:T(8,128)(2,1)S(1)}, bf16[2,160,384]{2,1,0:T(8,128)(2,1)S(1)}, u32[]{:S(2)}, u32[]{:S(2)}) collective-permute-start(bf16[2,160,384]{2,1,0:T(8,128)(2,1)S(1)} %collective-permute-done.13.refs_3_), channel_id=1, source_target_pairs={{0,1},{1,0},{2,3},{3,2},{4,5},{5,4},{6,7},{7,6},{8,9},{9,8},{10,11... | collective-permute-start | bytes 737288 | tf_op jit(solution)/shard_map/ppermute | solution.py:302
  42.3 6.6 %collective-permute-start.21 = (bf16[2,160,384]{2,1,0:T(8,128)(2,1)S(1)}, bf16[2,160,384]{2,1,0:T(8,128)(2,1)S(1)}, u32[]{:S(2)}, u32[]{:S(2)}) collective-permute-start(bf16[2,160,384]{2,1,0:T(8,128)(2,1)S(1)} %collective-permute-done.14.refs_1_), channel_id=1, source_target_pairs={{0,1},{1,0},{2,3},{3,2},{4,5},{5,4},{6,7},{7,6},{8,9},{9,8},{10,11... | collective-permute-start | bytes 737288 | tf_op jit(solution)/shard_map/ppermute | solution.py:302
  45.2 9.4 %collective-permute-start.22 = (bf16[2,160,384]{2,1,0:T(8,128)(2,1)S(1)}, bf16[2,160,384]{2,1,0:T(8,128)(2,1)S(1)}, u32[]{:S(2)}, u32[]{:S(2)}) collective-permute-start(bf16[2,160,384]{2,1,0:T(8,128)(2,1)S(1)} %collective-permute-done.15.refs_2_), channel_id=1, source_target_pairs={{0,1},{1,0},{2,3},{3,2},{4,5},{5,4},{6,7},{7,6},{8,9},{9,8},{10,11... | collective-permute-start | bytes 737288 | tf_op jit(solution)/shard_map/ppermute | solution.py:302
  45.4 7.1 %collective-permute-start.26 = (bf16[160,384]{1,0:T(8,128)(2,1)S(1)}, bf16[160,384]{1,0:T(8,128)(2,1)S(1)}, u32[]{:S(2)}, u32[]{:S(2)}) collective-permute-start(bf16[160,384]{1,0:T(8,128)(2,1)S(1)} %pad_maximum_fusion.refs_8_), channel_id=1, source_target_pairs={{0,18},{2,16},{16,2},{18,0},{1,19},{3,17},{17,3},{19,1},{4,22},{6,... | collective-permute-start | bytes 368648 | tf_op jit(solution)/shard_map/ppermute | solution.py:302
  47.6 6.1 %collective-permute-start.25 = (bf16[160,384]{1,0:T(8,128)(2,1)S(1)}, bf16[160,384]{1,0:T(8,128)(2,1)S(1)}, u32[]{:S(2)}, u32[]{:S(2)}) collective-permute-start(bf16[160,384]{1,0:T(8,128)(2,1)S(1)} %pad_maximum_fusion.refs_8_), channel_id=1, source_target_pairs={{0,16},{2,18},{16,0},{18,2},{1,17},{3,19},{17,1},{19,3},{4,20},{6,... | collective-permute-start | bytes 368648 | tf_op jit(solution)/shard_map/ppermute | solution.py:302
  48.4 6.3 %collective-permute-start.24 = (bf16[160,384]{1,0:T(8,128)(2,1)S(1)}, bf16[160,384]{1,0:T(8,128)(2,1)S(1)}, u32[]{:S(2)}, u32[]{:S(2)}) collective-permute-start(bf16[160,384]{1,0:T(8,128)(2,1)S(1)} %pad_maximum_fusion.refs_8_), channel_id=1, source_target_pairs={{0,2},{2,0},{16,18},{18,16},{1,3},{3,1},{17,19},{19,17},{4,6},{6,4... | collective-permute-start | bytes 368648 | tf_op jit(solution)/shard_map/ppermute | solution.py:302
  48.9 5.7 %collective-permute-start.27 = (bf16[160,384]{1,0:T(8,128)(2,1)S(1)}, bf16[160,384]{1,0:T(8,128)(2,1)S(1)}, u32[]{:S(2)}, u32[]{:S(2)}) collective-permute-start(bf16[160,384]{1,0:T(8,128)(2,1)S(1)} %pad_maximum_fusion.refs_8_), channel_id=1, source_target_pairs={{0,1},{1,0},{2,3},{3,2},{4,5},{5,4},{6,7},{7,6},{8,9},{9,8},{10,11... | collective-permute-start | bytes 368648 | tf_op jit(solution)/shard_map/ppermute | solution.py:302
  52.5 2.2 %collective-permute-start.30 = (bf16[160,384]{1,0:T(8,128)(2,1)S(1)}, bf16[160,384]{1,0:T(8,128)(2,1)S(1)}, u32[]{:S(2)}, u32[]{:S(2)}) collective-permute-start(bf16[160,384]{1,0:T(8,128)(2,1)S(1)} %collective-permute-done.26.refs_11_), channel_id=1, source_target_pairs={{0,1},{1,0},{2,3},{3,2},{4,5},{5,4},{6,7},{7,6},{8,9},{9,8},{10,11... | collective-permute-start | bytes 368648 | tf_op jit(solution)/shard_map/ppermute | solution.py:302
  53.7 1.3 %collective-permute-start.29 = (bf16[160,384]{1,0:T(8,128)(2,1)S(1)}, bf16[160,384]{1,0:T(8,128)(2,1)S(1)}, u32[]{:S(2)}, u32[]{:S(2)}) collective-permute-start(bf16[160,384]{1,0:T(8,128)(2,1)S(1)} %collective-permute-done.25.refs_10_), channel_id=1, source_target_pairs={{0,1},{1,0},{2,3},{3,2},{4,5},{5,4},{6,7},{7,6},{8,9},{9,8},{10,11... | collective-permute-start | bytes 368648 | tf_op jit(solution)/shard_map/ppermute | solution.py:302
  54.6 1.3 %collective-permute-start.28 = (bf16[160,384]{1,0:T(8,128)(2,1)S(1)}, bf16[160,384]{1,0:T(8,128)(2,1)S(1)}, u32[]{:S(2)}, u32[]{:S(2)}) collective-permute-start(bf16[160,384]{1,0:T(8,128)(2,1)S(1)} %collective-permute-done.24.refs_9_), channel_id=1, source_target_pairs={{0,1},{1,0},{2,3},{3,2},{4,5},{5,4},{6,7},{7,6},{8,9},{9,8},{10,11... | collective-permute-start | bytes 368648 | tf_op jit(solution)/shard_map/ppermute | solution.py:302
  57.0 5.6 %collective-permute-start.31 = (bf16[96,384]{1,0:T(8,128)(2,1)S(1)}, bf16[96,384]{1,0:T(8,128)(2,1)S(1)}, u32[]{:S(2)}, u32[]{:S(2)}) collective-permute-start(bf16[96,384]{1,0:T(8,128)(2,1)S(1)} %get-tuple-element.81), channel_id=1, source_target_pairs={{0,4},{4,0},{8,12},{12,8},{1,5},{5,1},{9,13},{13,9},{2,6},{6,2},{1... | collective-permute-start | bytes 221192 | tf_op jit(solution)/shard_map/ppermute | solution.py:302
  57.1 8.2 %collective-permute-start.32 = (bf16[96,384]{1,0:T(8,128)(2,1)S(1)}, bf16[96,384]{1,0:T(8,128)(2,1)S(1)}, u32[]{:S(2)}, u32[]{:S(2)}) collective-permute-start(bf16[96,384]{1,0:T(8,128)(2,1)S(1)} %get-tuple-element.82), channel_id=1, source_target_pairs={{0,8},{4,12},{8,0},{12,4},{1,9},{5,13},{9,1},{13,5},{2,10},{6,14},... | collective-permute-start | bytes 221192 | tf_op jit(solution)/shard_map/ppermute | solution.py:302
  60.0 6.3 %collective-permute-start.33 = (bf16[96,384]{1,0:T(8,128)(2,1)S(1)}, bf16[96,384]{1,0:T(8,128)(2,1)S(1)}, u32[]{:S(2)}, u32[]{:S(2)}) collective-permute-start(bf16[96,384]{1,0:T(8,128)(2,1)S(1)} %get-tuple-element.83), channel_id=1, source_target_pairs={{0,12},{4,8},{8,4},{12,0},{1,13},{5,9},{9,5},{13,1},{2,14},{6,10},... | collective-permute-start | bytes 221192 | tf_op jit(solution)/shard_map/ppermute | solution.py:302
  66.3 4.4 %collective-permute-start.34 = (bf16[96,384]{1,0:T(8,128)(2,1)S(1)}, bf16[96,384]{1,0:T(8,128)(2,1)S(1)}, u32[]{:S(2)}, u32[]{:S(2)}) collective-permute-start(bf16[96,384]{1,0:T(8,128)(2,1)S(1)} %get-tuple-element.84), channel_id=1, source_target_pairs={{0,16},{16,0},{1,17},{17,1},{2,18},{18,2},{3,19},{19,3},{4,20},{20... | collective-permute-start | bytes 221192 | tf_op jit(solution)/shard_map/ppermute | solution.py:302

commit v3 on v2

--- a/solution.py
+++ b/solution.py
@@ -19,6 +19,11 @@
 BF16 = jnp.bfloat16
 VMEM = pl.BlockSpec(memory_space=pltpu.VMEM)
 HBM = pl.BlockSpec(memory_space=pltpu.HBM)
+
+
+def plane_places(plane, n_y):
+    row_id, y_id = lax.axis_index("row"), lax.axis_index("y")
+    return [(row_id ^ a) * n_y + (y_id ^ b) for a, b in plane]
 
 
 def dot_nt(left, right, precision=None):
@@ -122,19 +127,24 @@
         out_ref[me_row ^ offset] = ref[...].astype(F32)
 
 
+def lines_kernel(count, width, n_q, *refs):
+    qg_refs, (queries, grads, rows) = refs[:n_q], refs[n_q:]
+    for slot, ref in enumerate(qg_refs):
+        where = slice(slot * count, (slot + 1) * count)
+        queries[where, :] = ref[:count, :width]
+        grads[where, :] = ref[:count, width:]
+        tail = ref[count:, :].astype(F32)
+        rows[0:1, where] = (tail[0:1] + tail[1:2] + tail[2:3])[:, :count]
+        rows[1:2, where] = tail[3:4, :count]
+
+
 def forward_kernel(count, width, n_q, n_kv, *refs):
-    qg_refs, refs = refs[:n_q], refs[n_q:]
+    queries, grads, rows, refs = *refs[:3], refs[3:]
     kv_refs, refs = refs[:n_kv], refs[n_kv:]
     w_ref, u_ref, stat_ref, own_ref, refs = *refs[:4], refs[4:]
-    send_refs, (queries, grads, keys, rows) = refs[: n_q - 1], refs[n_q - 1 :]
+    send_refs, keys = refs[: n_q - 1], refs[n_q - 1]
     total = n_q * count
     factor = LOG2E / math.sqrt(width)
-    for slot, ref in enumerate(qg_refs):
-        queries[slot * count : (slot + 1) * count, :] = ref[:count, :width]
-        grads[slot * count : (slot + 1) * count, :] = ref[:count, width:]
-        tail = ref[count:, :].astype(F32)
-        rows[0:1, slot * count : (slot + 1) * count] = (tail[0:1] + tail[1:2] + tail[2:3])[:, :count]
-        rows[1:2, slot * count : (slot + 1) * count] = tail[3:4, :count]
     delta = rows[0:1, :]
     query_ids = rows[1:2, :]
 
@@ -142,8 +152,9 @@
         base = 0
         for ref in kv_refs:
             depth = ref.shape[0]
-            if depth == 1:
-                state = body(ref.at[0], base, state)
+            if depth <= 4:
+                for i in range(depth):
+                    state = body(ref.at[i], base + i, state)
             else:
                 state = lax.fori_loop(
                     0, depth, lambda i, s, ref=ref, base=base: body(ref.at[i], base + i, s), state
@@ -200,22 +211,23 @@
     chunks = total // LANES
     parts = split_three(level)
     tail_rows = send_refs[0].shape[0] - count
-    lines = [part[:, c * LANES : (c + 1) * LANES] for part in parts for c in range(chunks)]
+    step = tail_rows // 4
     row = lax.broadcasted_iota(jnp.int32, (tail_rows, LANES), 0)
     tail = jnp.zeros((tail_rows, LANES), F32)
-    for place, line in enumerate(lines):
-        tail = jnp.where(row == place, line, tail)
+    for index, part in enumerate(parts):
+        for chunk in range(chunks):
+            line = part[:, chunk * LANES : (chunk + 1) * LANES]
+            tail = jnp.where(row == index * step + chunk, line, tail)
     tail = tail.astype(BF16)
     for slot, ref in enumerate(send_refs, 1):
         ref[:count, :] = query_part[slot * count : (slot + 1) * count].astype(BF16)
         ref[count:, :] = tail
 
 
-def backward_kernel(count, width, n_q, *refs):
-    w_ref, u_ref, stat_ref, own_ref, refs = *refs[:4], refs[4:]
-    qg_refs, refs = refs[:n_q], refs[n_q:]
+def backward_kernel(count, width, n_q, plane, n_y, *refs):
+    w_ref, u_ref, stat_ref, own_ref, all_queries, all_grads, refs = *refs[:6], refs[6:]
     got_refs, refs = refs[: n_q - 1], refs[n_q - 1 :]
-    mine_ref, other_ref, dq_ref, queries, grads = refs
+    mine_k_ref, mine_v_ref, other_k_ref, other_v_ref, dq_ref, queries, grads = refs
     total = n_q * count
     chunks = total // LANES
     scale = 1.0 / math.sqrt(width)
@@ -224,9 +236,8 @@
     levels = [[level[s * count : (s + 1) * count] for s in range(n_q)]]
     for offset, ref in enumerate(got_refs, 1):
         tail = ref[count:, :].astype(F32)
-        summed = tail[:chunks] + tail[chunks : 2 * chunks] + tail[2 * chunks : 3 * chunks]
-        summed = jnp.concatenate([summed, jnp.zeros((-chunks % 8, LANES), F32)], axis=0)
-        across = jnp.transpose(summed)
+        step = tail.shape[0] // 4
+        across = jnp.transpose(tail[:step] + tail[step : 2 * step] + tail[2 * step : 3 * step])
         column = jnp.concatenate([across[:, c : c + 1] for c in range(chunks)], axis=0)
         levels.append(
             [column[(s ^ offset) * count : ((s ^ offset) + 1) * count] for s in range(n_q)]
@@ -238,51 +249,59 @@
         mass = functools.reduce(jnp.add, shares)
         rows = slice(slot * count, (slot + 1) * count)
         share = jnp.exp2(peak[rows] - top) / mass
-        queries[rows, :] = (qg_refs[slot][:count, :width].astype(F32) * share).astype(BF16)
-        grads[rows, :] = (qg_refs[slot][:count, width:].astype(F32) * share).astype(BF16)
+        queries[rows, :] = (all_queries[rows, :].astype(F32) * share).astype(BF16)
+        grads[rows, :] = (all_grads[rows, :].astype(F32) * share).astype(BF16)
         if slot == 0:
             query_grad = own_ref[...] * shares[0]
             for one, ref in zip(shares[1:], got_refs):
                 query_grad = query_grad + ref[:count, :].astype(F32) * one
-            dq_ref[...] = (query_grad * (scale / mass)).astype(BF16)
+            dq_ref[...] = query_grad * (scale / mass)
 
     n_pieces = w_ref.shape[0]
     half = n_pieces // 2
 
-    def emit(first, size, ref, place):
+    def emit(first, size, places, key_ref, value_ref):
         many = (size * count, total)
+        shape = (size, count, width)
         value_part = jnp.dot(
             w_ref[pl.ds(first, size)].reshape(many), grads[...], preferred_element_type=F32
-        )
+        ).reshape(shape)
         key_part = jnp.dot(
             u_ref[pl.ds(first, size)].reshape(many), queries[...], preferred_element_type=F32
-        )
-        shape = (size, count, width)
-        ref[pl.ds(place, size), :, :width] = (key_part * scale).reshape(shape).astype(ref.dtype)
-        ref[pl.ds(place, size), :, width:] = value_part.reshape(shape).astype(ref.dtype)
-
+        ).reshape(shape)
+        for step, place in enumerate(places):
+            key_ref[place] = (key_part[step] * scale).astype(key_ref.dtype)
+            value_ref[place] = value_part[step].astype(value_ref.dtype)
+
+    places = plane_places(plane, n_y)
     if half <= 4:
-        emit(half, half, other_ref, 0)
-        emit(0, half, mine_ref, 0)
+        emit(half, half, places, other_k_ref, other_v_ref)
+        emit(0, half, places, mine_k_ref, mine_v_ref)
     else:
-
-        @pl.loop(0, half)
-        def _(i):
-            emit(half + i, 1, other_ref, i)
-            emit(i, 1, mine_ref, i)
-
-
-def weight_kernel(n_pairs, n_z, *refs):
+        for i, place in enumerate(places):
+            emit(half + i, 1, [place], other_k_ref, other_v_ref)
+            emit(i, 1, [place], mine_k_ref, mine_v_ref)
+
+
+def weight_kernel(plane, n_y, n_core, n_z, *refs):
+    n_plane = len(plane)
+    n_pairs = n_core * n_plane
     x_refs, refs = refs[:n_pairs], refs[n_pairs:]
-    g_refs, refs = refs[:n_pairs], refs[n_pairs:]
-    out_refs, sums = refs[:n_z], refs[n_z]
-    core_id = lax.axis_index("core")
-    total = None
-    for x_ref, g_ref in zip(x_refs, g_refs):
-        part = dot_tn(x_ref[core_id], g_ref[...])
-        total = part if total is None else total + part
-    sums[...] = total.reshape(sums.shape)
-    z_id = lax.axis_index("z")
+    g_refs, refs = refs[: 3 * n_core], refs[3 * n_core :]
+    out_refs, (inputs, grads, sums) = refs[:n_z], refs[n_z:]
+    count, width = g_refs[1].shape[1:]
+    places = plane_places(plane, n_y)
+    core_id, z_id = lax.axis_index("core"), lax.axis_index("z")
+    for core in range(n_core):
+        query_ref, key_ref, value_ref = g_refs[3 * core : 3 * core + 3]
+        for slot, place in enumerate(places):
+            index = core * n_plane + slot
+            rows = slice(index * count, (index + 1) * count)
+            inputs[rows, :] = x_refs[index][core_id]
+            grads[rows, :width] = query_ref[slot * count : (slot + 1) * count, :]
+            grads[rows, width : 2 * width] = key_ref[place]
+            grads[rows, 2 * width :] = value_ref[place]
+    sums[...] = dot_tn(inputs[...], grads[...]).reshape(sums.shape)
     for slot, ref in enumerate(out_refs):
         ref[...] = sums[z_id ^ slot].astype(ref.dtype)
 
@@ -365,16 +384,25 @@
         compiler_params=params(16 * MIB),
         name="deal",
     )(x_here)
-    kv_near[1:], x_send = lax.optimization_barrier((kv_near[1:], x_send))
-    kv_all = kv_near + [over_core(piece) for piece in kv_near]
-    if n_pieces <= 8:
-        kv_all = [piece[None] for piece in kv_all]
-    else:
-        kv_all = [jnp.stack(kv_all)]
-
-    mass_rows = 3 * total // LANES
-    tail_rows = -(-mass_rows // PAD_ROWS) * PAD_ROWS
+    stacked = jnp.stack(kv_near)
+    kv_all = [piece[None] for piece in kv_near] if n_pieces <= 8 else [stacked]
+    kv_all = kv_all + [over_core(stacked)]
+
+    tail_rows = 4 * -(-total // (8 * LANES)) * 8
     big = jax.ShapeDtypeStruct((n_pieces, count, total), BF16)
+    lines = pl.pallas_call(
+        functools.partial(lines_kernel, count, width, n_z),
+        out_shape=[
+            jax.ShapeDtypeStruct((total, width), BF16),
+            jax.ShapeDtypeStruct((total, width), BF16),
+            jax.ShapeDtypeStruct((8, total), F32),
+        ],
+        in_specs=[VMEM] * n_z,
+        out_specs=[VMEM] * 3,
+        compiler_params=params(8 * MIB),
+        cost_estimate=pl.CostEstimate(flops=int(5e9), bytes_accessed=0, transcendentals=0),
+        name="lines",
+    )(*qg_all)
     w, u, stat, own_part, *send = pl.pallas_call(
         functools.partial(forward_kernel, count, width, n_z, len(kv_all)),
         out_shape=[
@@ -384,19 +412,14 @@
             jax.ShapeDtypeStruct((count, width), F32),
         ]
         + [jax.ShapeDtypeStruct((count + tail_rows, width), BF16)] * (n_z - 1),
-        in_specs=[VMEM] * (n_z + len(kv_all)),
+        in_specs=[VMEM] * (3 + len(kv_all)),
         out_specs=[VMEM] * (4 + n_z - 1),
-        scratch_shapes=[
-            pltpu.VMEM((total, width), BF16),
-            pltpu.VMEM((total, width), BF16),
-            pltpu.VMEM((n_pieces, count, width), BF16),
-            pltpu.VMEM((8, total), F32),
-        ],
+        scratch_shapes=[pltpu.VMEM((n_pieces, count, width), BF16)],
         compiler_params=params(16 * MIB if n_pieces <= 8 else 56 * MIB),
+        cost_estimate=pl.CostEstimate(flops=int(3e10), bytes_accessed=0, transcendentals=0),
         name="forward",
-    )(*qg_all, *kv_all)
+    )(*lines, *kv_all)
     got = [over_z(piece, offset) for offset, piece in enumerate(send, 1)]
-    x_send, stat = lax.optimization_barrier((x_send, stat))
     x_all = [x_send[0]] + [over_plane(x, where) for x, where in zip(x_send[1:], plane[1:])]
     far = [index for index, (a, b) in enumerate(plane) if a and b]
     near = [index for index, (a, b) in enumerate(plane) if (a or b) and not (a and b)]
@@ -407,46 +430,63 @@
             x_all[index] = value
         return values
 
-    got = together(got, far)
-
-    mine, other, query_grad = pl.pallas_call(
-        functools.partial(backward_kernel, count, width, n_z),
-        out_shape=[
-            jax.ShapeDtypeStruct((n_pieces // 2, count, 2 * width), F32),
-            jax.ShapeDtypeStruct((n_pieces // 2, count, 2 * width), BF16),
-            jax.ShapeDtypeStruct((count, width), BF16),
-        ],
-        in_specs=[VMEM] * (4 + n_z + n_z - 1),
-        out_specs=[VMEM] * 3,
+    got = together(got, far + near)
+
+    half = (n_plane, count, width)
+    mine_k, mine_v, other_k, other_v, query_sum = pl.pallas_call(
+        functools.partial(backward_kernel, count, width, n_z, plane, n_y),
+        out_shape=[jax.ShapeDtypeStruct(half, F32 if n_pieces <= 8 else BF16)] * 2
+        + [jax.ShapeDtypeStruct(half, BF16)] * 2
+        + [jax.ShapeDtypeStruct((count, width), F32)],
+        in_specs=[VMEM] * (6 + n_z - 1),
+        out_specs=[VMEM] * 5,
         scratch_shapes=[pltpu.VMEM((total, width), BF16), pltpu.VMEM((total, width), BF16)],
         compiler_params=params(16 * MIB if n_pieces <= 8 else 56 * MIB),
         cost_estimate=pl.CostEstimate(flops=int(3e10), bytes_accessed=0, transcendentals=0),
         name="backward",
-    )(w, u, stat, own_part, *qg_all, *got)
-
-    other = together(other, near)
-    both = mine + over_core(other).astype(F32)
-
+    )(w, u, stat, own_part, *lines[:2], *got)
+    query_grad = query_sum.astype(BF16)
+
+    key_sum = mine_k.astype(F32) + over_core(other_k).astype(F32)
+    value_sum = mine_v.astype(F32) + over_core(other_v).astype(F32)
     x_pair = [over_core(x) for x in x_all]
-    arrived = [
-        over_plane(both[index].astype(BF16), where) for index, where in enumerate(plane[1:], 1)
-    ]
-    kv_sum = both[0]
-    for part in arrived:
-        kv_sum = kv_sum + part.astype(F32)
-    kv_grad = kv_sum.astype(BF16)
-    all_grads = jnp.concatenate([query_grad, kv_grad], axis=1)
-    g_all = [all_grads] + [over_plane(all_grads, where) for where in plane[1:]]
-    g_all = g_all + [over_core(g) for g in g_all]
+    row_bits = [(1 << bit, 0) for bit in range(n_row.bit_length() - 1)]
+    y_bits = [(0, 1 << bit) for bit in range(n_y.bit_length() - 1)]
+    query_pieces = {(0, 0): query_grad}
+    for key_hop, value_hop in zip(row_bits + y_bits, y_bits + row_bits):
+        offsets = list(query_pieces)
+        sent = [key_sum.astype(BF16).reshape(n_plane * count, width)]
+        sent = jnp.concatenate(sent + [query_pieces[offset] for offset in offsets])
+        sent, value_sent = lax.optimization_barrier((sent, value_sum.astype(BF16)))
+        key_got, value_got = lax.optimization_barrier(
+            (over_plane(sent, key_hop), over_plane(value_sent, value_hop))
+        )
+        key_sum = key_sum + key_got[: n_plane * count].reshape(half).astype(F32)
+        value_sum = value_sum + value_got.astype(F32)
+        for index, (a, b) in enumerate(offsets, n_plane):
+            piece = key_got[index * count : (index + 1) * count]
+            query_pieces[a ^ key_hop[0], b ^ key_hop[1]] = piece
+    place = plane_places(plane, n_y)[0]
+    key_low, value_low = key_sum.astype(BF16), value_sum.astype(BF16)
+    key_grad = lax.dynamic_index_in_dim(key_low, place, 0, False)
+    value_grad = lax.dynamic_index_in_dim(value_low, place, 0, False)
+    g_near = [jnp.concatenate([query_pieces[where] for where in plane]), key_low, value_low]
+    g_all = g_near + [over_core(g) for g in g_near]
+
     x_all = x_all + x_pair
+    rows = n_pieces * count
     mine, *send = pl.pallas_call(
-        functools.partial(weight_kernel, len(x_all), n_z),
+        functools.partial(weight_kernel, plane, n_y, n_core, n_z),
         out_shape=[jax.ShapeDtypeStruct((blk, 3 * width), F32)]
         + [jax.ShapeDtypeStruct((blk, 3 * width), BF16)] * (n_z - 1),
-        in_specs=[VMEM] * (2 * len(x_all)),
+        in_specs=[VMEM] * (n_pieces + 3 * n_core),
         out_specs=[VMEM] * n_z,
-        scratch_shapes=[pltpu.VMEM((n_z, blk, 3 * width), F32)],
-        compiler_params=params(24 * MIB),
+        scratch_shapes=[
+            pltpu.VMEM((rows, n_z * blk), BF16),
+            pltpu.VMEM((rows, 3 * width), BF16),
+            pltpu.VMEM((n_z, blk, 3 * width), F32),
+        ],
+        compiler_params=params(24 * MIB if n_pieces <= 8 else 56 * MIB),
         name="weights",
     )(*x_all, *g_all)
     both = [mine] + send
@@ -463,7 +503,7 @@
         compiler_params=params(8 * MIB),
         name="assemble",
     )(*parts).reshape(n_row * blk, 3 * width)
-    return query_grad, kv_grad[:, :width], kv_grad[:, width:], weight_grad
+    return query_grad, key_grad, value_grad, weight_grad
 
 
 def solution(mesh):

time: 71.7 us -> 67.7 us (0.944)
  waiting for transfers between devices: 29.9 us -> 25.2 us
    ppermute x35 -> x30, waiting for transfers between devices: 29.9 us -> 25.2 us  [xor_permute(): return lax.ppermute(value, tuple(names), pairs)]
    squeeze x0 -> x2, local copies, waits for them, and re-layouts: none -> 1.24 us  [the longest x1 0.62 us: local(): value_grad = lax.dynamic_index_in_dim(value_low, place, 0, False)]
    ppermute x35 -> x30, starting transfers between devices: 31.2 us -> 31.1 us  [xor_permute(): return lax.ppermute(value, tuple(names), pairs)]
    pallas_call x2 -> x3, Pallas kernels: 3.32 us -> 3.23 us  [the longest x1 2.27 us: local(): pl.pallas_call(functools.partial(backward_kernel, count, width, n_z, plan...]
  transfers between devices with their start and end apart: 35 -> 30, of which waited for: 21 -> 16; matrix products, arithmetic and copies ran while one was open for 1% -> 2% of each run, Pallas kernels for 4% -> 5%
where the time goes in v3:
time: 67.7 us; the launch traced here: 67.6 us
  starting transfers between devices  31.1 us (46%)
  waiting for transfers between devices  25.2 us (37%)
  Pallas kernels  8.66 us (13%)
  local copies, waits for them, and re-layouts  1.28 us (2%)
  between operations  0.82 us (1%)
    ppermute x30, starting transfers between devices, xor_permute(): return lax.ppermute(value, tuple(names), pairs)  31.1 us
    ppermute x30, waiting for transfers between devices, xor_permute(): return lax.ppermute(value, tuple(names), pairs)  25.2 us
    pallas_call x1, Pallas kernels, local(): pl.pallas_call(functools.partial(forward_kernel, count, width, n_z, len(k...  2.62 us
    pallas_call x1, Pallas kernels, local(): pl.pallas_call(functools.partial(backward_kernel, count, width, n_z, plan...  2.27 us
    pallas_call x1, Pallas kernels, local(): pl.pallas_call(functools.partial(pack_kernel, axes), out_shape=(packed, p...  1.41 us
  transfers between devices with their start and end apart: 30, of which 16 were waited for; matrix products, arithmetic and copies ran while one was open for 2% of the time, Pallas kernels for 5%

profile of v3, /device:TPU:0, one launch (start us, length us, event | category | flops | bytes accessed | tf_op | source)
XLA Modules:
  0.0 67.6 jit_solution(12922520965882918994)
XLA Ops:
  0.6 1.4 %pack.1 = (bf16[176,256]{1,0:T(8,128)(2,1)S(1)}, bf16[176,256]{1,0:T(8,128)(2,1)S(1)}, bf16[160,3072]{1,0:T(8,128)(2,1)S(1)}) custom-call(bf16[160,128]{1,0:T(8,128)(2,1)} %q_hbm.1, bf16[160,128]{1,0:T(8,128)(2,1)} %k_hbm.1, bf16[160,128]{1,0:T(8,128)(2,1)} %v_hbm.1, bf16[160,128]{1,0:T(8,128)(2,1)} %o_hbm.1, bf16[160,128]{1,0:T(8,128)(2,1)} %g_hbm.1, ...), custom_call_target="tpu_custom_call" | custom-call | tf_op jit(solution)/shard_map/pack/pallas_call | solution.py:344
  2.1 3.0 %collective-permute-start.3 = (bf16[176,256]{1,0:T(8,128)(2,1)S(1)}, bf16[176,256]{1,0:T(8,128)(2,1)S(1)}, u32[]{:S(2)}, u32[]{:S(2)}) collective-permute-start(bf16[176,256]{1,0:T(8,128)(2,1)S(1)} %get-tuple-element.48), channel_id=1, source_target_pairs={{0,2},{2,0},{16,18},{18,16},{1,3},{3,1},{17,19},{19,17},{4,6},{6,4... | collective-permute-start | bytes 270344 | tf_op jit(solution)/shard_map/ppermute | solution.py:321
  5.1 1.5 %collective-permute-start.4 = (bf16[176,256]{1,0:T(8,128)(2,1)S(1)}, bf16[176,256]{1,0:T(8,128)(2,1)S(1)}, u32[]{:S(2)}, u32[]{:S(2)}) collective-permute-start(bf16[176,256]{1,0:T(8,128)(2,1)S(1)} %get-tuple-element.48), channel_id=1, source_target_pairs={{0,16},{2,18},{16,0},{18,2},{1,17},{3,19},{17,1},{19,3},{4,20},{6,... | collective-permute-start | bytes 270344 | tf_op jit(solution)/shard_map/ppermute | solution.py:321
  6.6 2.0 %collective-permute-start = (bf16[176,256]{1,0:T(8,128)(2,1)S(1)}, bf16[176,256]{1,0:T(8,128)(2,1)S(1)}, u32[]{:S(2)}, u32[]{:S(2)}) collective-permute-start(bf16[176,256]{1,0:T(8,128)(2,1)S(1)} %get-tuple-element.44.refs_0_), channel_id=1, source_target_pairs={{0,4},{4,0},{8,12},{12,8},{1,5},{5,1},{9,13},{13,9},{2,6},{6,2},{1... | collective-permute-start | bytes 270344 | tf_op jit(solution)/shard_map/ppermute | solution.py:321
  8.6 2.6 %collective-permute-start.1 = (bf16[176,256]{1,0:T(8,128)(2,1)S(1)}, bf16[176,256]{1,0:T(8,128)(2,1)S(1)}, u32[]{:S(2)}, u32[]{:S(2)}) collective-permute-start(bf16[176,256]{1,0:T(8,128)(2,1)S(1)} %get-tuple-element.44.refs_0_), channel_id=1, source_target_pairs={{0,8},{4,12},{8,0},{12,4},{1,9},{5,13},{9,1},{13,5},{2,10},{6,14},... | collective-permute-start | bytes 270344 | tf_op jit(solution)/shard_map/ppermute | solution.py:321
  11.2 0.7 deal.1
  12.0 2.7 %collective-permute-start.10 = (bf16[2,160,384]{2,1,0:T(8,128)(2,1)S(1)}, bf16[2,160,384]{2,1,0:T(8,128)(2,1)S(1)}, u32[]{:S(2)}, u32[]{:S(2)}) collective-permute-start(bf16[2,160,384]{2,1,0:T(8,128)(2,1)S(1)} %get-tuple-element.57), channel_id=1, source_target_pairs={{0,18},{2,16},{16,2},{18,0},{1,19},{3,17},{17,3},{19,1},{4,22},{6,... | collective-permute-start | bytes 737288 | tf_op jit(solution)/shard_map/ppermute | solution.py:321
  14.7 0.5 collective-permute-start.11
  15.2 0.5 collective-permute-start.12
  15.7 1.1 %collective-permute-done.1.refs_2_ = bf16[176,256]{1,0:T(8,128)(2,1)S(1)} collective-permute-done((bf16[176,256]{1,0:T(8,128)(2,1)S(1)}, bf16[176,256]{1,0:T(8,128)(2,1)S(1)}, u32[]{:S(2)}, u32[]{:S(2)}) %collective-permute-start.1) | collective-permute-done | bytes 90144 | tf_op jit(solution)/shard_map/ppermute | solution.py:321
  16.7 1.7 %collective-permute-done.2.refs_3_ = bf16[176,256]{1,0:T(8,128)(2,1)S(1)} collective-permute-done((bf16[176,256]{1,0:T(8,128)(2,1)S(1)}, bf16[176,256]{1,0:T(8,128)(2,1)S(1)}, u32[]{:S(2)}, u32[]{:S(2)}) %collective-permute-start.2) | collective-permute-done | bytes 90144 | tf_op jit(solution)/shard_map/ppermute | solution.py:321
  18.4 0.1 lines.1
  18.5 2.6 %forward.1 = (bf16[8,160,640]{2,1,0:T(8,128)(2,1)S(1)}, bf16[8,160,640]{2,1,0:T(8,128)(2,1)S(1)}, f32[8,640]{1,0:T(8,128)S(1)}, f32[160,128]{1,0:T(8,128)S(1)}, ...) custom-call(bf16[640,128]{1,0:T(8,128)(2,1)S(1)} %get-tuple-element.45.refs_0_.refs_4_, ...), custom_call_target="tpu_custom_call" | custom-call | flops 30000001024 | tf_op jit(solution)/shard_map/forward/pallas_call | solution.py:406
  21.1 0.9 %collective-permute-start.7 = (bf16[192,128]{1,0:T(8,128)(2,1)S(1)}, bf16[192,128]{1,0:T(8,128)(2,1)S(1)}, u32[]{:S(2)}, u32[]{:S(2)}) collective-permute-start(bf16[192,128]{1,0:T(8,128)(2,1)S(1)} %get-tuple-element.53), channel_id=1, source_target_pairs={{0,4},{4,0},{8,12},{12,8},{1,5},{5,1},{9,13},{13,9},{2,6},{6,2},{1... | collective-permute-start | bytes 147464 | tf_op jit(solution)/shard_map/ppermute | solution.py:321
  22.0 3.0 %collective-permute-start.8 = (bf16[192,128]{1,0:T(8,128)(2,1)S(1)}, bf16[192,128]{1,0:T(8,128)(2,1)S(1)}, u32[]{:S(2)}, u32[]{:S(2)}) collective-permute-start(bf16[192,128]{1,0:T(8,128)(2,1)S(1)} %get-tuple-element.54), channel_id=1, source_target_pairs={{0,8},{4,12},{8,0},{12,4},{1,9},{5,13},{9,1},{13,5},{2,10},{6,14},... | collective-permute-start | bytes 147464 | tf_op jit(solution)/shard_map/ppermute | solution.py:321
  25.0 0.6 collective-permute-start.9
  25.6 2.5 %collective-permute-done.8.refs_7_ = bf16[192,128]{1,0:T(8,128)(2,1)S(1)} collective-permute-done((bf16[192,128]{1,0:T(8,128)(2,1)S(1)}, bf16[192,128]{1,0:T(8,128)(2,1)S(1)}, u32[]{:S(2)}, u32[]{:S(2)}) %collective-permute-start.8) | collective-permute-done | bytes 49184 | tf_op jit(solution)/shard_map/ppermute | solution.py:321
  28.2 2.7 %collective-permute-done.9.refs_8_ = bf16[192,128]{1,0:T(8,128)(2,1)S(1)} collective-permute-done((bf16[192,128]{1,0:T(8,128)(2,1)S(1)}, bf16[192,128]{1,0:T(8,128)(2,1)S(1)}, u32[]{:S(2)}, u32[]{:S(2)}) %collective-permute-start.9) | collective-permute-done | bytes 49184 | tf_op jit(solution)/shard_map/ppermute | solution.py:321
  30.9 2.3 %backward.1 = (f32[4,160,128]{2,1,0:T(8,128)S(1)}, f32[4,160,128]{2,1,0:T(8,128)S(1)}, bf16[4,160,128]{2,1,0:T(8,128)(2,1)S(1)}, bf16[4,160,128]{2,1,0:T(8,128)(2,1)S(1)}, f32[160,128]{1,0:T(8,128)S(1)}) custom-call(bf16[8,160,640]{2,1,0:T(8,128)(2,1)S(1)} %get-tuple-element.49.refs_0_, bf16[8,160,640]{2,1,0:T(8,128)(2,1)S(1)} %get-tuple-element.50.refs_1_, ...), custom_call_target="tpu_custom_call" | custom-call | flops 30000001024 | tf_op jit(solution)/shard_map/backward/pallas_call | solution.py:436
  33.2 0.5 collective-permute-start.14
  33.8 0.9 %collective-permute-done.13 = bf16[4,160,128]{2,1,0:T(8,128)(2,1)S(1)} collective-permute-done((bf16[4,160,128]{2,1,0:T(8,128)(2,1)S(1)}, bf16[4,160,128]{2,1,0:T(8,128)(2,1)S(1)}, u32[]{:S(2)}, u32[]{:S(2)}) %collective-permute-start.13) | collective-permute-done | bytes 163872 | tf_op jit(solution)/shard_map/ppermute | solution.py:321
  34.7 0.2 collective-permute-done.14
  34.9 1.6 %collective-permute-start.15 = (bf16[800,128]{1,0:T(8,128)(2,1)S(1)}, bf16[800,128]{1,0:T(8,128)(2,1)S(1)}, u32[]{:S(2)}, u32[]{:S(2)}) collective-permute-start(bf16[800,128]{1,0:T(8,128)(2,1)S(1)} %pad_maximum_fusion.2), channel_id=1, source_target_pairs={{0,16},{2,18},{16,0},{18,2},{1,17},{3,19},{17,1},{19,3},{4,20},{6,... | collective-permute-start | bytes 614408 | tf_op jit(solution)/shard_map/ppermute | solution.py:321
  36.5 1.5 %collective-permute-start.16 = (bf16[4,160,128]{2,1,0:T(8,128)(2,1)S(1)}, bf16[4,160,128]{2,1,0:T(8,128)(2,1)S(1)}, u32[]{:S(2)}, u32[]{:S(2)}) collective-permute-start(bf16[4,160,128]{2,1,0:T(8,128)(2,1)S(1)} %fusion.2), channel_id=1, source_target_pairs={{0,2},{2,0},{16,18},{18,16},{1,3},{3,1},{17,19},{19,17},{4,6},{6,4... | collective-permute-start | bytes 491528 | tf_op jit(solution)/shard_map/ppermute | solution.py:321
  38.0 4.6 %collective-permute-done.16 = bf16[4,160,128]{2,1,0:T(8,128)(2,1)S(1)} collective-permute-done((bf16[4,160,128]{2,1,0:T(8,128)(2,1)S(1)}, bf16[4,160,128]{2,1,0:T(8,128)(2,1)S(1)}, u32[]{:S(2)}, u32[]{:S(2)}) %collective-permute-start.16) | collective-permute-done | bytes 163872 | tf_op jit(solution)/shard_map/ppermute | solution.py:321
  42.6 0.1 fusion.3
  42.8 1.6 %collective-permute-start.17 = (bf16[960,128]{1,0:T(8,128)(2,1)S(1)}, bf16[960,128]{1,0:T(8,128)(2,1)S(1)}, u32[]{:S(2)}, u32[]{:S(2)}) collective-permute-start(bf16[960,128]{1,0:T(8,128)(2,1)S(1)} %pad_maximum_fusion.1), channel_id=1, source_target_pairs={{0,2},{2,0},{16,18},{18,16},{1,3},{3,1},{17,19},{19,17},{4,6},{6,4... | collective-permute-start | bytes 737288 | tf_op jit(solution)/shard_map/ppermute | solution.py:321
  44.3 1.2 %collective-permute-start.18 = (bf16[4,160,128]{2,1,0:T(8,128)(2,1)S(1)}, bf16[4,160,128]{2,1,0:T(8,128)(2,1)S(1)}, u32[]{:S(2)}, u32[]{:S(2)}) collective-permute-start(bf16[4,160,128]{2,1,0:T(8,128)(2,1)S(1)} %get-tuple-element.73), channel_id=1, source_target_pairs={{0,16},{2,18},{16,0},{18,2},{1,17},{3,19},{17,1},{19,3},{4,20},{6,... | collective-permute-start | bytes 491528 | tf_op jit(solution)/shard_map/ppermute | solution.py:321
  45.5 0.5 collective-permute-start.20
  46.0 3.7 %collective-permute-done.18 = bf16[4,160,128]{2,1,0:T(8,128)(2,1)S(1)} collective-permute-done((bf16[4,160,128]{2,1,0:T(8,128)(2,1)S(1)}, bf16[4,160,128]{2,1,0:T(8,128)(2,1)S(1)}, u32[]{:S(2)}, u32[]{:S(2)}) %collective-permute-start.18) | collective-permute-done | bytes 163872 | tf_op jit(solution)/shard_map/ppermute | solution.py:321
  49.7 0.2 collective-permute-done.17
  49.9 0.4 collective-permute-start.23
  50.5 0.2 collective-permute-start.25
  50.7 0.4 collective-permute-start.24
  51.1 0.1 collective-permute-done.22.refs_7_
  51.2 0.2 collective-permute-done.23.refs_11_
  51.4 0.5 collective-permute-done.25.refs_13_
  52.0 0.2 collective-permute-done.24.refs_12_
  52.2 0.8 %weights.1 = (f32[96,384]{1,0:T(8,128)S(1)}, bf16[96,384]{1,0:T(8,128)(2,1)S(1)}, bf16[96,384]{1,0:T(8,128)(2,1)S(1)}, bf16[96,384]{1,0:T(8,128)(2,1)S(1)}) custom-call(bf16[2,160,384]{2,1,0:T(8,128)(2,1)S(1)} %get-tuple-element.76.refs_0_, bf16[2,160,384]{2,1,0:T(8,128)(2,1)S(1)} %collective-permute-done.11.refs_1_, ...), custom_call_target="tpu_custom_call" | custom-call | tf_op jit(solution)/shard_map/weights/pallas_call | solution.py:478
  53.1 1.5 %collective-permute-start.27 = (bf16[96,384]{1,0:T(8,128)(2,1)S(1)}, bf16[96,384]{1,0:T(8,128)(2,1)S(1)}, u32[]{:S(2)}, u32[]{:S(2)}) collective-permute-start(bf16[96,384]{1,0:T(8,128)(2,1)S(1)} %get-tuple-element.82), channel_id=1, source_target_pairs={{0,8},{4,12},{8,0},{12,4},{1,9},{5,13},{9,1},{13,5},{2,10},{6,14},... | collective-permute-start | bytes 221192 | tf_op jit(solution)/shard_map/ppermute | solution.py:321
  54.6 2.9 %collective-permute-start.28 = (bf16[96,384]{1,0:T(8,128)(2,1)S(1)}, bf16[96,384]{1,0:T(8,128)(2,1)S(1)}, u32[]{:S(2)}, u32[]{:S(2)}) collective-permute-start(bf16[96,384]{1,0:T(8,128)(2,1)S(1)} %get-tuple-element.83), channel_id=1, source_target_pairs={{0,12},{4,8},{8,4},{12,0},{1,13},{5,9},{9,5},{13,1},{2,14},{6,10},... | collective-permute-start | bytes 221192 | tf_op jit(solution)/shard_map/ppermute | solution.py:321
  57.5 0.6 dynamic-slice_bitcast_fusion
  58.1 0.5 collective-permute-done.26
  58.6 3.7 %collective-permute-done.27 = bf16[96,384]{1,0:T(8,128)(2,1)S(1)} collective-permute-done((bf16[96,384]{1,0:T(8,128)(2,1)S(1)}, bf16[96,384]{1,0:T(8,128)(2,1)S(1)}, u32[]{:S(2)}, u32[]{:S(2)}) %collective-permute-start.27) | collective-permute-done | bytes 73760 | tf_op jit(solution)/shard_map/ppermute | solution.py:321
  62.4 1.4 %collective-permute-start.29 = (bf16[96,384]{1,0:T(8,128)(2,1)S(1)}, bf16[96,384]{1,0:T(8,128)(2,1)S(1)}, u32[]{:S(2)}, u32[]{:S(2)}) collective-permute-start(bf16[96,384]{1,0:T(8,128)(2,1)S(1)} %get-tuple-element.84), channel_id=1, source_target_pairs={{0,16},{16,0},{1,17},{17,1},{2,18},{18,2},{3,19},{19,3},{4,20},{20... | collective-permute-start | bytes 221192 | tf_op jit(solution)/shard_map/ppermute | solution.py:321
  63.9 0.6 dynamic-slice_bitcast_fusion.1
  64.5 2.4 %collective-permute-done.29.refs_0_ = bf16[96,384]{1,0:T(8,128)(2,1)S(1)} collective-permute-done((bf16[96,384]{1,0:T(8,128)(2,1)S(1)}, bf16[96,384]{1,0:T(8,128)(2,1)S(1)}, u32[]{:S(2)}, u32[]{:S(2)}) %collective-permute-start.29) | collective-permute-done | bytes 73760 | tf_op jit(solution)/shard_map/ppermute | solution.py:321
  66.8 0.7 %assemble.1 = f32[2,96,384]{2,1,0:T(8,128)} custom-call(f32[96,384]{1,0:T(8,128)S(1)} %get-tuple-element.85.own_ref, bf16[96,384]{1,0:T(8,128)(2,1)S(1)} %collective-permute-done.29.refs_0_), custom_call_target="tpu_custom_call" | custom-call | tf_op jit(solution)/shard_map/assemble/pallas_call | solution.py:498
  (38 shorter events, 0.8 us)
Async XLA Ops:
  2.1 9.8 %collective-permute-start.3 = (bf16[176,256]{1,0:T(8,128)(2,1)S(1)}, bf16[176,256]{1,0:T(8,128)(2,1)S(1)}, u32[]{:S(2)}, u32[]{:S(2)}) collective-permute-start(bf16[176,256]{1,0:T(8,128)(2,1)S(1)} %get-tuple-element.48), channel_id=1, source_target_pairs={{0,2},{2,0},{16,18},{18,16},{1,3},{3,1},{17,19},{19,17},{4,6},{6,4... | collective-permute-start | bytes 270344 | tf_op jit(solution)/shard_map/ppermute | solution.py:321
  5.1 6.9 %collective-permute-start.4 = (bf16[176,256]{1,0:T(8,128)(2,1)S(1)}, bf16[176,256]{1,0:T(8,128)(2,1)S(1)}, u32[]{:S(2)}, u32[]{:S(2)}) collective-permute-start(bf16[176,256]{1,0:T(8,128)(2,1)S(1)} %get-tuple-element.48), channel_id=1, source_target_pairs={{0,16},{2,18},{16,0},{18,2},{1,17},{3,19},{17,1},{19,3},{4,20},{6,... | collective-permute-start | bytes 270344 | tf_op jit(solution)/shard_map/ppermute | solution.py:321
  6.6 8.1 %collective-permute-start.5 = (bf16[176,256]{1,0:T(8,128)(2,1)S(1)}, bf16[176,256]{1,0:T(8,128)(2,1)S(1)}, u32[]{:S(2)}, u32[]{:S(2)}) collective-permute-start(bf16[176,256]{1,0:T(8,128)(2,1)S(1)} %get-tuple-element.48), channel_id=1, source_target_pairs={{0,18},{2,16},{16,2},{18,0},{1,19},{3,17},{17,3},{19,1},{4,22},{6,... | collective-permute-start | bytes 270344 | tf_op jit(solution)/shard_map/ppermute | solution.py:321
  6.6 8.6 %collective-permute-start = (bf16[176,256]{1,0:T(8,128)(2,1)S(1)}, bf16[176,256]{1,0:T(8,128)(2,1)S(1)}, u32[]{:S(2)}, u32[]{:S(2)}) collective-permute-start(bf16[176,256]{1,0:T(8,128)(2,1)S(1)} %get-tuple-element.44.refs_0_), channel_id=1, source_target_pairs={{0,4},{4,0},{8,12},{12,8},{1,5},{5,1},{9,13},{13,9},{2,6},{6,2},{1... | collective-permute-start | bytes 270344 | tf_op jit(solution)/shard_map/ppermute | solution.py:321
  8.6 8.1 %collective-permute-start.1 = (bf16[176,256]{1,0:T(8,128)(2,1)S(1)}, bf16[176,256]{1,0:T(8,128)(2,1)S(1)}, u32[]{:S(2)}, u32[]{:S(2)}) collective-permute-start(bf16[176,256]{1,0:T(8,128)(2,1)S(1)} %get-tuple-element.44.refs_0_), channel_id=1, source_target_pairs={{0,8},{4,12},{8,0},{12,4},{1,9},{5,13},{9,1},{13,5},{2,10},{6,14},... | collective-permute-start | bytes 270344 | tf_op jit(solution)/shard_map/ppermute | solution.py:321
  11.9 6.5 %collective-permute-start.2 = (bf16[176,256]{1,0:T(8,128)(2,1)S(1)}, bf16[176,256]{1,0:T(8,128)(2,1)S(1)}, u32[]{:S(2)}, u32[]{:S(2)}) collective-permute-start(bf16[176,256]{1,0:T(8,128)(2,1)S(1)} %get-tuple-element.44.refs_0_), channel_id=1, source_target_pairs={{0,12},{4,8},{8,4},{12,0},{1,13},{5,9},{9,5},{13,1},{2,14},{6,10},... | collective-permute-start | bytes 270344 | tf_op jit(solution)/shard_map/ppermute | solution.py:321
  12.0 13.0 %collective-permute-start.10 = (bf16[2,160,384]{2,1,0:T(8,128)(2,1)S(1)}, bf16[2,160,384]{2,1,0:T(8,128)(2,1)S(1)}, u32[]{:S(2)}, u32[]{:S(2)}) collective-permute-start(bf16[2,160,384]{2,1,0:T(8,128)(2,1)S(1)} %get-tuple-element.57), channel_id=1, source_target_pairs={{0,18},{2,16},{16,2},{18,0},{1,19},{3,17},{17,3},{19,1},{4,22},{6,... | collective-permute-start | bytes 737288 | tf_op jit(solution)/shard_map/ppermute | solution.py:321
  14.7 11.0 %collective-permute-start.11 = (bf16[2,160,384]{2,1,0:T(8,128)(2,1)S(1)}, bf16[2,160,384]{2,1,0:T(8,128)(2,1)S(1)}, u32[]{:S(2)}, u32[]{:S(2)}) collective-permute-start(bf16[2,160,384]{2,1,0:T(8,128)(2,1)S(1)} %get-tuple-element.58), channel_id=1, source_target_pairs={{0,2},{2,0},{16,18},{18,16},{1,3},{3,1},{17,19},{19,17},{4,6},{6,4... | collective-permute-start | bytes 737288 | tf_op jit(solution)/shard_map/ppermute | solution.py:321
  15.2 10.4 %collective-permute-start.12 = (bf16[2,160,384]{2,1,0:T(8,128)(2,1)S(1)}, bf16[2,160,384]{2,1,0:T(8,128)(2,1)S(1)}, u32[]{:S(2)}, u32[]{:S(2)}) collective-permute-start(bf16[2,160,384]{2,1,0:T(8,128)(2,1)S(1)} %get-tuple-element.59), channel_id=1, source_target_pairs={{0,16},{2,18},{16,0},{18,2},{1,17},{3,19},{17,1},{19,3},{4,20},{6,... | collective-permute-start | bytes 737288 | tf_op jit(solution)/shard_map/ppermute | solution.py:321
  16.7 1.8 %collective-permute-start.6 = (bf16[4,176,256]{2,1,0:T(8,128)(2,1)S(1)}, bf16[4,176,256]{2,1,0:T(8,128)(2,1)S(1)}, u32[]{:S(2)}, u32[]{:S(2)}) collective-permute-start(bf16[4,176,256]{2,1,0:T(8,128)(2,1)S(1)} %pad_maximum_fusion), channel_id=1, source_target_pairs={{0,1},{1,0},{2,3},{3,2},{4,5},{5,4},{6,7},{7,6},{8,9},{9,8},{10,11... | collective-permute-start | bytes 1081352 | tf_op jit(solution)/shard_map/ppermute | solution.py:321
  21.1 4.5 %collective-permute-start.7 = (bf16[192,128]{1,0:T(8,128)(2,1)S(1)}, bf16[192,128]{1,0:T(8,128)(2,1)S(1)}, u32[]{:S(2)}, u32[]{:S(2)}) collective-permute-start(bf16[192,128]{1,0:T(8,128)(2,1)S(1)} %get-tuple-element.53), channel_id=1, source_target_pairs={{0,4},{4,0},{8,12},{12,8},{1,5},{5,1},{9,13},{13,9},{2,6},{6,2},{1... | collective-permute-start | bytes 147464 | tf_op jit(solution)/shard_map/ppermute | solution.py:321
  22.0 6.1 %collective-permute-start.8 = (bf16[192,128]{1,0:T(8,128)(2,1)S(1)}, bf16[192,128]{1,0:T(8,128)(2,1)S(1)}, u32[]{:S(2)}, u32[]{:S(2)}) collective-permute-start(bf16[192,128]{1,0:T(8,128)(2,1)S(1)} %get-tuple-element.54), channel_id=1, source_target_pairs={{0,8},{4,12},{8,0},{12,4},{1,9},{5,13},{9,1},{13,5},{2,10},{6,14},... | collective-permute-start | bytes 147464 | tf_op jit(solution)/shard_map/ppermute | solution.py:321
  25.0 5.9 %collective-permute-start.9 = (bf16[192,128]{1,0:T(8,128)(2,1)S(1)}, bf16[192,128]{1,0:T(8,128)(2,1)S(1)}, u32[]{:S(2)}, u32[]{:S(2)}) collective-permute-start(bf16[192,128]{1,0:T(8,128)(2,1)S(1)} %get-tuple-element.55), channel_id=1, source_target_pairs={{0,12},{4,8},{8,4},{12,0},{1,13},{5,9},{9,5},{13,1},{2,14},{6,10},... | collective-permute-start | bytes 147464 | tf_op jit(solution)/shard_map/ppermute | solution.py:321
  33.2 1.5 %collective-permute-start.13 = (bf16[4,160,128]{2,1,0:T(8,128)(2,1)S(1)}, bf16[4,160,128]{2,1,0:T(8,128)(2,1)S(1)}, u32[]{:S(2)}, u32[]{:S(2)}) collective-permute-start(bf16[4,160,128]{2,1,0:T(8,128)(2,1)S(1)} %get-tuple-element.65), channel_id=1, source_target_pairs={{0,1},{1,0},{2,3},{3,2},{4,5},{5,4},{6,7},{7,6},{8,9},{9,8},{10,11... | collective-permute-start | bytes 491528 | tf_op jit(solution)/shard_map/ppermute | solution.py:321
  33.2 1.6 %collective-permute-start.14 = (bf16[4,160,128]{2,1,0:T(8,128)(2,1)S(1)}, bf16[4,160,128]{2,1,0:T(8,128)(2,1)S(1)}, u32[]{:S(2)}, u32[]{:S(2)}) collective-permute-start(bf16[4,160,128]{2,1,0:T(8,128)(2,1)S(1)} %get-tuple-element.67), channel_id=1, source_target_pairs={{0,1},{1,0},{2,3},{3,2},{4,5},{5,4},{6,7},{7,6},{8,9},{9,8},{10,11... | collective-permute-start | bytes 491528 | tf_op jit(solution)/shard_map/ppermute | solution.py:321
  33.8 16.1 %copy-start = (bf16[160,128]{1,0:T(8,128)(2,1)}, bf16[160,128]{1,0:T(8,128)(2,1)S(1)}, u32[]{:S(2)}) copy-start(bf16[160,128]{1,0:T(8,128)(2,1)S(1)} %convert_element_type.57) | copy-start | bytes 122884
  34.9 7.7 %collective-permute-start.15 = (bf16[800,128]{1,0:T(8,128)(2,1)S(1)}, bf16[800,128]{1,0:T(8,128)(2,1)S(1)}, u32[]{:S(2)}, u32[]{:S(2)}) collective-permute-start(bf16[800,128]{1,0:T(8,128)(2,1)S(1)} %pad_maximum_fusion.2), channel_id=1, source_target_pairs={{0,16},{2,18},{16,0},{18,2},{1,17},{3,19},{17,1},{19,3},{4,20},{6,... | collective-permute-start | bytes 614408 | tf_op jit(solution)/shard_map/ppermute | solution.py:321
  36.5 6.1 %collective-permute-start.16 = (bf16[4,160,128]{2,1,0:T(8,128)(2,1)S(1)}, bf16[4,160,128]{2,1,0:T(8,128)(2,1)S(1)}, u32[]{:S(2)}, u32[]{:S(2)}) collective-permute-start(bf16[4,160,128]{2,1,0:T(8,128)(2,1)S(1)} %fusion.2), channel_id=1, source_target_pairs={{0,2},{2,0},{16,18},{18,16},{1,3},{3,1},{17,19},{19,17},{4,6},{6,4... | collective-permute-start | bytes 491528 | tf_op jit(solution)/shard_map/ppermute | solution.py:321
  42.8 7.1 %collective-permute-start.17 = (bf16[960,128]{1,0:T(8,128)(2,1)S(1)}, bf16[960,128]{1,0:T(8,128)(2,1)S(1)}, u32[]{:S(2)}, u32[]{:S(2)}) collective-permute-start(bf16[960,128]{1,0:T(8,128)(2,1)S(1)} %pad_maximum_fusion.1), channel_id=1, source_target_pairs={{0,2},{2,0},{16,18},{18,16},{1,3},{3,1},{17,19},{19,17},{4,6},{6,4... | collective-permute-start | bytes 737288 | tf_op jit(solution)/shard_map/ppermute | solution.py:321
  44.3 5.3 %collective-permute-start.18 = (bf16[4,160,128]{2,1,0:T(8,128)(2,1)S(1)}, bf16[4,160,128]{2,1,0:T(8,128)(2,1)S(1)}, u32[]{:S(2)}, u32[]{:S(2)}) collective-permute-start(bf16[4,160,128]{2,1,0:T(8,128)(2,1)S(1)} %get-tuple-element.73), channel_id=1, source_target_pairs={{0,16},{2,18},{16,0},{18,2},{1,17},{3,19},{17,1},{19,3},{4,20},{6,... | collective-permute-start | bytes 491528 | tf_op jit(solution)/shard_map/ppermute | solution.py:321
  45.5 5.0 %collective-permute-start.19 = (bf16[2,160,384]{2,1,0:T(8,128)(2,1)S(1)}, bf16[2,160,384]{2,1,0:T(8,128)(2,1)S(1)}, u32[]{:S(2)}, u32[]{:S(2)}) collective-permute-start(bf16[2,160,384]{2,1,0:T(8,128)(2,1)S(1)} %get-tuple-element.76.refs_0_), channel_id=1, source_target_pairs={{0,1},{1,0},{2,3},{3,2},{4,5},{5,4},{6,7},{7,6},{8,9},{9,8},{10,11... | collective-permute-start | bytes 737288 | tf_op jit(solution)/shard_map/ppermute | solution.py:321
  45.5 5.2 %collective-permute-start.20 = (bf16[2,160,384]{2,1,0:T(8,128)(2,1)S(1)}, bf16[2,160,384]{2,1,0:T(8,128)(2,1)S(1)}, u32[]{:S(2)}, u32[]{:S(2)}) collective-permute-start(bf16[2,160,384]{2,1,0:T(8,128)(2,1)S(1)} %collective-permute-done.11.refs_1_), channel_id=1, source_target_pairs={{0,1},{1,0},{2,3},{3,2},{4,5},{5,4},{6,7},{7,6},{8,9},{9,8},{10,11... | collective-permute-start | bytes 737288 | tf_op jit(solution)/shard_map/ppermute | solution.py:321
  46.0 5.1 %collective-permute-start.21 = (bf16[2,160,384]{2,1,0:T(8,128)(2,1)S(1)}, bf16[2,160,384]{2,1,0:T(8,128)(2,1)S(1)}, u32[]{:S(2)}, u32[]{:S(2)}) collective-permute-start(bf16[2,160,384]{2,1,0:T(8,128)(2,1)S(1)} %collective-permute-done.12.refs_2_), channel_id=1, source_target_pairs={{0,1},{1,0},{2,3},{3,2},{4,5},{5,4},{6,7},{7,6},{8,9},{9,8},{10,11... | collective-permute-start | bytes 737288 | tf_op jit(solution)/shard_map/ppermute | solution.py:321
  49.7 1.5 %collective-permute-start.22 = (bf16[2,160,384]{2,1,0:T(8,128)(2,1)S(1)}, bf16[2,160,384]{2,1,0:T(8,128)(2,1)S(1)}, u32[]{:S(2)}, u32[]{:S(2)}) collective-permute-start(bf16[2,160,384]{2,1,0:T(8,128)(2,1)S(1)} %collective-permute-done.10.refs_3_), channel_id=1, source_target_pairs={{0,1},{1,0},{2,3},{3,2},{4,5},{5,4},{6,7},{7,6},{8,9},{9,8},{10,11... | collective-permute-start | bytes 737288 | tf_op jit(solution)/shard_map/ppermute | solution.py:321
  49.9 1.5 %collective-permute-start.23 = (bf16[640,128]{1,0:T(8,128)(2,1)S(1)}, bf16[640,128]{1,0:T(8,128)(2,1)S(1)}, u32[]{:S(2)}, u32[]{:S(2)}) collective-permute-start(bf16[640,128]{1,0:T(8,128)(2,1)S(1)} %pad_maximum_fusion.3.refs_8_), channel_id=1, source_target_pairs={{0,1},{1,0},{2,3},{3,2},{4,5},{5,4},{6,7},{7,6},{8,9},{9,8},{10,11... | collective-permute-start | bytes 491528 | tf_op jit(solution)/shard_map/ppermute | solution.py:321
  50.5 1.5 %collective-permute-start.25 = (bf16[4,160,128]{2,1,0:T(8,128)(2,1)S(1)}, bf16[4,160,128]{2,1,0:T(8,128)(2,1)S(1)}, u32[]{:S(2)}, u32[]{:S(2)}) collective-permute-start(bf16[4,160,128]{2,1,0:T(8,128)(2,1)S(1)} %add_convert_fusion.refs_10_), channel_id=1, source_target_pairs={{0,1},{1,0},{2,3},{3,2},{4,5},{5,4},{6,7},{7,6},{8,9},{9,8},{10,11... | collective-permute-start | bytes 491528 | tf_op jit(solution)/shard_map/ppermute | solution.py:321
  50.7 1.5 %collective-permute-start.24 = (bf16[4,160,128]{2,1,0:T(8,128)(2,1)S(1)}, bf16[4,160,128]{2,1,0:T(8,128)(2,1)S(1)}, u32[]{:S(2)}, u32[]{:S(2)}) collective-permute-start(bf16[4,160,128]{2,1,0:T(8,128)(2,1)S(1)} %fusion.refs_9_), channel_id=1, source_target_pairs={{0,1},{1,0},{2,3},{3,2},{4,5},{5,4},{6,7},{7,6},{8,9},{9,8},{10,11... | collective-permute-start | bytes 491528 | tf_op jit(solution)/shard_map/ppermute | solution.py:321
  53.0 5.6 %collective-permute-start.26 = (bf16[96,384]{1,0:T(8,128)(2,1)S(1)}, bf16[96,384]{1,0:T(8,128)(2,1)S(1)}, u32[]{:S(2)}, u32[]{:S(2)}) collective-permute-start(bf16[96,384]{1,0:T(8,128)(2,1)S(1)} %get-tuple-element.81), channel_id=1, source_target_pairs={{0,4},{4,0},{8,12},{12,8},{1,5},{5,1},{9,13},{13,9},{2,6},{6,2},{1... | collective-permute-start | bytes 221192 | tf_op jit(solution)/shard_map/ppermute | solution.py:321
  53.1 9.2 %collective-permute-start.27 = (bf16[96,384]{1,0:T(8,128)(2,1)S(1)}, bf16[96,384]{1,0:T(8,128)(2,1)S(1)}, u32[]{:S(2)}, u32[]{:S(2)}) collective-permute-start(bf16[96,384]{1,0:T(8,128)(2,1)S(1)} %get-tuple-element.82), channel_id=1, source_target_pairs={{0,8},{4,12},{8,0},{12,4},{1,9},{5,13},{9,1},{13,5},{2,10},{6,14},... | collective-permute-start | bytes 221192 | tf_op jit(solution)/shard_map/ppermute | solution.py:321
  54.6 7.7 %collective-permute-start.28 = (bf16[96,384]{1,0:T(8,128)(2,1)S(1)}, bf16[96,384]{1,0:T(8,128)(2,1)S(1)}, u32[]{:S(2)}, u32[]{:S(2)}) collective-permute-start(bf16[96,384]{1,0:T(8,128)(2,1)S(1)} %get-tuple-element.83), channel_id=1, source_target_pairs={{0,12},{4,8},{8,4},{12,0},{1,13},{5,9},{9,5},{13,1},{2,14},{6,10},... | collective-permute-start | bytes 221192 | tf_op jit(solution)/shard_map/ppermute | solution.py:321
  62.4 4.4 %collective-permute-start.29 = (bf16[96,384]{1,0:T(8,128)(2,1)S(1)}, bf16[96,384]{1,0:T(8,128)(2,1)S(1)}, u32[]{:S(2)}, u32[]{:S(2)}) collective-permute-start(bf16[96,384]{1,0:T(8,128)(2,1)S(1)} %get-tuple-element.84), channel_id=1, source_target_pairs={{0,16},{16,0},{1,17},{17,1},{2,18},{18,2},{3,19},{19,3},{4,20},{20... | collective-permute-start | bytes 221192 | tf_op jit(solution)/shard_map/ppermute | solution.py:321

commit v4 on v3

v4 whole, which is shorter than its diff:
```python
import functools
import math

import jax
import jax.numpy as jnp
from jax import lax
from jax.experimental import pallas as pl
from jax.experimental.pallas import tpu as pltpu
from jax.sharding import Mesh
from jax.sharding import PartitionSpec as P

BLK = 128
LANES = 128
PAD_ROWS = 16
NEG_FILL = -1e30
LOG2E = math.log2(math.e)
MIB = 1 << 20
F32 = jnp.float32
BF16 = jnp.bfloat16
VMEM = pl.BlockSpec(memory_space=pltpu.VMEM)
HBM = pl.BlockSpec(memory_space=pltpu.HBM)


def cut_rows(count):
    return count * 3 // (4 * PAD_ROWS) * PAD_ROWS


def plane_places(plane, n_y):
    row_id, y_id = lax.axis_index("row"), lax.axis_index("y")
    return [(row_id ^ a) * n_y + (y_id ^ b) for a, b in plane]


def dot_nt(left, right, precision=None):
    return lax.dot_general(
        left, right, (((1,), (1,)), ((), ())), preferred_element_type=F32, precision=precision
    )


def dot_tn(left, right):
    return lax.dot_general(left, right, (((0,), (0,)), ((), ())), preferred_element_type=F32)


def params(nbytes):
    return pltpu.CompilerParams(vmem_limit_bytes=nbytes)


def split_three(values):
    high = values.astype(BF16).astype(F32)
    rest = values - high
    middle = rest.astype(BF16).astype(F32)
    return high, middle, rest - middle


def pack_kernel(
    axes, q_hbm, k_hbm, v_hbm, o_hbm, g_hbm, x_hbm, pos_hbm, ids_hbm, qg_ref, kv_ref, x_ref, *scratch
):
    outs, prod, extra, pos, ids, sems = scratch
    count, width = outs.shape
    copies = [
        pltpu.make_async_copy(source, target, sems.at[place])
        for place, (source, target) in enumerate(
            (
                (pos_hbm, pos),
                (ids_hbm, ids),
                (g_hbm, qg_ref.at[:count, width:]),
                (o_hbm, outs),
                (q_hbm, qg_ref.at[:count, :width]),
                (k_hbm, kv_ref.at[:count, :width]),
                (v_hbm, kv_ref.at[:count, width:]),
                (x_hbm, x_ref),
            )
        )
    ]
    for copy in copies:
        copy.start()
    me = jnp.int32(0)
    for name, size in axes:
        me = me * size + lax.axis_index(name)
    prod[...] = jnp.zeros_like(prod)
    copies[0].wait()
    copies[1].wait()
    lines = min(pos.shape[0], (count + LANES - 2) // LANES + 1)
    first = jnp.minimum(me * count // LANES, pos.shape[0] - lines)
    shift = me * count - first * LANES
    block = jnp.concatenate([pos[pl.ds(first + i, 1), :] for i in range(lines)], axis=1) // BLK

    def add_id(index, found):
        return jnp.where(block == index, ids[index], found)

    found = lax.fori_loop(0, ids.shape[0], add_id, jnp.zeros_like(block), unroll=8)
    found = jnp.broadcast_to(found.astype(F32), (8, lines * LANES))
    found = pltpu.roll(found, lines * LANES - shift, 1)
    copies[2].wait()
    copies[3].wait()
    prod[:count, :] = qg_ref[:count, width:].astype(F32) * outs[...].astype(F32)
    delta = dot_nt(
        jnp.ones((PAD_ROWS, width), F32), prod[...], precision=lax.Precision.HIGHEST
    )
    high, middle, low = split_three(delta)
    row = lax.broadcasted_iota(jnp.int32, delta.shape, 0)
    extra[...] = jnp.where(row == 0, high, jnp.where(row == 1, middle, jnp.where(row == 2, low, 0.0)))
    extra[3:4, :count] = found[0:1, :count]
    tail = extra[...].astype(BF16)
    qg_ref[count:, :] = tail
    kv_ref[count:, :] = tail
    for copy in copies[4:]:
        copy.wait()


def deal_kernel(sizes, x_ref, *refs):
    *out_refs, dealt = refs
    n_row, n_z, n_y, n_core = sizes
    blk = x_ref.shape[1] // (n_row * n_z * n_y * n_core)
    for a in range(n_row):
        for b in range(n_y):
            for core in range(n_core):
                for z in range(n_z):
                    first = (((z * n_y + b) * n_core + core) * n_row + a) * blk
                    dealt[a * n_y + b, core, :, z * blk : (z + 1) * blk] = x_ref[:, first : first + blk]
    me_row, me_y = lax.axis_index("row"), lax.axis_index("y")
    for a in range(n_row):
        for b in range(n_y):
            out_refs[a * n_y + b][...] = dealt[(me_row ^ a) * n_y + (me_y ^ b)]


def assemble_kernel(own_ref, *refs):
    *got_refs, out_ref = refs
    me_row = lax.axis_index("row")
    out_ref[me_row] = own_ref[...]
    for offset, ref in enumerate(got_refs, 1):
        out_ref[me_row ^ offset] = ref[...].astype(F32)


def line_rows(slot, count):
    place = lax.axis_index("z") ^ slot
    return pl.ds(pl.multiple_of(place * count, PAD_ROWS), count)


def lines_kernel(count, width, n_q, *refs):
    qg_refs, (queries, grads, rows) = refs[:n_q][::-1], refs[n_q:]
    z_id = lax.axis_index("z")
    for slot, ref in enumerate(qg_refs):
        queries[line_rows(slot, count), :] = ref[:count, :width]
        grads[line_rows(slot, count), :] = ref[:count, width:]
    tails = [ref[count:, :].astype(F32) for ref in qg_refs]
    deltas = [(tail[0:1] + tail[1:2] + tail[2:3])[:, :count] for tail in tails]
    samples = [tail[3:4, :count] for tail in tails]
    for place in range(n_q):
        where = slice(place * count, (place + 1) * count)
        delta, sample = deltas[0], samples[0]
        for slot in range(1, n_q):
            here = (z_id ^ slot) == place
            delta = jnp.where(here, deltas[slot], delta)
            sample = jnp.where(here, samples[slot], sample)
        rows[0:1, where] = delta
        rows[1:2, where] = sample


def forward_kernel(count, width, n_q, n_kv, *refs):
    queries, grads, lines, refs = *refs[:3], refs[3:]
    kv_refs, refs = refs[:n_kv], refs[n_kv:]
    w_ref, u_ref, stat_ref, own_ref, refs = *refs[:4], refs[4:]
    send_refs, (keys, values, samples, scores, slopes, parts) = refs[: n_q - 1], refs[n_q - 1 :]
    total = n_q * count
    factor = LOG2E / math.sqrt(width)
    delta, query_samples = lines[0:1, :], lines[1:2, :]
    n_pieces = w_ref.shape[0]
    block = scores.shape[0]
    n_blocks = n_pieces // block

    def load(ref, index):
        keys[index] = ref[:count, :width]
        values[index] = ref[:count, width:]
        samples[index] = jnp.transpose(ref[count:, :].astype(F32))[:count, :8]

    base = 0
    for ref in kv_refs:
        depth = ref.shape[0]
        if depth <= 4:
            for i in range(depth):
                load(ref.at[i], base + i)
        else:

            @pl.loop(0, depth)
            def _(i, ref=ref, base=base):
                load(ref.at[i], base + i)

        base += depth

    def over_blocks(body, state):
        if n_blocks == 1:
            return body(0, state)
        return lax.fori_loop(0, n_blocks, lambda i, s: body(i * block, s), state)

    def fold(part, combine):
        out = part[0:8]
        for start in range(8, count, 8):
            out = combine(out, part[start : start + 8])
        return out

    def product(left, right, first):
        left = left[pl.ds(first, block)].reshape(block * count, width)
        return dot_nt(left, right[...]).reshape(block, count, total)

    def peak_step(first, peak):
        scores[...] = product(keys, queries, first)
        if n_blocks == 1:
            slopes[...] = product(values, grads, first)
        for piece in range(block):
            live = samples[first + piece][:, 3:4] == query_samples
            masked = jnp.where(live, scores[piece], NEG_FILL)
            scores[piece] = masked
            peak = jnp.maximum(peak, fold(masked, jnp.maximum))
        return peak

    turned = jnp.transpose(keys[:block].reshape(block * count, width))

    peak8 = over_blocks(peak_step, jnp.full((8, total), NEG_FILL, F32))
    peak = jnp.max(peak8, axis=0, keepdims=True)

    def grad_step(first, mass):
        if n_blocks > 1:
            peak_step(first, peak8)
            slopes[...] = product(values, grads, first)
        for piece in range(block):
            weight = jnp.exp2((scores[piece] - peak) * factor)
            w_ref[first + piece] = weight.astype(BF16)
            u_ref[first + piece] = (weight * (slopes[piece] - delta)).astype(BF16)
            mass = mass + fold(weight, jnp.add)
            if n_blocks == 1 and (piece + 1) % 4 == 0:
                rows = 4 * count
                first_row = (piece + 1) * count - rows
                known = u_ref[piece + 1 - 4 : piece + 1].reshape(rows, total)
                left = turned[:, first_row : first_row + rows]
                joins.append(jnp.dot(left, known, preferred_element_type=F32))
        return mass

    joins = []
    mass8 = over_blocks(grad_step, jnp.zeros((8, total), F32))
    mass = jnp.sum(mass8, axis=0, keepdims=True)
    level = peak * factor + jnp.log2(mass)
    stat_ref[...] = jnp.zeros_like(stat_ref)
    stat_ref[0:1, :] = peak * factor
    stat_ref[1:2, :] = level

    def join_step(first, joined):
        rows = block * count
        return joined + dot_tn(
            keys[pl.ds(first, block)].reshape(rows, width),
            u_ref[pl.ds(first, block)].reshape(rows, total),
        )

    if n_blocks == 1:
        joined = functools.reduce(jnp.add, joins)
    else:
        joined = over_blocks(join_step, jnp.zeros((width, total), F32))
    parts[...] = jnp.transpose((joined * (1.0 / mass)).astype(BF16))
    own_ref[...] = parts[line_rows(0, count), :]
    tail_rows = send_refs[0].shape[0] - count
    step = tail_rows // 4
    row = lax.broadcasted_iota(jnp.int32, (tail_rows, LANES), 0)
    tail = jnp.zeros((tail_rows, LANES), F32)
    for index, part in enumerate(split_three(level)):
        for chunk in range(total // LANES):
            line = part[:, chunk * LANES : (chunk + 1) * LANES]
            tail = jnp.where(row == index * step + chunk, line, tail)
    for offset, ref in enumerate(send_refs, 1):
        ref[:count, :] = parts[line_rows(offset, count), :]
        ref[count:, :] = tail.astype(BF16)


def products(w_ref, u_ref, first, size, places, queries, grads, key_ref, value_ref, scale):
    _, count, total = w_ref.shape
    many, shape = (size * count, total), (size, count, key_ref.shape[2])
    value_part = jnp.dot(
        w_ref[pl.ds(first, size)].reshape(many), grads[...], preferred_element_type=F32
    ).reshape(shape)
    key_part = jnp.dot(
        u_ref[pl.ds(first, size)].reshape(many), queries[...], preferred_element_type=F32
    ).reshape(shape)
    for step, place in enumerate(places):
        key_ref[place] = (key_part[step] * scale).astype(key_ref.dtype)
        value_ref[place] = value_part[step].astype(value_ref.dtype)


def away_kernel(count, width, n_q, plane, n_y, *refs):
    w_ref, u_ref, stat_ref, all_queries, all_grads, refs = *refs[:5], refs[5:]
    got_refs, refs = refs[: n_q - 1][::-1], refs[n_q - 1 :]
    other_k_ref, other_v_ref, queries, grads, shares_ref, table = refs
    chunks = n_q * count // LANES
    scale = 1.0 / math.sqrt(width)
    levels = [stat_ref[1:2, :]]
    for ref in got_refs:
        tail = ref[count:, :].astype(F32)
        step = tail.shape[0] // 4
        summed = tail[:step] + tail[step : 2 * step] + tail[2 * step : 3 * step]
        levels.append(jnp.concatenate([summed[c : c + 1] for c in range(chunks)], axis=1))
    top = functools.reduce(jnp.maximum, levels)
    shares = [jnp.exp2(one - top) for one in levels]
    inverse = 1.0 / functools.reduce(jnp.add, shares)
    table[...] = jnp.zeros_like(table)
    table[0:1, :] = jnp.exp2(stat_ref[0:1, :] - top) * inverse
    for index, share in enumerate(shares, 1):
        table[index : index + 1, :] = share * inverse * scale
    columns = jnp.transpose(table[...])
    shares_ref[...] = columns
    queries[...] = (all_queries[...].astype(F32) * columns[:, 0:1]).astype(BF16)
    grads[...] = (all_grads[...].astype(F32) * columns[:, 0:1]).astype(BF16)
    half = w_ref.shape[0] // 2
    places = plane_places(plane, n_y)
    if half <= 4:
        products(
            w_ref, u_ref, half, half, places, queries, grads, other_k_ref, other_v_ref, scale
        )
    else:
        for i, place in enumerate(places):
            products(
                w_ref, u_ref, half + i, 1, [place], queries, grads, other_k_ref, other_v_ref, scale
            )


def query_kernel(own_ref, shares_ref, *refs):
    *got_refs, low_ref, high_ref = refs
    count, _ = own_ref.shape
    own = shares_ref[line_rows(0, count), :]
    query_grad = own_ref[...].astype(F32) * own[:, 1:2]
    for index, ref in enumerate(got_refs, 2):
        query_grad = query_grad + ref[:count, :].astype(F32) * own[:, index : index + 1]
    cut = low_ref.shape[0]
    low_ref[...] = query_grad[:cut].astype(BF16)
    high_ref[...] = query_grad[cut:].astype(BF16)


def home_kernel(plane, n_y, w_ref, u_ref, queries, grads, key_ref, value_ref):
    half = w_ref.shape[0] // 2
    places = plane_places(plane, n_y)
    scale = 1.0 / math.sqrt(queries.shape[1])
    if half <= 4:
        products(w_ref, u_ref, 0, half, places, queries, grads, key_ref, value_ref, scale)
    else:
        for i, place in enumerate(places):
            products(w_ref, u_ref, i, 1, [place], queries, grads, key_ref, value_ref, scale)


def token_product(plane, n_y, x_refs, g_refs, inputs, grads):
    query_ref, key_ref, value_ref = g_refs
    n_plane = len(plane)
    count, width = key_ref.shape[1:]
    cut = cut_rows(count)
    high, rest = n_plane * cut, count - cut
    core_id = lax.axis_index("core")
    for slot, place in enumerate(plane_places(plane, n_y)):
        rows = slice(slot * count, (slot + 1) * count)
        inputs[rows, :] = x_refs[slot][core_id]
        middle = slot * count + cut
        grads[slot * count : middle, :width] = query_ref[slot * cut : (slot + 1) * cut, :]
        grads[middle : (slot + 1) * count, :width] = query_ref[
            high + slot * rest : high + (slot + 1) * rest, :
        ]
        grads[rows, width : 2 * width] = key_ref[place]
        grads[rows, 2 * width :] = value_ref[place]
    return dot_tn(inputs[...], grads[...])


def near_kernel(plane, n_y, *refs):
    x_refs, g_refs = refs[: len(plane)], refs[len(plane) : len(plane) + 3]
    sum_ref, inputs, grads = refs[len(plane) + 3 :]
    sum_ref[...] = token_product(plane, n_y, x_refs, g_refs, inputs, grads)


def far_kernel(plane, n_y, n_z, near_ref, *refs):
    x_refs, g_refs = refs[: len(plane)], refs[len(plane) : len(plane) + 3]
    refs = refs[len(plane) + 3 :]
    out_refs, (inputs, grads, sums) = refs[:n_z], refs[n_z:]
    total = near_ref[...] + token_product(plane, n_y, x_refs, g_refs, inputs, grads)
    sums[...] = total.reshape(sums.shape)
    z_id = lax.axis_index("z")
    for slot, ref in enumerate(out_refs):
        ref[...] = sums[z_id ^ slot].astype(ref.dtype)


def xor_permute(value, names, offsets):
    sizes = [lax.axis_size(name) for name in names]
    pairs = []
    for source in range(math.prod(sizes)):
        rest, digits = source, []
        for size in reversed(sizes):
            digits.append(rest % size)
            rest //= size
        target = 0
        for digit, size, offset in zip(reversed(digits), sizes, offsets):
            target = target * size + (digit ^ offset)
        pairs.append((source, target))
    return lax.ppermute(value, tuple(names), pairs)


def local(axes, layer_input, queries, keys, values, forward_out, out_grad, token_pos, block_sample):
    sizes = dict(axes)
    n_row, n_z, n_y, n_core = (sizes[name] for name in ("row", "z", "y", "core"))
    count, width = queries.shape
    model_width = layer_input.shape[1]
    total = n_z * count
    plane = [(a, b) for a in range(n_row) for b in range(n_y)]
    n_plane = len(plane)
    n_pieces = n_core * n_plane

    def over_plane(value, where):
        return xor_permute(value, ("row", "y"), where)

    def over_z(values):
        far_first = reversed(list(enumerate(values, 1)))
        return [xor_permute(value, ("z",), (offset,)) for offset, value in far_first][::-1]

    def over_core(value):
        return xor_permute(value, ("core",), (1,))

    packed = jax.ShapeDtypeStruct((count + PAD_ROWS, 2 * width), BF16)
    qg, kv, x_here = pl.pallas_call(
        functools.partial(pack_kernel, axes),
        out_shape=(packed, packed, jax.ShapeDtypeStruct(layer_input.shape, BF16)),
        in_specs=[HBM] * 8,
        out_specs=(VMEM, VMEM, VMEM),
        scratch_shapes=[
            pltpu.VMEM((count, width), BF16),
            pltpu.VMEM((2 * width, width), F32),
            pltpu.VMEM((PAD_ROWS, 2 * width), F32),
            pltpu.VMEM((token_pos.shape[0] // LANES, LANES), jnp.int32),
            pltpu.SMEM(block_sample.shape, jnp.int32),
            pltpu.SemaphoreType.DMA((8,)),
        ],
        compiler_params=params(8 * MIB),
        name="pack",
    )(
        *(
            pltpu.with_memory_space_constraint(value, pltpu.HBM)
            for value in (
                queries,
                keys,
                values,
                forward_out,
                out_grad,
                layer_input,
                token_pos.reshape(-1, LANES),
                block_sample,
            )
        )
    )

    blk = model_width // (n_z * n_y * n_core * n_row)
    kv_near = [kv] + [over_plane(kv, where) for where in plane[1:]]
    qg_all = [qg] + over_z([qg] * (n_z - 1))
    x_here, kv_near[1] = lax.optimization_barrier((x_here, kv_near[1]))
    x_send = pl.pallas_call(
        functools.partial(deal_kernel, (n_row, n_z, n_y, n_core)),
        out_shape=[jax.ShapeDtypeStruct((n_core, count, n_z * blk), BF16)] * n_plane,
        in_specs=[VMEM],
        out_specs=[VMEM] * n_plane,
        scratch_shapes=[pltpu.VMEM((n_plane, n_core, count, n_z * blk), BF16)],
        compiler_params=params(16 * MIB),
        name="deal",
    )(x_here)
    stacked = jnp.stack(kv_near)
    kv_all = [piece[None] for piece in kv_near] if n_pieces <= 8 else [stacked]
    kv_all = kv_all + [over_core(stacked)]

    tail_rows = 4 * -(-total // (8 * LANES)) * 8
    big = jax.ShapeDtypeStruct((n_pieces, count, total), BF16)
    lines = pl.pallas_call(
        functools.partial(lines_kernel, count, width, n_z),
        out_shape=[jax.ShapeDtypeStruct((total, width), BF16)] * 2
        + [jax.ShapeDtypeStruct((8, total), F32)],
        in_specs=[VMEM] * n_z,
        out_specs=[VMEM] * 3,
        compiler_params=params(8 * MIB),
        cost_estimate=pl.CostEstimate(flops=int(5e9), bytes_accessed=0, transcendentals=0),
        name="lines",
    )(*qg_all[::-1])
    w, u, stat, own_part, *send = pl.pallas_call(
        functools.partial(forward_kernel, count, width, n_z, len(kv_all)),
        out_shape=[
            big,
            big,
            jax.ShapeDtypeStruct((8, total), F32),
            jax.ShapeDtypeStruct((count, width), BF16),
        ]
        + [jax.ShapeDtypeStruct((count + tail_rows, width), BF16)] * (n_z - 1),
        in_specs=[VMEM] * (3 + len(kv_all)),
        out_specs=[VMEM] * (4 + n_z - 1),
        scratch_shapes=[
            pltpu.VMEM((n_pieces, count, width), BF16),
            pltpu.VMEM((n_pieces, count, width), BF16),
            pltpu.VMEM((n_pieces, count, 8), F32),
            pltpu.VMEM((math.gcd(n_pieces, 8), count, total), F32),
            pltpu.VMEM((math.gcd(n_pieces, 8), count, total), F32),
            pltpu.VMEM((total, width), BF16),
        ],
        compiler_params=params(24 * MIB if n_pieces <= 8 else 56 * MIB),
        cost_estimate=pl.CostEstimate(flops=int(3e10), bytes_accessed=0, transcendentals=0),
        name="forward",
    )(*lines, *kv_all)
    got = over_z(send)
    x_all = [x_send[0]] + [over_plane(x, where) for x, where in zip(x_send[1:], plane[1:])]
    far = [index for index, (a, b) in enumerate(plane) if a and b]
    near = [index for index, (a, b) in enumerate(plane) if (a or b) and not (a and b)]

    def together(values, indices):
        values, some = lax.optimization_barrier((values, [x_all[index] for index in indices]))
        for index, value in zip(indices, some):
            x_all[index] = value
        return values

    got = together(got, far)

    half = (n_plane, count, width)
    cut = cut_rows(count)
    other_k, other_v, queries_low, grads_low, shares = pl.pallas_call(
        functools.partial(away_kernel, count, width, n_z, plane, n_y),
        out_shape=[jax.ShapeDtypeStruct(half, BF16)] * 2
        + [jax.ShapeDtypeStruct((total, width), BF16)] * 2
        + [jax.ShapeDtypeStruct((total, 8), F32)],
        in_specs=[VMEM] * (5 + n_z - 1),
        out_specs=[VMEM] * 5,
        scratch_shapes=[pltpu.VMEM((8, total), F32)],
        compiler_params=params(16 * MIB if n_pieces <= 8 else 56 * MIB),
        cost_estimate=pl.CostEstimate(flops=int(3e10), bytes_accessed=0, transcendentals=0),
        name="away",
    )(w, u, stat, *lines[:2], *got[::-1])
    query_low, query_high = pl.pallas_call(
        query_kernel,
        out_shape=[
            jax.ShapeDtypeStruct((cut, width), BF16),
            jax.ShapeDtypeStruct((count - cut, width), BF16),
        ],
        in_specs=[VMEM] * (2 + n_z - 1),
        out_specs=[VMEM] * 2,
        compiler_params=params(8 * MIB),
        name="query",
    )(own_part, shares, *got)
    mine_k, mine_v = pl.pallas_call(
        functools.partial(home_kernel, plane, n_y),
        out_shape=[jax.ShapeDtypeStruct(half, F32 if n_pieces <= 8 else BF16)] * 2,
        in_specs=[VMEM] * 4,
        out_specs=[VMEM] * 2,
        compiler_params=params(16 * MIB if n_pieces <= 8 else 56 * MIB),
        name="home",
    )(w, u, queries_low, grads_low)
    mine_k, mine_v = together([mine_k, mine_v], near)
    key_sum = mine_k.astype(F32) + over_core(other_k).astype(F32)
    value_sum = mine_v.astype(F32) + over_core(other_v).astype(F32)
    x_pair = [over_core(x) for x in x_all]
    row_bits = [(1 << bit, 0) for bit in range(n_row.bit_length() - 1)]
    y_bits = [(0, 1 << bit) for bit in range(n_y.bit_length() - 1)]
    lows, highs = {(0, 0): query_low}, {(0, 0): query_high}
    body = n_plane * count

    def payload(sums, pieces):
        return jnp.concatenate([sums.astype(BF16).reshape(body, width), *pieces.values()])

    def take(sums, pieces, got, hop, rows):
        for index, (a, b) in enumerate(list(pieces)):
            first = body + index * rows
            pieces[a ^ hop[0], b ^ hop[1]] = got[first : first + rows]
        return sums + got[:body].reshape(half).astype(F32)

    for key_hop, value_hop in zip(row_bits + y_bits, y_bits + row_bits):
        sent = lax.optimization_barrier((payload(key_sum, lows), payload(value_sum, highs)))
        key_got, value_got = lax.optimization_barrier(
            (over_plane(sent[0], key_hop), over_plane(sent[1], value_hop))
        )
        key_sum = take(key_sum, lows, key_got, key_hop, cut)
        value_sum = take(value_sum, highs, value_got, value_hop, count - cut)
    place = plane_places(plane, n_y)[0]
    key_low, value_low = key_sum.astype(BF16), value_sum.astype(BF16)
    key_grad = lax.dynamic_index_in_dim(key_low, place, 0, False)
    value_grad = lax.dynamic_index_in_dim(value_low, place, 0, False)
    query_all = [pieces[where] for pieces in (lows, highs) for where in plane]
    g_near = [jnp.concatenate(query_all), key_low, value_low]
    g_far = [over_core(g) for g in g_near]

    tokens = n_plane * count
    operands = [pltpu.VMEM((tokens, n_z * blk), BF16), pltpu.VMEM((tokens, 3 * width), BF16)]
    near_sum = pl.pallas_call(
        functools.partial(near_kernel, plane, n_y),
        out_shape=jax.ShapeDtypeStruct((n_z * blk, 3 * width), F32),
        in_specs=[VMEM] * (n_plane + 3),
        out_specs=VMEM,
        scratch_shapes=operands,
        compiler_params=params(24 * MIB),
        name="near",
    )(*x_all, *g_near)
    mine, *send = pl.pallas_call(
        functools.partial(far_kernel, plane, n_y, n_z),
        out_shape=[jax.ShapeDtypeStruct((blk, 3 * width), F32)]
        + [jax.ShapeDtypeStruct((blk, 3 * width), BF16)] * (n_z - 1),
        in_specs=[VMEM] * (n_plane + 4),
        out_specs=[VMEM] * n_z,
        scratch_shapes=operands + [pltpu.VMEM((n_z, blk, 3 * width), F32)],
        compiler_params=params(24 * MIB),
        name="far",
    )(near_sum, *x_pair, *g_far)
    mine, query_low, query_high = lax.optimization_barrier((mine, query_low, query_high))
    both = [mine] + send
    piece = both[0]
    for part in over_z(both[1:]):
        piece = piece + part.astype(F32)
    low = piece.astype(BF16)
    parts = [piece] + [xor_permute(low, ("row",), (a,)) for a in range(1, n_row)]
    weight_grad = pl.pallas_call(
        assemble_kernel,
        out_shape=jax.ShapeDtypeStruct((n_row, blk, 3 * width), F32),
        in_specs=[VMEM] * n_row,
        out_specs=VMEM,
        compiler_params=params(8 * MIB),
        name="assemble",
    )(*parts).reshape(n_row * blk, 3 * width)
    query_grad = jnp.concatenate([query_low, query_high])
    return query_grad, key_grad, value_grad, weight_grad


def solution(mesh):
    n_row, n_col = mesh.shape["row"], mesh.shape["col"]
    n_core = 2
    n_z = 1 << ((n_col.bit_length() - 1) // 2)
    n_y = n_col // (n_core * n_z)
    axes = (("row", n_row), ("z", n_z), ("y", n_y), ("core", n_core))
    split = Mesh(
        mesh.devices.reshape(tuple(size for _, size in axes)), tuple(name for name, _ in axes)
    )
    tokens = P(("row", "z", "y", "core"), None)
    return jax.shard_map(
        functools.partial(local, axes),
        mesh=split,
        in_specs=(tokens,) * 6 + (P(), P()),
        out_specs=(tokens, tokens, tokens, P(("z", "y", "core"), None)),
        check_vma=False,
    )
```

time: 67.7 us -> 64.9 us (0.959)
  waiting for transfers between devices: 25.2 us -> 22.4 us
    ppermute x30, waiting for transfers between devices: 25.2 us -> 22.4 us  [xor_permute(): return lax.ppermute(value, tuple(names), pairs)]
    pallas_call x2 -> x5, Pallas kernels: 3.1 us -> 2.78 us  [the longest x1 0.94 us: local(): pl.pallas_call(functools.partial(away_kernel, count, width, n_z, plane, n...]
  transfers between devices with their start and end apart: 30 -> 30, of which waited for: 16 -> 9; matrix products, arithmetic and copies ran while one was open for 2% -> 3% of each run, Pallas kernels for 5% -> 8%
where the time goes in v4:
time: 64.9 us; the launch traced here: 64.7 us
  starting transfers between devices  30.9 us (48%)
  waiting for transfers between devices  22.4 us (35%)
  Pallas kernels  8 us (12%)
  local copies, waits for them, and re-layouts  1.37 us (2%)
  other arithmetic  1.12 us (2%)
  between operations  0.94 us (1%)
    ppermute x30, starting transfers between devices, xor_permute(): return lax.ppermute(value, tuple(names), pairs)  30.9 us
    ppermute x30, waiting for transfers between devices, xor_permute(): return lax.ppermute(value, tuple(names), pairs)  22.4 us
    pallas_call x1, Pallas kernels, local(): pl.pallas_call(functools.partial(forward_kernel, count, width, n_z, len(k...  2.26 us
    pallas_call x1, Pallas kernels, local(): pl.pallas_call(functools.partial(pack_kernel, axes), out_shape=(packed, p...  1.41 us
  transfers between devices with their start and end apart: 30, of which 9 were waited for; matrix products, arithmetic and copies ran while one was open for 3% of the time, Pallas kernels for 8%

profile of v4, /device:TPU:0, one launch (start us, length us, event | category | flops | bytes accessed | tf_op | source)
XLA Modules:
  0.0 64.7 jit_solution(3586677470406880864)
XLA Ops:
  0.6 1.4 %pack.1 = (bf16[176,256]{1,0:T(8,128)(2,1)S(1)}, bf16[176,256]{1,0:T(8,128)(2,1)S(1)}, bf16[160,3072]{1,0:T(8,128)(2,1)S(1)}) custom-call(bf16[160,128]{1,0:T(8,128)(2,1)} %q_hbm.1, bf16[160,128]{1,0:T(8,128)(2,1)} %k_hbm.1, bf16[160,128]{1,0:T(8,128)(2,1)} %v_hbm.1, bf16[160,128]{1,0:T(8,128)(2,1)} %o_hbm.1, bf16[160,128]{1,0:T(8,128)(2,1)} %g_hbm.1, ...), custom_call_target="tpu_custom_call" | custom-call | tf_op jit(solution)/shard_map/pack/pallas_call | solution.py:418
  2.1 3.0 %collective-permute-start = (bf16[176,256]{1,0:T(8,128)(2,1)S(1)}, bf16[176,256]{1,0:T(8,128)(2,1)S(1)}, u32[]{:S(2)}, u32[]{:S(2)}) collective-permute-start(bf16[176,256]{1,0:T(8,128)(2,1)S(1)} %get-tuple-element.56), channel_id=1, source_target_pairs={{0,2},{2,0},{16,18},{18,16},{1,3},{3,1},{17,19},{19,17},{4,6},{6,4... | collective-permute-start | bytes 270344 | tf_op jit(solution)/shard_map/ppermute | solution.py:394
  5.1 1.5 %collective-permute-start.4 = (bf16[176,256]{1,0:T(8,128)(2,1)S(1)}, bf16[176,256]{1,0:T(8,128)(2,1)S(1)}, u32[]{:S(2)}, u32[]{:S(2)}) collective-permute-start(bf16[176,256]{1,0:T(8,128)(2,1)S(1)} %get-tuple-element.56), channel_id=1, source_target_pairs={{0,16},{2,18},{16,0},{18,2},{1,17},{3,19},{17,1},{19,3},{4,20},{6,... | collective-permute-start | bytes 270344 | tf_op jit(solution)/shard_map/ppermute | solution.py:394
  6.6 4.0 %collective-permute-start.1 = (bf16[176,256]{1,0:T(8,128)(2,1)S(1)}, bf16[176,256]{1,0:T(8,128)(2,1)S(1)}, u32[]{:S(2)}, u32[]{:S(2)}) collective-permute-start(bf16[176,256]{1,0:T(8,128)(2,1)S(1)} %get-tuple-element.59.refs_3_), channel_id=1, source_target_pairs={{0,12},{4,8},{8,4},{12,0},{1,13},{5,9},{9,5},{13,1},{2,14},{6,10},... | collective-permute-start | bytes 270344 | tf_op jit(solution)/shard_map/ppermute | solution.py:394
  10.7 0.6 collective-permute-start.3
  11.2 0.8 %collective-permute-done.5 = bf16[176,256]{1,0:T(8,128)(2,1)S(1)} collective-permute-done((bf16[176,256]{1,0:T(8,128)(2,1)S(1)}, bf16[176,256]{1,0:T(8,128)(2,1)S(1)}, u32[]{:S(2)}, u32[]{:S(2)}) %collective-permute-start.5) | collective-permute-done | bytes 90144 | tf_op jit(solution)/shard_map/ppermute | solution.py:394
  12.1 0.1 collective-permute-start.6
  12.1 0.7 %deal.1 = (bf16[2,160,384]{2,1,0:T(8,128)(2,1)S(1)}, bf16[2,160,384]{2,1,0:T(8,128)(2,1)S(1)}, bf16[2,160,384]{2,1,0:T(8,128)(2,1)S(1)}, bf16[2,160,384]{2,1,0:T(8,128)(2,1)S(1)}) custom-call(bf16[160,3072]{1,0:T(8,128)(2,1)S(1)} %get-tuple-element.57.x_ref), custom_call_target="tpu_custom_call" | custom-call | tf_op jit(solution)/shard_map/deal/pallas_call | solution.py:453
  12.8 2.0 %collective-permute-start.10 = (bf16[2,160,384]{2,1,0:T(8,128)(2,1)S(1)}, bf16[2,160,384]{2,1,0:T(8,128)(2,1)S(1)}, u32[]{:S(2)}, u32[]{:S(2)}) collective-permute-start(bf16[2,160,384]{2,1,0:T(8,128)(2,1)S(1)} %get-tuple-element.70), channel_id=1, source_target_pairs={{0,18},{2,16},{16,2},{18,0},{1,19},{3,17},{17,3},{19,1},{4,22},{6,... | collective-permute-start | bytes 737288 | tf_op jit(solution)/shard_map/ppermute | solution.py:394
  14.8 2.6 %collective-permute-done.2.refs_1_ = bf16[176,256]{1,0:T(8,128)(2,1)S(1)} collective-permute-done((bf16[176,256]{1,0:T(8,128)(2,1)S(1)}, bf16[176,256]{1,0:T(8,128)(2,1)S(1)}, u32[]{:S(2)}, u32[]{:S(2)}) %collective-permute-start.2) | collective-permute-done | bytes 90144 | tf_op jit(solution)/shard_map/ppermute | solution.py:394
  17.4 0.1 lines.1
  17.6 2.3 %forward.1 = (bf16[8,160,640]{2,1,0:T(8,128)(2,1)S(1)}, bf16[8,160,640]{2,1,0:T(8,128)(2,1)S(1)}, f32[8,640]{1,0:T(8,128)S(1)}, bf16[160,128]{1,0:T(8,128)(2,1)S...) custom-call(bf16[640,128]{1,0:T(8,128)(2,1)S(1)} %get-tuple-element.60.refs_0_.refs_3_, ...), custom_call_target="tpu_custom_call" | custom-call | flops 30000001024 | tf_op jit(solution)/shard_map/forward/pallas_call | solution.py:478
  19.8 0.7 %collective-permute-start.7 = (bf16[192,128]{1,0:T(8,128)(2,1)S(1)}, bf16[192,128]{1,0:T(8,128)(2,1)S(1)}, u32[]{:S(2)}, u32[]{:S(2)}) collective-permute-start(bf16[192,128]{1,0:T(8,128)(2,1)S(1)} %get-tuple-element.67), channel_id=1, source_target_pairs={{0,4},{4,0},{8,12},{12,8},{1,5},{5,1},{9,13},{13,9},{2,6},{6,2},{1... | collective-permute-start | bytes 147464 | tf_op jit(solution)/shard_map/ppermute | solution.py:394
  20.6 2.4 %collective-permute-start.8 = (bf16[192,128]{1,0:T(8,128)(2,1)S(1)}, bf16[192,128]{1,0:T(8,128)(2,1)S(1)}, u32[]{:S(2)}, u32[]{:S(2)}) collective-permute-start(bf16[192,128]{1,0:T(8,128)(2,1)S(1)} %get-tuple-element.68), channel_id=1, source_target_pairs={{0,8},{4,12},{8,0},{12,4},{1,9},{5,13},{9,1},{13,5},{2,10},{6,14},... | collective-permute-start | bytes 147464 | tf_op jit(solution)/shard_map/ppermute | solution.py:394
  23.0 1.3 %collective-permute-start.9 = (bf16[192,128]{1,0:T(8,128)(2,1)S(1)}, bf16[192,128]{1,0:T(8,128)(2,1)S(1)}, u32[]{:S(2)}, u32[]{:S(2)}) collective-permute-start(bf16[192,128]{1,0:T(8,128)(2,1)S(1)} %get-tuple-element.69), channel_id=1, source_target_pairs={{0,12},{4,8},{8,4},{12,0},{1,13},{5,9},{9,5},{13,1},{2,14},{6,10},... | collective-permute-start | bytes 147464 | tf_op jit(solution)/shard_map/ppermute | solution.py:394
  24.3 1.5 %collective-permute-start.11 = (bf16[2,160,384]{2,1,0:T(8,128)(2,1)S(1)}, bf16[2,160,384]{2,1,0:T(8,128)(2,1)S(1)}, u32[]{:S(2)}, u32[]{:S(2)}) collective-permute-start(bf16[2,160,384]{2,1,0:T(8,128)(2,1)S(1)} %get-tuple-element.78), channel_id=1, source_target_pairs={{0,2},{2,0},{16,18},{18,16},{1,3},{3,1},{17,19},{19,17},{4,6},{6,4... | collective-permute-start | bytes 737288 | tf_op jit(solution)/shard_map/ppermute | solution.py:394
  25.8 1.5 %collective-permute-start.12 = (bf16[2,160,384]{2,1,0:T(8,128)(2,1)S(1)}, bf16[2,160,384]{2,1,0:T(8,128)(2,1)S(1)}, u32[]{:S(2)}, u32[]{:S(2)}) collective-permute-start(bf16[2,160,384]{2,1,0:T(8,128)(2,1)S(1)} %get-tuple-element.79), channel_id=1, source_target_pairs={{0,16},{2,18},{16,0},{18,2},{1,17},{3,19},{17,1},{19,3},{4,20},{6,... | collective-permute-start | bytes 737288 | tf_op jit(solution)/shard_map/ppermute | solution.py:394
  27.3 1.5 %collective-permute-done.9.refs_5_.refs_2_ = bf16[192,128]{1,0:T(8,128)(2,1)S(1)} collective-permute-done((bf16[192,128]{1,0:T(8,128)(2,1)S(1)}, bf16[192,128]{1,0:T(8,128)(2,1)S(1)}, u32[]{:S(2)}, u32[]{:S(2)}) %collective-permute-start.9) | collective-permute-done | bytes 49184 | tf_op jit(solution)/shard_map/ppermute | solution.py:394
  28.9 0.9 %away.1 = (bf16[4,160,128]{2,1,0:T(8,128)(2,1)S(1)}, bf16[4,160,128]{2,1,0:T(8,128)(2,1)S(1)}, bf16[640,128]{1,0:T(8,128)(2,1)S(1)}, bf16[640,128]{1,0:T(8,128)(2,1)S(1)}, f32[640,8]{1,0:T(8,128)S(1)}) custom-call(bf16[8,160,640]{2,1,0:T(8,128)(2,1)S(1)} %get-tuple-element.64.refs_0_.w_ref, bf16[8,160,640]{2,1,0:T(8,128)(2,1)S(1)} %get-tuple-element.65.refs_1_.u_ref, ...), custom_call_target="tpu_custom_call" | custom-call | flops 30000001024 | tf_op jit(solution)/shard_map/away/pallas_call | solution.py:516
  29.9 0.5 collective-permute-start.14
  30.4 0.6 home.1
  31.0 1.0 %collective-permute-done.12.refs_2_ = bf16[2,160,384]{2,1,0:T(8,128)(2,1)S(1)} collective-permute-done((bf16[2,160,384]{2,1,0:T(8,128)(2,1)S(1)}, bf16[2,160,384]{2,1,0:T(8,128)(2,1)S(1)}, u32[]{:S(2)}, u32[]{:S(2)}) %collective-permute-start.12) | collective-permute-done | bytes 245792 | tf_op jit(solution)/shard_map/ppermute | solution.py:394
  32.0 0.2 query.1
  32.3 1.6 %collective-permute-start.15 = (bf16[752,128]{1,0:T(8,128)(2,1)S(1)}, bf16[752,128]{1,0:T(8,128)(2,1)S(1)}, u32[]{:S(2)}, u32[]{:S(2)}) collective-permute-start(bf16[752,128]{1,0:T(8,128)(2,1)S(1)} %pad_maximum_fusion.2), channel_id=1, source_target_pairs={{0,16},{2,18},{16,0},{18,2},{1,17},{3,19},{17,1},{19,3},{4,20},{6,... | collective-permute-start | bytes 577544 | tf_op jit(solution)/shard_map/ppermute | solution.py:394
  33.9 0.8 %collective-permute-start.16 = (bf16[688,128]{1,0:T(8,128)(2,1)S(1)}, bf16[688,128]{1,0:T(8,128)(2,1)S(1)}, u32[]{:S(2)}, u32[]{:S(2)}) collective-permute-start(bf16[688,128]{1,0:T(8,128)(2,1)S(1)} %pad_maximum_fusion.4), channel_id=1, source_target_pairs={{0,2},{2,0},{16,18},{18,16},{1,3},{3,1},{17,19},{19,17},{4,6},{6,4... | collective-permute-start | bytes 528392 | tf_op jit(solution)/shard_map/ppermute | solution.py:394
  34.7 4.8 %collective-permute-done.16 = bf16[688,128]{1,0:T(8,128)(2,1)S(1)} collective-permute-done((bf16[688,128]{1,0:T(8,128)(2,1)S(1)}, bf16[688,128]{1,0:T(8,128)(2,1)S(1)}, u32[]{:S(2)}, u32[]{:S(2)}) %collective-permute-start.16) | collective-permute-done | bytes 176160 | tf_op jit(solution)/shard_map/ppermute | solution.py:394
  39.8 1.6 %collective-permute-start.17 = (bf16[864,128]{1,0:T(8,128)(2,1)S(1)}, bf16[864,128]{1,0:T(8,128)(2,1)S(1)}, u32[]{:S(2)}, u32[]{:S(2)}) collective-permute-start(bf16[864,128]{1,0:T(8,128)(2,1)S(1)} %pad_maximum_fusion.1), channel_id=1, source_target_pairs={{0,2},{2,0},{16,18},{18,16},{1,3},{3,1},{17,19},{19,17},{4,6},{6,4... | collective-permute-start | bytes 663560 | tf_op jit(solution)/shard_map/ppermute | solution.py:394
  41.4 0.6 collective-permute-start.18
  42.0 0.5 collective-permute-start.20
  42.5 4.4 %collective-permute-done.18 = bf16[736,128]{1,0:T(8,128)(2,1)S(1)} collective-permute-done((bf16[736,128]{1,0:T(8,128)(2,1)S(1)}, bf16[736,128]{1,0:T(8,128)(2,1)S(1)}, u32[]{:S(2)}, u32[]{:S(2)}) %collective-permute-start.18) | collective-permute-done | bytes 188448 | tf_op jit(solution)/shard_map/ppermute | solution.py:394
  47.1 0.1 fusion.refs_6_
  47.1 0.6 collective-permute-start.25
  47.7 0.1 fusion.1.refs_5_
  47.8 0.1 collective-permute-start.24
  47.9 0.5 collective-permute-start.23
  48.4 0.5 near.1.near_ref
  48.9 0.6 dynamic-slice_bitcast_fusion
  49.6 0.6 far.1
  50.2 0.1 collective-permute-start.26
  50.3 1.9 %collective-permute-start.27 = (bf16[96,384]{1,0:T(8,128)(2,1)S(1)}, bf16[96,384]{1,0:T(8,128)(2,1)S(1)}, u32[]{:S(2)}, u32[]{:S(2)}) collective-permute-start(bf16[96,384]{1,0:T(8,128)(2,1)S(1)} %get-tuple-element.104), channel_id=1, source_target_pairs={{0,8},{4,12},{8,0},{12,4},{1,9},{5,13},{9,1},{13,5},{2,10},{6,14},... | collective-permute-start | bytes 221192 | tf_op jit(solution)/shard_map/ppermute | solution.py:394
  52.2 2.5 %collective-permute-start.28 = (bf16[96,384]{1,0:T(8,128)(2,1)S(1)}, bf16[96,384]{1,0:T(8,128)(2,1)S(1)}, u32[]{:S(2)}, u32[]{:S(2)}) collective-permute-start(bf16[96,384]{1,0:T(8,128)(2,1)S(1)} %get-tuple-element.105), channel_id=1, source_target_pairs={{0,12},{4,8},{8,4},{12,0},{1,13},{5,9},{9,5},{13,1},{2,14},{6,10},... | collective-permute-start | bytes 221192 | tf_op jit(solution)/shard_map/ppermute | solution.py:394
  54.6 0.6 dynamic-slice_bitcast_fusion.1
  55.3 0.4 collective-permute-done.26
  55.7 3.8 %collective-permute-done.27 = bf16[96,384]{1,0:T(8,128)(2,1)S(1)} collective-permute-done((bf16[96,384]{1,0:T(8,128)(2,1)S(1)}, bf16[96,384]{1,0:T(8,128)(2,1)S(1)}, u32[]{:S(2)}, u32[]{:S(2)}) %collective-permute-start.27) | collective-permute-done | bytes 73760 | tf_op jit(solution)/shard_map/ppermute | solution.py:394
  59.6 0.9 %collective-permute-start.29 = (bf16[96,384]{1,0:T(8,128)(2,1)S(1)}, bf16[96,384]{1,0:T(8,128)(2,1)S(1)}, u32[]{:S(2)}, u32[]{:S(2)}) collective-permute-start(bf16[96,384]{1,0:T(8,128)(2,1)S(1)} %get-tuple-element.106), channel_id=1, source_target_pairs={{0,16},{16,0},{1,17},{17,1},{2,18},{18,2},{3,19},{19,3},{4,20},{20... | collective-permute-start | bytes 221192 | tf_op jit(solution)/shard_map/ppermute | solution.py:394
  60.5 0.6 pad_maximum_fusion.5
  61.1 2.9 %collective-permute-done.29.refs_0_ = bf16[96,384]{1,0:T(8,128)(2,1)S(1)} collective-permute-done((bf16[96,384]{1,0:T(8,128)(2,1)S(1)}, bf16[96,384]{1,0:T(8,128)(2,1)S(1)}, u32[]{:S(2)}, u32[]{:S(2)}) %collective-permute-start.29) | collective-permute-done | bytes 73760 | tf_op jit(solution)/shard_map/ppermute | solution.py:394
  64.0 0.7 %assemble.1 = f32[2,96,384]{2,1,0:T(8,128)} custom-call(f32[96,384]{1,0:T(8,128)S(1)} %get-tuple-element.107.own_ref, bf16[96,384]{1,0:T(8,128)(2,1)S(1)} %collective-permute-done.29.refs_0_), custom_call_target="tpu_custom_call" | custom-call | tf_op jit(solution)/shard_map/assemble/pallas_call | solution.py:608
  (49 shorter events, 0.6 us)
Async XLA Ops:
  2.1 8.6 %collective-permute-start = (bf16[176,256]{1,0:T(8,128)(2,1)S(1)}, bf16[176,256]{1,0:T(8,128)(2,1)S(1)}, u32[]{:S(2)}, u32[]{:S(2)}) collective-permute-start(bf16[176,256]{1,0:T(8,128)(2,1)S(1)} %get-tuple-element.56), channel_id=1, source_target_pairs={{0,2},{2,0},{16,18},{18,16},{1,3},{3,1},{17,19},{19,17},{4,6},{6,4... | collective-permute-start | bytes 270344 | tf_op jit(solution)/shard_map/ppermute | solution.py:394
  5.1 6.1 %collective-permute-start.4 = (bf16[176,256]{1,0:T(8,128)(2,1)S(1)}, bf16[176,256]{1,0:T(8,128)(2,1)S(1)}, u32[]{:S(2)}, u32[]{:S(2)}) collective-permute-start(bf16[176,256]{1,0:T(8,128)(2,1)S(1)} %get-tuple-element.56), channel_id=1, source_target_pairs={{0,16},{2,18},{16,0},{18,2},{1,17},{3,19},{17,1},{19,3},{4,20},{6,... | collective-permute-start | bytes 270344 | tf_op jit(solution)/shard_map/ppermute | solution.py:394
  6.6 5.4 %collective-permute-start.5 = (bf16[176,256]{1,0:T(8,128)(2,1)S(1)}, bf16[176,256]{1,0:T(8,128)(2,1)S(1)}, u32[]{:S(2)}, u32[]{:S(2)}) collective-permute-start(bf16[176,256]{1,0:T(8,128)(2,1)S(1)} %get-tuple-element.56), channel_id=1, source_target_pairs={{0,18},{2,16},{16,2},{18,0},{1,19},{3,17},{17,3},{19,1},{4,22},{6,... | collective-permute-start | bytes 270344 | tf_op jit(solution)/shard_map/ppermute | solution.py:394
  6.6 8.2 %collective-permute-start.1 = (bf16[176,256]{1,0:T(8,128)(2,1)S(1)}, bf16[176,256]{1,0:T(8,128)(2,1)S(1)}, u32[]{:S(2)}, u32[]{:S(2)}) collective-permute-start(bf16[176,256]{1,0:T(8,128)(2,1)S(1)} %get-tuple-element.59.refs_3_), channel_id=1, source_target_pairs={{0,12},{4,8},{8,4},{12,0},{1,13},{5,9},{9,5},{13,1},{2,14},{6,10},... | collective-permute-start | bytes 270344 | tf_op jit(solution)/shard_map/ppermute | solution.py:394
  10.7 6.8 %collective-permute-start.2 = (bf16[176,256]{1,0:T(8,128)(2,1)S(1)}, bf16[176,256]{1,0:T(8,128)(2,1)S(1)}, u32[]{:S(2)}, u32[]{:S(2)}) collective-permute-start(bf16[176,256]{1,0:T(8,128)(2,1)S(1)} %get-tuple-element.59.refs_3_), channel_id=1, source_target_pairs={{0,8},{4,12},{8,0},{12,4},{1,9},{5,13},{9,1},{13,5},{2,10},{6,14},... | collective-permute-start | bytes 270344 | tf_op jit(solution)/shard_map/ppermute | solution.py:394
  10.7 6.8 %collective-permute-start.3 = (bf16[176,256]{1,0:T(8,128)(2,1)S(1)}, bf16[176,256]{1,0:T(8,128)(2,1)S(1)}, u32[]{:S(2)}, u32[]{:S(2)}) collective-permute-start(bf16[176,256]{1,0:T(8,128)(2,1)S(1)} %get-tuple-element.59.refs_3_), channel_id=1, source_target_pairs={{0,4},{4,0},{8,12},{12,8},{1,5},{5,1},{9,13},{13,9},{2,6},{6,2},{1... | collective-permute-start | bytes 270344 | tf_op jit(solution)/shard_map/ppermute | solution.py:394
  12.1 5.5 %collective-permute-start.6 = (bf16[4,176,256]{2,1,0:T(8,128)(2,1)S(1)}, bf16[4,176,256]{2,1,0:T(8,128)(2,1)S(1)}, u32[]{:S(2)}, u32[]{:S(2)}) collective-permute-start(bf16[4,176,256]{2,1,0:T(8,128)(2,1)S(1)} %pad_maximum_fusion), channel_id=1, source_target_pairs={{0,1},{1,0},{2,3},{3,2},{4,5},{5,4},{6,7},{7,6},{8,9},{9,8},{10,11... | collective-permute-start | bytes 1081352 | tf_op jit(solution)/shard_map/ppermute | solution.py:394
  12.8 13.0 %collective-permute-start.10 = (bf16[2,160,384]{2,1,0:T(8,128)(2,1)S(1)}, bf16[2,160,384]{2,1,0:T(8,128)(2,1)S(1)}, u32[]{:S(2)}, u32[]{:S(2)}) collective-permute-start(bf16[2,160,384]{2,1,0:T(8,128)(2,1)S(1)} %get-tuple-element.70), channel_id=1, source_target_pairs={{0,18},{2,16},{16,2},{18,0},{1,19},{3,17},{17,3},{19,1},{4,22},{6,... | collective-permute-start | bytes 737288 | tf_op jit(solution)/shard_map/ppermute | solution.py:394
  19.8 7.5 %collective-permute-start.7 = (bf16[192,128]{1,0:T(8,128)(2,1)S(1)}, bf16[192,128]{1,0:T(8,128)(2,1)S(1)}, u32[]{:S(2)}, u32[]{:S(2)}) collective-permute-start(bf16[192,128]{1,0:T(8,128)(2,1)S(1)} %get-tuple-element.67), channel_id=1, source_target_pairs={{0,4},{4,0},{8,12},{12,8},{1,5},{5,1},{9,13},{13,9},{2,6},{6,2},{1... | collective-permute-start | bytes 147464 | tf_op jit(solution)/shard_map/ppermute | solution.py:394
  20.6 6.7 %collective-permute-start.8 = (bf16[192,128]{1,0:T(8,128)(2,1)S(1)}, bf16[192,128]{1,0:T(8,128)(2,1)S(1)}, u32[]{:S(2)}, u32[]{:S(2)}) collective-permute-start(bf16[192,128]{1,0:T(8,128)(2,1)S(1)} %get-tuple-element.68), channel_id=1, source_target_pairs={{0,8},{4,12},{8,0},{12,4},{1,9},{5,13},{9,1},{13,5},{2,10},{6,14},... | collective-permute-start | bytes 147464 | tf_op jit(solution)/shard_map/ppermute | solution.py:394
  23.0 5.9 %collective-permute-start.9 = (bf16[192,128]{1,0:T(8,128)(2,1)S(1)}, bf16[192,128]{1,0:T(8,128)(2,1)S(1)}, u32[]{:S(2)}, u32[]{:S(2)}) collective-permute-start(bf16[192,128]{1,0:T(8,128)(2,1)S(1)} %get-tuple-element.69), channel_id=1, source_target_pairs={{0,12},{4,8},{8,4},{12,0},{1,13},{5,9},{9,5},{13,1},{2,14},{6,10},... | collective-permute-start | bytes 147464 | tf_op jit(solution)/shard_map/ppermute | solution.py:394
  24.3 6.7 %collective-permute-start.11 = (bf16[2,160,384]{2,1,0:T(8,128)(2,1)S(1)}, bf16[2,160,384]{2,1,0:T(8,128)(2,1)S(1)}, u32[]{:S(2)}, u32[]{:S(2)}) collective-permute-start(bf16[2,160,384]{2,1,0:T(8,128)(2,1)S(1)} %get-tuple-element.78), channel_id=1, source_target_pairs={{0,2},{2,0},{16,18},{18,16},{1,3},{3,1},{17,19},{19,17},{4,6},{6,4... | collective-permute-start | bytes 737288 | tf_op jit(solution)/shard_map/ppermute | solution.py:394
  25.8 6.2 %collective-permute-start.12 = (bf16[2,160,384]{2,1,0:T(8,128)(2,1)S(1)}, bf16[2,160,384]{2,1,0:T(8,128)(2,1)S(1)}, u32[]{:S(2)}, u32[]{:S(2)}) collective-permute-start(bf16[2,160,384]{2,1,0:T(8,128)(2,1)S(1)} %get-tuple-element.79), channel_id=1, source_target_pairs={{0,16},{2,18},{16,0},{18,2},{1,17},{3,19},{17,1},{19,3},{4,20},{6,... | collective-permute-start | bytes 737288 | tf_op jit(solution)/shard_map/ppermute | solution.py:394
  29.8 2.4 %collective-permute-start.13 = (bf16[4,160,128]{2,1,0:T(8,128)(2,1)S(1)}, bf16[4,160,128]{2,1,0:T(8,128)(2,1)S(1)}, u32[]{:S(2)}, u32[]{:S(2)}) collective-permute-start(bf16[4,160,128]{2,1,0:T(8,128)(2,1)S(1)} %get-tuple-element.87), channel_id=1, source_target_pairs={{0,1},{1,0},{2,3},{3,2},{4,5},{5,4},{6,7},{7,6},{8,9},{9,8},{10,11... | collective-permute-start | bytes 491528 | tf_op jit(solution)/shard_map/ppermute | solution.py:394
  29.9 2.3 %collective-permute-start.14 = (bf16[4,160,128]{2,1,0:T(8,128)(2,1)S(1)}, bf16[4,160,128]{2,1,0:T(8,128)(2,1)S(1)}, u32[]{:S(2)}, u32[]{:S(2)}) collective-permute-start(bf16[4,160,128]{2,1,0:T(8,128)(2,1)S(1)} %get-tuple-element.89), channel_id=1, source_target_pairs={{0,1},{1,0},{2,3},{3,2},{4,5},{5,4},{6,7},{7,6},{8,9},{9,8},{10,11... | collective-permute-start | bytes 491528 | tf_op jit(solution)/shard_map/ppermute | solution.py:394
  32.3 7.2 %collective-permute-start.15 = (bf16[752,128]{1,0:T(8,128)(2,1)S(1)}, bf16[752,128]{1,0:T(8,128)(2,1)S(1)}, u32[]{:S(2)}, u32[]{:S(2)}) collective-permute-start(bf16[752,128]{1,0:T(8,128)(2,1)S(1)} %pad_maximum_fusion.2), channel_id=1, source_target_pairs={{0,16},{2,18},{16,0},{18,2},{1,17},{3,19},{17,1},{19,3},{4,20},{6,... | collective-permute-start | bytes 577544 | tf_op jit(solution)/shard_map/ppermute | solution.py:394
  33.9 5.7 %collective-permute-start.16 = (bf16[688,128]{1,0:T(8,128)(2,1)S(1)}, bf16[688,128]{1,0:T(8,128)(2,1)S(1)}, u32[]{:S(2)}, u32[]{:S(2)}) collective-permute-start(bf16[688,128]{1,0:T(8,128)(2,1)S(1)} %pad_maximum_fusion.4), channel_id=1, source_target_pairs={{0,2},{2,0},{16,18},{18,16},{1,3},{3,1},{17,19},{19,17},{4,6},{6,4... | collective-permute-start | bytes 528392 | tf_op jit(solution)/shard_map/ppermute | solution.py:394
  39.8 7.2 %collective-permute-start.17 = (bf16[864,128]{1,0:T(8,128)(2,1)S(1)}, bf16[864,128]{1,0:T(8,128)(2,1)S(1)}, u32[]{:S(2)}, u32[]{:S(2)}) collective-permute-start(bf16[864,128]{1,0:T(8,128)(2,1)S(1)} %pad_maximum_fusion.1), channel_id=1, source_target_pairs={{0,2},{2,0},{16,18},{18,16},{1,3},{3,1},{17,19},{19,17},{4,6},{6,4... | collective-permute-start | bytes 663560 | tf_op jit(solution)/shard_map/ppermute | solution.py:394
  41.4 5.6 %collective-permute-start.18 = (bf16[736,128]{1,0:T(8,128)(2,1)S(1)}, bf16[736,128]{1,0:T(8,128)(2,1)S(1)}, u32[]{:S(2)}, u32[]{:S(2)}) collective-permute-start(bf16[736,128]{1,0:T(8,128)(2,1)S(1)} %pad_maximum_fusion.3), channel_id=1, source_target_pairs={{0,16},{2,18},{16,0},{18,2},{1,17},{3,19},{17,1},{19,3},{4,20},{6,... | collective-permute-start | bytes 565256 | tf_op jit(solution)/shard_map/ppermute | solution.py:394
  42.0 5.8 %collective-permute-start.19 = (bf16[2,160,384]{2,1,0:T(8,128)(2,1)S(1)}, bf16[2,160,384]{2,1,0:T(8,128)(2,1)S(1)}, u32[]{:S(2)}, u32[]{:S(2)}) collective-permute-start(bf16[2,160,384]{2,1,0:T(8,128)(2,1)S(1)} %get-tuple-element.58.refs_0_), channel_id=1, source_target_pairs={{0,1},{1,0},{2,3},{3,2},{4,5},{5,4},{6,7},{7,6},{8,9},{9,8},{10,11... | collective-permute-start | bytes 737288 | tf_op jit(solution)/shard_map/ppermute | solution.py:394
  42.0 5.9 %collective-permute-start.20 = (bf16[2,160,384]{2,1,0:T(8,128)(2,1)S(1)}, bf16[2,160,384]{2,1,0:T(8,128)(2,1)S(1)}, u32[]{:S(2)}, u32[]{:S(2)}) collective-permute-start(bf16[2,160,384]{2,1,0:T(8,128)(2,1)S(1)} %collective-permute-done.11.refs_1_), channel_id=1, source_target_pairs={{0,1},{1,0},{2,3},{3,2},{4,5},{5,4},{6,7},{7,6},{8,9},{9,8},{10,11... | collective-permute-start | bytes 737288 | tf_op jit(solution)/shard_map/ppermute | solution.py:394
  42.5 7.1 %collective-permute-start.21 = (bf16[2,160,384]{2,1,0:T(8,128)(2,1)S(1)}, bf16[2,160,384]{2,1,0:T(8,128)(2,1)S(1)}, u32[]{:S(2)}, u32[]{:S(2)}) collective-permute-start(bf16[2,160,384]{2,1,0:T(8,128)(2,1)S(1)} %collective-permute-done.12.refs_2_), channel_id=1, source_target_pairs={{0,1},{1,0},{2,3},{3,2},{4,5},{5,4},{6,7},{7,6},{8,9},{9,8},{10,11... | collective-permute-start | bytes 737288 | tf_op jit(solution)/shard_map/ppermute | solution.py:394
  47.0 2.6 %collective-permute-start.22 = (bf16[2,160,384]{2,1,0:T(8,128)(2,1)S(1)}, bf16[2,160,384]{2,1,0:T(8,128)(2,1)S(1)}, u32[]{:S(2)}, u32[]{:S(2)}) collective-permute-start(bf16[2,160,384]{2,1,0:T(8,128)(2,1)S(1)} %collective-permute-done.10.refs_3_), channel_id=1, source_target_pairs={{0,1},{1,0},{2,3},{3,2},{4,5},{5,4},{6,7},{7,6},{8,9},{9,8},{10,11... | collective-permute-start | bytes 737288 | tf_op jit(solution)/shard_map/ppermute | solution.py:394
  47.1 2.4 %collective-permute-start.25 = (bf16[4,160,128]{2,1,0:T(8,128)(2,1)S(1)}, bf16[4,160,128]{2,1,0:T(8,128)(2,1)S(1)}, u32[]{:S(2)}, u32[]{:S(2)}) collective-permute-start(bf16[4,160,128]{2,1,0:T(8,128)(2,1)S(1)} %fusion.refs_6_), channel_id=1, source_target_pairs={{0,1},{1,0},{2,3},{3,2},{4,5},{5,4},{6,7},{7,6},{8,9},{9,8},{10,11... | collective-permute-start | bytes 491528 | tf_op jit(solution)/shard_map/ppermute | solution.py:394
  47.8 1.8 %collective-permute-start.24 = (bf16[4,160,128]{2,1,0:T(8,128)(2,1)S(1)}, bf16[4,160,128]{2,1,0:T(8,128)(2,1)S(1)}, u32[]{:S(2)}, u32[]{:S(2)}) collective-permute-start(bf16[4,160,128]{2,1,0:T(8,128)(2,1)S(1)} %fusion.1.refs_5_), channel_id=1, source_target_pairs={{0,1},{1,0},{2,3},{3,2},{4,5},{5,4},{6,7},{7,6},{8,9},{9,8},{10,11... | collective-permute-start | bytes 491528 | tf_op jit(solution)/shard_map/ppermute | solution.py:394
  47.9 1.7 %collective-permute-start.23 = (bf16[640,128]{1,0:T(8,128)(2,1)S(1)}, bf16[640,128]{1,0:T(8,128)(2,1)S(1)}, u32[]{:S(2)}, u32[]{:S(2)}) collective-permute-start(bf16[640,128]{1,0:T(8,128)(2,1)S(1)} %slice_dynamic-update-slice_fusion.2.refs_4_), channel_id=1, source_target_pairs={{0,1},{1,0},{2,3},{3,2},{4,5},{5,4},{6,7},{7,6},{8,9},{9,8},{10,11... | collective-permute-start | bytes 491528 | tf_op jit(solution)/shard_map/ppermute | solution.py:394
  50.2 5.5 %collective-permute-start.26 = (bf16[96,384]{1,0:T(8,128)(2,1)S(1)}, bf16[96,384]{1,0:T(8,128)(2,1)S(1)}, u32[]{:S(2)}, u32[]{:S(2)}) collective-permute-start(bf16[96,384]{1,0:T(8,128)(2,1)S(1)} %get-tuple-element.103), channel_id=1, source_target_pairs={{0,4},{4,0},{8,12},{12,8},{1,5},{5,1},{9,13},{13,9},{2,6},{6,2},{1... | collective-permute-start | bytes 221192 | tf_op jit(solution)/shard_map/ppermute | solution.py:394
  50.3 9.2 %collective-permute-start.27 = (bf16[96,384]{1,0:T(8,128)(2,1)S(1)}, bf16[96,384]{1,0:T(8,128)(2,1)S(1)}, u32[]{:S(2)}, u32[]{:S(2)}) collective-permute-start(bf16[96,384]{1,0:T(8,128)(2,1)S(1)} %get-tuple-element.104), channel_id=1, source_target_pairs={{0,8},{4,12},{8,0},{12,4},{1,9},{5,13},{9,1},{13,5},{2,10},{6,14},... | collective-permute-start | bytes 221192 | tf_op jit(solution)/shard_map/ppermute | solution.py:394
  52.2 7.3 %collective-permute-start.28 = (bf16[96,384]{1,0:T(8,128)(2,1)S(1)}, bf16[96,384]{1,0:T(8,128)(2,1)S(1)}, u32[]{:S(2)}, u32[]{:S(2)}) collective-permute-start(bf16[96,384]{1,0:T(8,128)(2,1)S(1)} %get-tuple-element.105), channel_id=1, source_target_pairs={{0,12},{4,8},{8,4},{12,0},{1,13},{5,9},{9,5},{13,1},{2,14},{6,10},... | collective-permute-start | bytes 221192 | tf_op jit(solution)/shard_map/ppermute | solution.py:394
  59.6 4.4 %collective-permute-start.29 = (bf16[96,384]{1,0:T(8,128)(2,1)S(1)}, bf16[96,384]{1,0:T(8,128)(2,1)S(1)}, u32[]{:S(2)}, u32[]{:S(2)}) collective-permute-start(bf16[96,384]{1,0:T(8,128)(2,1)S(1)} %get-tuple-element.106), channel_id=1, source_target_pairs={{0,16},{16,0},{1,17},{17,1},{2,18},{18,2},{3,19},{19,3},{4,20},{20... | collective-permute-start | bytes 221192 | tf_op jit(solution)/shard_map/ppermute | solution.py:394

commit v5 on v4

--- a/solution.py
+++ b/solution.py
@@ -22,7 +22,7 @@
 
 
 def cut_rows(count):
-    return count * 3 // (4 * PAD_ROWS) * PAD_ROWS
+    return count * 9 // (10 * PAD_ROWS) * PAD_ROWS
 
 
 def plane_places(plane, n_y):

time: 64.9 us -> 64.5 us (level)
  waiting for transfers between devices: 22.4 us -> 21.6 us
    ppermute x30, waiting for transfers between devices: 22.4 us -> 21.6 us  [xor_permute(): return lax.ppermute(value, tuple(names), pairs)]
where the time goes in v5:
time: 64.5 us; the launch traced here: 64.4 us
  starting transfers between devices  31.4 us (49%)
  waiting for transfers between devices  21.6 us (33%)
  Pallas kernels  8 us (12%)
  local copies, waits for them, and re-layouts  1.37 us (2%)
  other arithmetic  1.14 us (2%)
  between operations  0.93 us (1%)
    ppermute x30, starting transfers between devices, xor_permute(): return lax.ppermute(value, tuple(names), pairs)  31.4 us
    ppermute x30, waiting for transfers between devices, xor_permute(): return lax.ppermute(value, tuple(names), pairs)  21.6 us
    pallas_call x1, Pallas kernels, local(): pl.pallas_call(functools.partial(forward_kernel, count, width, n_z, len(k...  2.26 us
    pallas_call x1, Pallas kernels, local(): pl.pallas_call(functools.partial(pack_kernel, axes), out_shape=(packed, p...  1.41 us
  transfers between devices with their start and end apart: 30, of which 9 were waited for; matrix products, arithmetic and copies ran while one was open for 3% of the time, Pallas kernels for 8%

profile of v5, /device:TPU:0, one launch (start us, length us, event | category | flops | bytes accessed | tf_op | source)
XLA Modules:
  0.0 64.4 jit_solution(4669950157941707265)
XLA Ops:
  0.6 1.4 %pack.1 = (bf16[176,256]{1,0:T(8,128)(2,1)S(1)}, bf16[176,256]{1,0:T(8,128)(2,1)S(1)}, bf16[160,3072]{1,0:T(8,128)(2,1)S(1)}) custom-call(bf16[160,128]{1,0:T(8,128)(2,1)} %q_hbm.1, bf16[160,128]{1,0:T(8,128)(2,1)} %k_hbm.1, bf16[160,128]{1,0:T(8,128)(2,1)} %v_hbm.1, bf16[160,128]{1,0:T(8,128)(2,1)} %o_hbm.1, bf16[160,128]{1,0:T(8,128)(2,1)} %g_hbm.1, ...), custom_call_target="tpu_custom_call" | custom-call | tf_op jit(solution)/shard_map/pack/pallas_call | solution.py:418
  2.1 3.0 %collective-permute-start = (bf16[176,256]{1,0:T(8,128)(2,1)S(1)}, bf16[176,256]{1,0:T(8,128)(2,1)S(1)}, u32[]{:S(2)}, u32[]{:S(2)}) collective-permute-start(bf16[176,256]{1,0:T(8,128)(2,1)S(1)} %get-tuple-element.56), channel_id=1, source_target_pairs={{0,2},{2,0},{16,18},{18,16},{1,3},{3,1},{17,19},{19,17},{4,6},{6,4... | collective-permute-start | bytes 270344 | tf_op jit(solution)/shard_map/ppermute | solution.py:394
  5.1 1.5 %collective-permute-start.4 = (bf16[176,256]{1,0:T(8,128)(2,1)S(1)}, bf16[176,256]{1,0:T(8,128)(2,1)S(1)}, u32[]{:S(2)}, u32[]{:S(2)}) collective-permute-start(bf16[176,256]{1,0:T(8,128)(2,1)S(1)} %get-tuple-element.56), channel_id=1, source_target_pairs={{0,16},{2,18},{16,0},{18,2},{1,17},{3,19},{17,1},{19,3},{4,20},{6,... | collective-permute-start | bytes 270344 | tf_op jit(solution)/shard_map/ppermute | solution.py:394
  6.6 4.0 %collective-permute-start.1 = (bf16[176,256]{1,0:T(8,128)(2,1)S(1)}, bf16[176,256]{1,0:T(8,128)(2,1)S(1)}, u32[]{:S(2)}, u32[]{:S(2)}) collective-permute-start(bf16[176,256]{1,0:T(8,128)(2,1)S(1)} %get-tuple-element.59.refs_3_), channel_id=1, source_target_pairs={{0,12},{4,8},{8,4},{12,0},{1,13},{5,9},{9,5},{13,1},{2,14},{6,10},... | collective-permute-start | bytes 270344 | tf_op jit(solution)/shard_map/ppermute | solution.py:394
  10.7 0.6 collective-permute-start.3
  11.2 0.8 %collective-permute-done.5 = bf16[176,256]{1,0:T(8,128)(2,1)S(1)} collective-permute-done((bf16[176,256]{1,0:T(8,128)(2,1)S(1)}, bf16[176,256]{1,0:T(8,128)(2,1)S(1)}, u32[]{:S(2)}, u32[]{:S(2)}) %collective-permute-start.5) | collective-permute-done | bytes 90144 | tf_op jit(solution)/shard_map/ppermute | solution.py:394
  12.1 0.1 collective-permute-start.6
  12.1 0.7 %deal.1 = (bf16[2,160,384]{2,1,0:T(8,128)(2,1)S(1)}, bf16[2,160,384]{2,1,0:T(8,128)(2,1)S(1)}, bf16[2,160,384]{2,1,0:T(8,128)(2,1)S(1)}, bf16[2,160,384]{2,1,0:T(8,128)(2,1)S(1)}) custom-call(bf16[160,3072]{1,0:T(8,128)(2,1)S(1)} %get-tuple-element.57.x_ref), custom_call_target="tpu_custom_call" | custom-call | tf_op jit(solution)/shard_map/deal/pallas_call | solution.py:453
  12.8 2.0 %collective-permute-start.10 = (bf16[2,160,384]{2,1,0:T(8,128)(2,1)S(1)}, bf16[2,160,384]{2,1,0:T(8,128)(2,1)S(1)}, u32[]{:S(2)}, u32[]{:S(2)}) collective-permute-start(bf16[2,160,384]{2,1,0:T(8,128)(2,1)S(1)} %get-tuple-element.70), channel_id=1, source_target_pairs={{0,18},{2,16},{16,2},{18,0},{1,19},{3,17},{17,3},{19,1},{4,22},{6,... | collective-permute-start | bytes 737288 | tf_op jit(solution)/shard_map/ppermute | solution.py:394
  14.8 2.6 %collective-permute-done.2.refs_1_ = bf16[176,256]{1,0:T(8,128)(2,1)S(1)} collective-permute-done((bf16[176,256]{1,0:T(8,128)(2,1)S(1)}, bf16[176,256]{1,0:T(8,128)(2,1)S(1)}, u32[]{:S(2)}, u32[]{:S(2)}) %collective-permute-start.2) | collective-permute-done | bytes 90144 | tf_op jit(solution)/shard_map/ppermute | solution.py:394
  17.4 0.1 lines.1
  17.6 2.3 %forward.1 = (bf16[8,160,640]{2,1,0:T(8,128)(2,1)S(1)}, bf16[8,160,640]{2,1,0:T(8,128)(2,1)S(1)}, f32[8,640]{1,0:T(8,128)S(1)}, bf16[160,128]{1,0:T(8,128)(2,1)S...) custom-call(bf16[640,128]{1,0:T(8,128)(2,1)S(1)} %get-tuple-element.60.refs_0_.refs_3_, ...), custom_call_target="tpu_custom_call" | custom-call | flops 30000001024 | tf_op jit(solution)/shard_map/forward/pallas_call | solution.py:478
  19.8 0.7 %collective-permute-start.7 = (bf16[192,128]{1,0:T(8,128)(2,1)S(1)}, bf16[192,128]{1,0:T(8,128)(2,1)S(1)}, u32[]{:S(2)}, u32[]{:S(2)}) collective-permute-start(bf16[192,128]{1,0:T(8,128)(2,1)S(1)} %get-tuple-element.67), channel_id=1, source_target_pairs={{0,4},{4,0},{8,12},{12,8},{1,5},{5,1},{9,13},{13,9},{2,6},{6,2},{1... | collective-permute-start | bytes 147464 | tf_op jit(solution)/shard_map/ppermute | solution.py:394
  20.6 2.4 %collective-permute-start.8 = (bf16[192,128]{1,0:T(8,128)(2,1)S(1)}, bf16[192,128]{1,0:T(8,128)(2,1)S(1)}, u32[]{:S(2)}, u32[]{:S(2)}) collective-permute-start(bf16[192,128]{1,0:T(8,128)(2,1)S(1)} %get-tuple-element.68), channel_id=1, source_target_pairs={{0,8},{4,12},{8,0},{12,4},{1,9},{5,13},{9,1},{13,5},{2,10},{6,14},... | collective-permute-start | bytes 147464 | tf_op jit(solution)/shard_map/ppermute | solution.py:394
  23.0 1.3 %collective-permute-start.9 = (bf16[192,128]{1,0:T(8,128)(2,1)S(1)}, bf16[192,128]{1,0:T(8,128)(2,1)S(1)}, u32[]{:S(2)}, u32[]{:S(2)}) collective-permute-start(bf16[192,128]{1,0:T(8,128)(2,1)S(1)} %get-tuple-element.69), channel_id=1, source_target_pairs={{0,12},{4,8},{8,4},{12,0},{1,13},{5,9},{9,5},{13,1},{2,14},{6,10},... | collective-permute-start | bytes 147464 | tf_op jit(solution)/shard_map/ppermute | solution.py:394
  24.3 1.5 %collective-permute-start.11 = (bf16[2,160,384]{2,1,0:T(8,128)(2,1)S(1)}, bf16[2,160,384]{2,1,0:T(8,128)(2,1)S(1)}, u32[]{:S(2)}, u32[]{:S(2)}) collective-permute-start(bf16[2,160,384]{2,1,0:T(8,128)(2,1)S(1)} %get-tuple-element.78), channel_id=1, source_target_pairs={{0,2},{2,0},{16,18},{18,16},{1,3},{3,1},{17,19},{19,17},{4,6},{6,4... | collective-permute-start | bytes 737288 | tf_op jit(solution)/shard_map/ppermute | solution.py:394
  25.8 1.5 %collective-permute-start.12 = (bf16[2,160,384]{2,1,0:T(8,128)(2,1)S(1)}, bf16[2,160,384]{2,1,0:T(8,128)(2,1)S(1)}, u32[]{:S(2)}, u32[]{:S(2)}) collective-permute-start(bf16[2,160,384]{2,1,0:T(8,128)(2,1)S(1)} %get-tuple-element.79), channel_id=1, source_target_pairs={{0,16},{2,18},{16,0},{18,2},{1,17},{3,19},{17,1},{19,3},{4,20},{6,... | collective-permute-start | bytes 737288 | tf_op jit(solution)/shard_map/ppermute | solution.py:394
  27.3 1.5 %collective-permute-done.9.refs_5_.refs_2_ = bf16[192,128]{1,0:T(8,128)(2,1)S(1)} collective-permute-done((bf16[192,128]{1,0:T(8,128)(2,1)S(1)}, bf16[192,128]{1,0:T(8,128)(2,1)S(1)}, u32[]{:S(2)}, u32[]{:S(2)}) %collective-permute-start.9) | collective-permute-done | bytes 49184 | tf_op jit(solution)/shard_map/ppermute | solution.py:394
  28.9 0.9 %away.1 = (bf16[4,160,128]{2,1,0:T(8,128)(2,1)S(1)}, bf16[4,160,128]{2,1,0:T(8,128)(2,1)S(1)}, bf16[640,128]{1,0:T(8,128)(2,1)S(1)}, bf16[640,128]{1,0:T(8,128)(2,1)S(1)}, f32[640,8]{1,0:T(8,128)S(1)}) custom-call(bf16[8,160,640]{2,1,0:T(8,128)(2,1)S(1)} %get-tuple-element.64.refs_0_.w_ref, bf16[8,160,640]{2,1,0:T(8,128)(2,1)S(1)} %get-tuple-element.65.refs_1_.u_ref, ...), custom_call_target="tpu_custom_call" | custom-call | flops 30000001024 | tf_op jit(solution)/shard_map/away/pallas_call | solution.py:516
  29.9 0.5 collective-permute-start.14
  30.4 0.6 home.1
  31.0 1.0 %collective-permute-done.12.refs_2_ = bf16[2,160,384]{2,1,0:T(8,128)(2,1)S(1)} collective-permute-done((bf16[2,160,384]{2,1,0:T(8,128)(2,1)S(1)}, bf16[2,160,384]{2,1,0:T(8,128)(2,1)S(1)}, u32[]{:S(2)}, u32[]{:S(2)}) %collective-permute-start.12) | collective-permute-done | bytes 245792 | tf_op jit(solution)/shard_map/ppermute | solution.py:394
  32.0 0.2 query.1
  32.3 1.6 %collective-permute-start.15 = (bf16[784,128]{1,0:T(8,128)(2,1)S(1)}, bf16[784,128]{1,0:T(8,128)(2,1)S(1)}, u32[]{:S(2)}, u32[]{:S(2)}) collective-permute-start(bf16[784,128]{1,0:T(8,128)(2,1)S(1)} %pad_maximum_fusion.2), channel_id=1, source_target_pairs={{0,16},{2,18},{16,0},{18,2},{1,17},{3,19},{17,1},{19,3},{4,20},{6,... | collective-permute-start | bytes 602120 | tf_op jit(solution)/shard_map/ppermute | solution.py:394
  33.9 0.8 %collective-permute-start.16 = (bf16[656,128]{1,0:T(8,128)(2,1)S(1)}, bf16[656,128]{1,0:T(8,128)(2,1)S(1)}, u32[]{:S(2)}, u32[]{:S(2)}) collective-permute-start(bf16[656,128]{1,0:T(8,128)(2,1)S(1)} %pad_maximum_fusion.4), channel_id=1, source_target_pairs={{0,2},{2,0},{16,18},{18,16},{1,3},{3,1},{17,19},{19,17},{4,6},{6,4... | collective-permute-start | bytes 503816 | tf_op jit(solution)/shard_map/ppermute | solution.py:394
  34.7 4.7 %collective-permute-done.16 = bf16[656,128]{1,0:T(8,128)(2,1)S(1)} collective-permute-done((bf16[656,128]{1,0:T(8,128)(2,1)S(1)}, bf16[656,128]{1,0:T(8,128)(2,1)S(1)}, u32[]{:S(2)}, u32[]{:S(2)}) %collective-permute-start.16) | collective-permute-done | bytes 167968 | tf_op jit(solution)/shard_map/ppermute | solution.py:394
  39.6 1.6 %collective-permute-start.17 = (bf16[928,128]{1,0:T(8,128)(2,1)S(1)}, bf16[928,128]{1,0:T(8,128)(2,1)S(1)}, u32[]{:S(2)}, u32[]{:S(2)}) collective-permute-start(bf16[928,128]{1,0:T(8,128)(2,1)S(1)} %pad_maximum_fusion.1), channel_id=1, source_target_pairs={{0,2},{2,0},{16,18},{18,16},{1,3},{3,1},{17,19},{19,17},{4,6},{6,4... | collective-permute-start | bytes 712712 | tf_op jit(solution)/shard_map/ppermute | solution.py:394
  41.2 1.0 %collective-permute-start.18 = (bf16[672,128]{1,0:T(8,128)(2,1)S(1)}, bf16[672,128]{1,0:T(8,128)(2,1)S(1)}, u32[]{:S(2)}, u32[]{:S(2)}) collective-permute-start(bf16[672,128]{1,0:T(8,128)(2,1)S(1)} %pad_maximum_fusion.3), channel_id=1, source_target_pairs={{0,16},{2,18},{16,0},{18,2},{1,17},{3,19},{17,1},{19,3},{4,20},{6,... | collective-permute-start | bytes 516104 | tf_op jit(solution)/shard_map/ppermute | solution.py:394
  42.2 0.5 collective-permute-start.20
  42.7 3.9 %collective-permute-done.18 = bf16[672,128]{1,0:T(8,128)(2,1)S(1)} collective-permute-done((bf16[672,128]{1,0:T(8,128)(2,1)S(1)}, bf16[672,128]{1,0:T(8,128)(2,1)S(1)}, u32[]{:S(2)}, u32[]{:S(2)}) %collective-permute-start.18) | collective-permute-done | bytes 172064 | tf_op jit(solution)/shard_map/ppermute | solution.py:394
  46.7 0.1 fusion.refs_6_
  46.8 0.6 collective-permute-start.25
  47.4 0.1 fusion.1.refs_5_
  47.5 0.1 collective-permute-start.24
  47.6 0.5 collective-permute-start.23
  48.1 0.5 near.1.near_ref
  48.6 0.6 dynamic-slice_bitcast_fusion
  49.3 0.6 far.1
  49.8 0.1 collective-permute-start.26
  49.9 1.9 %collective-permute-start.27 = (bf16[96,384]{1,0:T(8,128)(2,1)S(1)}, bf16[96,384]{1,0:T(8,128)(2,1)S(1)}, u32[]{:S(2)}, u32[]{:S(2)}) collective-permute-start(bf16[96,384]{1,0:T(8,128)(2,1)S(1)} %get-tuple-element.104), channel_id=1, source_target_pairs={{0,8},{4,12},{8,0},{12,4},{1,9},{5,13},{9,1},{13,5},{2,10},{6,14},... | collective-permute-start | bytes 221192 | tf_op jit(solution)/shard_map/ppermute | solution.py:394
  51.8 2.5 %collective-permute-start.28 = (bf16[96,384]{1,0:T(8,128)(2,1)S(1)}, bf16[96,384]{1,0:T(8,128)(2,1)S(1)}, u32[]{:S(2)}, u32[]{:S(2)}) collective-permute-start(bf16[96,384]{1,0:T(8,128)(2,1)S(1)} %get-tuple-element.105), channel_id=1, source_target_pairs={{0,12},{4,8},{8,4},{12,0},{1,13},{5,9},{9,5},{13,1},{2,14},{6,10},... | collective-permute-start | bytes 221192 | tf_op jit(solution)/shard_map/ppermute | solution.py:394
  54.3 0.6 dynamic-slice_bitcast_fusion.1
  54.9 0.4 collective-permute-done.26
  55.3 3.8 %collective-permute-done.27 = bf16[96,384]{1,0:T(8,128)(2,1)S(1)} collective-permute-done((bf16[96,384]{1,0:T(8,128)(2,1)S(1)}, bf16[96,384]{1,0:T(8,128)(2,1)S(1)}, u32[]{:S(2)}, u32[]{:S(2)}) %collective-permute-start.27) | collective-permute-done | bytes 73760 | tf_op jit(solution)/shard_map/ppermute | solution.py:394
  59.2 1.1 %collective-permute-start.29 = (bf16[96,384]{1,0:T(8,128)(2,1)S(1)}, bf16[96,384]{1,0:T(8,128)(2,1)S(1)}, u32[]{:S(2)}, u32[]{:S(2)}) collective-permute-start(bf16[96,384]{1,0:T(8,128)(2,1)S(1)} %get-tuple-element.106), channel_id=1, source_target_pairs={{0,16},{16,0},{1,17},{17,1},{2,18},{18,2},{3,19},{19,3},{4,20},{20... | collective-permute-start | bytes 221192 | tf_op jit(solution)/shard_map/ppermute | solution.py:394
  60.3 0.6 pad_maximum_fusion.5
  60.9 2.7 %collective-permute-done.29.refs_0_ = bf16[96,384]{1,0:T(8,128)(2,1)S(1)} collective-permute-done((bf16[96,384]{1,0:T(8,128)(2,1)S(1)}, bf16[96,384]{1,0:T(8,128)(2,1)S(1)}, u32[]{:S(2)}, u32[]{:S(2)}) %collective-permute-start.29) | collective-permute-done | bytes 73760 | tf_op jit(solution)/shard_map/ppermute | solution.py:394
  63.6 0.7 %assemble.1 = f32[2,96,384]{2,1,0:T(8,128)} custom-call(f32[96,384]{1,0:T(8,128)S(1)} %get-tuple-element.107.own_ref, bf16[96,384]{1,0:T(8,128)(2,1)S(1)} %collective-permute-done.29.refs_0_), custom_call_target="tpu_custom_call" | custom-call | tf_op jit(solution)/shard_map/assemble/pallas_call | solution.py:608
  (49 shorter events, 0.7 us)
Async XLA Ops:
  2.1 8.6 %collective-permute-start = (bf16[176,256]{1,0:T(8,128)(2,1)S(1)}, bf16[176,256]{1,0:T(8,128)(2,1)S(1)}, u32[]{:S(2)}, u32[]{:S(2)}) collective-permute-start(bf16[176,256]{1,0:T(8,128)(2,1)S(1)} %get-tuple-element.56), channel_id=1, source_target_pairs={{0,2},{2,0},{16,18},{18,16},{1,3},{3,1},{17,19},{19,17},{4,6},{6,4... | collective-permute-start | bytes 270344 | tf_op jit(solution)/shard_map/ppermute | solution.py:394
  5.1 6.1 %collective-permute-start.4 = (bf16[176,256]{1,0:T(8,128)(2,1)S(1)}, bf16[176,256]{1,0:T(8,128)(2,1)S(1)}, u32[]{:S(2)}, u32[]{:S(2)}) collective-permute-start(bf16[176,256]{1,0:T(8,128)(2,1)S(1)} %get-tuple-element.56), channel_id=1, source_target_pairs={{0,16},{2,18},{16,0},{18,2},{1,17},{3,19},{17,1},{19,3},{4,20},{6,... | collective-permute-start | bytes 270344 | tf_op jit(solution)/shard_map/ppermute | solution.py:394
  6.6 5.4 %collective-permute-start.5 = (bf16[176,256]{1,0:T(8,128)(2,1)S(1)}, bf16[176,256]{1,0:T(8,128)(2,1)S(1)}, u32[]{:S(2)}, u32[]{:S(2)}) collective-permute-start(bf16[176,256]{1,0:T(8,128)(2,1)S(1)} %get-tuple-element.56), channel_id=1, source_target_pairs={{0,18},{2,16},{16,2},{18,0},{1,19},{3,17},{17,3},{19,1},{4,22},{6,... | collective-permute-start | bytes 270344 | tf_op jit(solution)/shard_map/ppermute | solution.py:394
  6.6 8.2 %collective-permute-start.1 = (bf16[176,256]{1,0:T(8,128)(2,1)S(1)}, bf16[176,256]{1,0:T(8,128)(2,1)S(1)}, u32[]{:S(2)}, u32[]{:S(2)}) collective-permute-start(bf16[176,256]{1,0:T(8,128)(2,1)S(1)} %get-tuple-element.59.refs_3_), channel_id=1, source_target_pairs={{0,12},{4,8},{8,4},{12,0},{1,13},{5,9},{9,5},{13,1},{2,14},{6,10},... | collective-permute-start | bytes 270344 | tf_op jit(solution)/shard_map/ppermute | solution.py:394
  10.7 6.8 %collective-permute-start.2 = (bf16[176,256]{1,0:T(8,128)(2,1)S(1)}, bf16[176,256]{1,0:T(8,128)(2,1)S(1)}, u32[]{:S(2)}, u32[]{:S(2)}) collective-permute-start(bf16[176,256]{1,0:T(8,128)(2,1)S(1)} %get-tuple-element.59.refs_3_), channel_id=1, source_target_pairs={{0,8},{4,12},{8,0},{12,4},{1,9},{5,13},{9,1},{13,5},{2,10},{6,14},... | collective-permute-start | bytes 270344 | tf_op jit(solution)/shard_map/ppermute | solution.py:394
  10.7 6.8 %collective-permute-start.3 = (bf16[176,256]{1,0:T(8,128)(2,1)S(1)}, bf16[176,256]{1,0:T(8,128)(2,1)S(1)}, u32[]{:S(2)}, u32[]{:S(2)}) collective-permute-start(bf16[176,256]{1,0:T(8,128)(2,1)S(1)} %get-tuple-element.59.refs_3_), channel_id=1, source_target_pairs={{0,4},{4,0},{8,12},{12,8},{1,5},{5,1},{9,13},{13,9},{2,6},{6,2},{1... | collective-permute-start | bytes 270344 | tf_op jit(solution)/shard_map/ppermute | solution.py:394
  12.1 5.5 %collective-permute-start.6 = (bf16[4,176,256]{2,1,0:T(8,128)(2,1)S(1)}, bf16[4,176,256]{2,1,0:T(8,128)(2,1)S(1)}, u32[]{:S(2)}, u32[]{:S(2)}) collective-permute-start(bf16[4,176,256]{2,1,0:T(8,128)(2,1)S(1)} %pad_maximum_fusion), channel_id=1, source_target_pairs={{0,1},{1,0},{2,3},{3,2},{4,5},{5,4},{6,7},{7,6},{8,9},{9,8},{10,11... | collective-permute-start | bytes 1081352 | tf_op jit(solution)/shard_map/ppermute | solution.py:394
  12.8 13.0 %collective-permute-start.10 = (bf16[2,160,384]{2,1,0:T(8,128)(2,1)S(1)}, bf16[2,160,384]{2,1,0:T(8,128)(2,1)S(1)}, u32[]{:S(2)}, u32[]{:S(2)}) collective-permute-start(bf16[2,160,384]{2,1,0:T(8,128)(2,1)S(1)} %get-tuple-element.70), channel_id=1, source_target_pairs={{0,18},{2,16},{16,2},{18,0},{1,19},{3,17},{17,3},{19,1},{4,22},{6,... | collective-permute-start | bytes 737288 | tf_op jit(solution)/shard_map/ppermute | solution.py:394
  19.8 7.5 %collective-permute-start.7 = (bf16[192,128]{1,0:T(8,128)(2,1)S(1)}, bf16[192,128]{1,0:T(8,128)(2,1)S(1)}, u32[]{:S(2)}, u32[]{:S(2)}) collective-permute-start(bf16[192,128]{1,0:T(8,128)(2,1)S(1)} %get-tuple-element.67), channel_id=1, source_target_pairs={{0,4},{4,0},{8,12},{12,8},{1,5},{5,1},{9,13},{13,9},{2,6},{6,2},{1... | collective-permute-start | bytes 147464 | tf_op jit(solution)/shard_map/ppermute | solution.py:394
  20.6 6.8 %collective-permute-start.8 = (bf16[192,128]{1,0:T(8,128)(2,1)S(1)}, bf16[192,128]{1,0:T(8,128)(2,1)S(1)}, u32[]{:S(2)}, u32[]{:S(2)}) collective-permute-start(bf16[192,128]{1,0:T(8,128)(2,1)S(1)} %get-tuple-element.68), channel_id=1, source_target_pairs={{0,8},{4,12},{8,0},{12,4},{1,9},{5,13},{9,1},{13,5},{2,10},{6,14},... | collective-permute-start | bytes 147464 | tf_op jit(solution)/shard_map/ppermute | solution.py:394
  23.0 5.9 %collective-permute-start.9 = (bf16[192,128]{1,0:T(8,128)(2,1)S(1)}, bf16[192,128]{1,0:T(8,128)(2,1)S(1)}, u32[]{:S(2)}, u32[]{:S(2)}) collective-permute-start(bf16[192,128]{1,0:T(8,128)(2,1)S(1)} %get-tuple-element.69), channel_id=1, source_target_pairs={{0,12},{4,8},{8,4},{12,0},{1,13},{5,9},{9,5},{13,1},{2,14},{6,10},... | collective-permute-start | bytes 147464 | tf_op jit(solution)/shard_map/ppermute | solution.py:394
  24.3 6.7 %collective-permute-start.11 = (bf16[2,160,384]{2,1,0:T(8,128)(2,1)S(1)}, bf16[2,160,384]{2,1,0:T(8,128)(2,1)S(1)}, u32[]{:S(2)}, u32[]{:S(2)}) collective-permute-start(bf16[2,160,384]{2,1,0:T(8,128)(2,1)S(1)} %get-tuple-element.78), channel_id=1, source_target_pairs={{0,2},{2,0},{16,18},{18,16},{1,3},{3,1},{17,19},{19,17},{4,6},{6,4... | collective-permute-start | bytes 737288 | tf_op jit(solution)/shard_map/ppermute | solution.py:394
  25.8 6.2 %collective-permute-start.12 = (bf16[2,160,384]{2,1,0:T(8,128)(2,1)S(1)}, bf16[2,160,384]{2,1,0:T(8,128)(2,1)S(1)}, u32[]{:S(2)}, u32[]{:S(2)}) collective-permute-start(bf16[2,160,384]{2,1,0:T(8,128)(2,1)S(1)} %get-tuple-element.79), channel_id=1, source_target_pairs={{0,16},{2,18},{16,0},{18,2},{1,17},{3,19},{17,1},{19,3},{4,20},{6,... | collective-permute-start | bytes 737288 | tf_op jit(solution)/shard_map/ppermute | solution.py:394
  29.8 2.4 %collective-permute-start.13 = (bf16[4,160,128]{2,1,0:T(8,128)(2,1)S(1)}, bf16[4,160,128]{2,1,0:T(8,128)(2,1)S(1)}, u32[]{:S(2)}, u32[]{:S(2)}) collective-permute-start(bf16[4,160,128]{2,1,0:T(8,128)(2,1)S(1)} %get-tuple-element.87), channel_id=1, source_target_pairs={{0,1},{1,0},{2,3},{3,2},{4,5},{5,4},{6,7},{7,6},{8,9},{9,8},{10,11... | collective-permute-start | bytes 491528 | tf_op jit(solution)/shard_map/ppermute | solution.py:394
  29.9 2.3 %collective-permute-start.14 = (bf16[4,160,128]{2,1,0:T(8,128)(2,1)S(1)}, bf16[4,160,128]{2,1,0:T(8,128)(2,1)S(1)}, u32[]{:S(2)}, u32[]{:S(2)}) collective-permute-start(bf16[4,160,128]{2,1,0:T(8,128)(2,1)S(1)} %get-tuple-element.89), channel_id=1, source_target_pairs={{0,1},{1,0},{2,3},{3,2},{4,5},{5,4},{6,7},{7,6},{8,9},{9,8},{10,11... | collective-permute-start | bytes 491528 | tf_op jit(solution)/shard_map/ppermute | solution.py:394
  32.3 7.0 %collective-permute-start.15 = (bf16[784,128]{1,0:T(8,128)(2,1)S(1)}, bf16[784,128]{1,0:T(8,128)(2,1)S(1)}, u32[]{:S(2)}, u32[]{:S(2)}) collective-permute-start(bf16[784,128]{1,0:T(8,128)(2,1)S(1)} %pad_maximum_fusion.2), channel_id=1, source_target_pairs={{0,16},{2,18},{16,0},{18,2},{1,17},{3,19},{17,1},{19,3},{4,20},{6,... | collective-permute-start | bytes 602120 | tf_op jit(solution)/shard_map/ppermute | solution.py:394
  33.9 5.5 %collective-permute-start.16 = (bf16[656,128]{1,0:T(8,128)(2,1)S(1)}, bf16[656,128]{1,0:T(8,128)(2,1)S(1)}, u32[]{:S(2)}, u32[]{:S(2)}) collective-permute-start(bf16[656,128]{1,0:T(8,128)(2,1)S(1)} %pad_maximum_fusion.4), channel_id=1, source_target_pairs={{0,2},{2,0},{16,18},{18,16},{1,3},{3,1},{17,19},{19,17},{4,6},{6,4... | collective-permute-start | bytes 503816 | tf_op jit(solution)/shard_map/ppermute | solution.py:394
  39.6 7.0 %collective-permute-start.17 = (bf16[928,128]{1,0:T(8,128)(2,1)S(1)}, bf16[928,128]{1,0:T(8,128)(2,1)S(1)}, u32[]{:S(2)}, u32[]{:S(2)}) collective-permute-start(bf16[928,128]{1,0:T(8,128)(2,1)S(1)} %pad_maximum_fusion.1), channel_id=1, source_target_pairs={{0,2},{2,0},{16,18},{18,16},{1,3},{3,1},{17,19},{19,17},{4,6},{6,4... | collective-permute-start | bytes 712712 | tf_op jit(solution)/shard_map/ppermute | solution.py:394
  41.2 5.4 %collective-permute-start.18 = (bf16[672,128]{1,0:T(8,128)(2,1)S(1)}, bf16[672,128]{1,0:T(8,128)(2,1)S(1)}, u32[]{:S(2)}, u32[]{:S(2)}) collective-permute-start(bf16[672,128]{1,0:T(8,128)(2,1)S(1)} %pad_maximum_fusion.3), channel_id=1, source_target_pairs={{0,16},{2,18},{16,0},{18,2},{1,17},{3,19},{17,1},{19,3},{4,20},{6,... | collective-permute-start | bytes 516104 | tf_op jit(solution)/shard_map/ppermute | solution.py:394
  42.2 5.3 %collective-permute-start.19 = (bf16[2,160,384]{2,1,0:T(8,128)(2,1)S(1)}, bf16[2,160,384]{2,1,0:T(8,128)(2,1)S(1)}, u32[]{:S(2)}, u32[]{:S(2)}) collective-permute-start(bf16[2,160,384]{2,1,0:T(8,128)(2,1)S(1)} %get-tuple-element.58.refs_0_), channel_id=1, source_target_pairs={{0,1},{1,0},{2,3},{3,2},{4,5},{5,4},{6,7},{7,6},{8,9},{9,8},{10,11... | collective-permute-start | bytes 737288 | tf_op jit(solution)/shard_map/ppermute | solution.py:394
  42.2 5.4 %collective-permute-start.20 = (bf16[2,160,384]{2,1,0:T(8,128)(2,1)S(1)}, bf16[2,160,384]{2,1,0:T(8,128)(2,1)S(1)}, u32[]{:S(2)}, u32[]{:S(2)}) collective-permute-start(bf16[2,160,384]{2,1,0:T(8,128)(2,1)S(1)} %collective-permute-done.11.refs_1_), channel_id=1, source_target_pairs={{0,1},{1,0},{2,3},{3,2},{4,5},{5,4},{6,7},{7,6},{8,9},{9,8},{10,11... | collective-permute-start | bytes 737288 | tf_op jit(solution)/shard_map/ppermute | solution.py:394
  42.7 6.5 %collective-permute-start.21 = (bf16[2,160,384]{2,1,0:T(8,128)(2,1)S(1)}, bf16[2,160,384]{2,1,0:T(8,128)(2,1)S(1)}, u32[]{:S(2)}, u32[]{:S(2)}) collective-permute-start(bf16[2,160,384]{2,1,0:T(8,128)(2,1)S(1)} %collective-permute-done.12.refs_2_), channel_id=1, source_target_pairs={{0,1},{1,0},{2,3},{3,2},{4,5},{5,4},{6,7},{7,6},{8,9},{9,8},{10,11... | collective-permute-start | bytes 737288 | tf_op jit(solution)/shard_map/ppermute | solution.py:394
  46.6 2.6 %collective-permute-start.22 = (bf16[2,160,384]{2,1,0:T(8,128)(2,1)S(1)}, bf16[2,160,384]{2,1,0:T(8,128)(2,1)S(1)}, u32[]{:S(2)}, u32[]{:S(2)}) collective-permute-start(bf16[2,160,384]{2,1,0:T(8,128)(2,1)S(1)} %collective-permute-done.10.refs_3_), channel_id=1, source_target_pairs={{0,1},{1,0},{2,3},{3,2},{4,5},{5,4},{6,7},{7,6},{8,9},{9,8},{10,11... | collective-permute-start | bytes 737288 | tf_op jit(solution)/shard_map/ppermute | solution.py:394
  46.8 2.4 %collective-permute-start.25 = (bf16[4,160,128]{2,1,0:T(8,128)(2,1)S(1)}, bf16[4,160,128]{2,1,0:T(8,128)(2,1)S(1)}, u32[]{:S(2)}, u32[]{:S(2)}) collective-permute-start(bf16[4,160,128]{2,1,0:T(8,128)(2,1)S(1)} %fusion.refs_6_), channel_id=1, source_target_pairs={{0,1},{1,0},{2,3},{3,2},{4,5},{5,4},{6,7},{7,6},{8,9},{9,8},{10,11... | collective-permute-start | bytes 491528 | tf_op jit(solution)/shard_map/ppermute | solution.py:394
  47.5 1.8 %collective-permute-start.24 = (bf16[4,160,128]{2,1,0:T(8,128)(2,1)S(1)}, bf16[4,160,128]{2,1,0:T(8,128)(2,1)S(1)}, u32[]{:S(2)}, u32[]{:S(2)}) collective-permute-start(bf16[4,160,128]{2,1,0:T(8,128)(2,1)S(1)} %fusion.1.refs_5_), channel_id=1, source_target_pairs={{0,1},{1,0},{2,3},{3,2},{4,5},{5,4},{6,7},{7,6},{8,9},{9,8},{10,11... | collective-permute-start | bytes 491528 | tf_op jit(solution)/shard_map/ppermute | solution.py:394
  47.6 1.7 %collective-permute-start.23 = (bf16[640,128]{1,0:T(8,128)(2,1)S(1)}, bf16[640,128]{1,0:T(8,128)(2,1)S(1)}, u32[]{:S(2)}, u32[]{:S(2)}) collective-permute-start(bf16[640,128]{1,0:T(8,128)(2,1)S(1)} %constant_dynamic-update-slice_fusion.refs_4_), channel_id=1, source_target_pairs={{0,1},{1,0},{2,3},{3,2},{4,5},{5,4},{6,7},{7,6},{8,9},{9,8},{10,11... | collective-permute-start | bytes 491528 | tf_op jit(solution)/shard_map/ppermute | solution.py:394
  49.8 5.5 %collective-permute-start.26 = (bf16[96,384]{1,0:T(8,128)(2,1)S(1)}, bf16[96,384]{1,0:T(8,128)(2,1)S(1)}, u32[]{:S(2)}, u32[]{:S(2)}) collective-permute-start(bf16[96,384]{1,0:T(8,128)(2,1)S(1)} %get-tuple-element.103), channel_id=1, source_target_pairs={{0,4},{4,0},{8,12},{12,8},{1,5},{5,1},{9,13},{13,9},{2,6},{6,2},{1... | collective-permute-start | bytes 221192 | tf_op jit(solution)/shard_map/ppermute | solution.py:394
  49.9 9.2 %collective-permute-start.27 = (bf16[96,384]{1,0:T(8,128)(2,1)S(1)}, bf16[96,384]{1,0:T(8,128)(2,1)S(1)}, u32[]{:S(2)}, u32[]{:S(2)}) collective-permute-start(bf16[96,384]{1,0:T(8,128)(2,1)S(1)} %get-tuple-element.104), channel_id=1, source_target_pairs={{0,8},{4,12},{8,0},{12,4},{1,9},{5,13},{9,1},{13,5},{2,10},{6,14},... | collective-permute-start | bytes 221192 | tf_op jit(solution)/shard_map/ppermute | solution.py:394
  51.8 7.3 %collective-permute-start.28 = (bf16[96,384]{1,0:T(8,128)(2,1)S(1)}, bf16[96,384]{1,0:T(8,128)(2,1)S(1)}, u32[]{:S(2)}, u32[]{:S(2)}) collective-permute-start(bf16[96,384]{1,0:T(8,128)(2,1)S(1)} %get-tuple-element.105), channel_id=1, source_target_pairs={{0,12},{4,8},{8,4},{12,0},{1,13},{5,9},{9,5},{13,1},{2,14},{6,10},... | collective-permute-start | bytes 221192 | tf_op jit(solution)/shard_map/ppermute | solution.py:394
  59.2 4.4 %collective-permute-start.29 = (bf16[96,384]{1,0:T(8,128)(2,1)S(1)}, bf16[96,384]{1,0:T(8,128)(2,1)S(1)}, u32[]{:S(2)}, u32[]{:S(2)}) collective-permute-start(bf16[96,384]{1,0:T(8,128)(2,1)S(1)} %get-tuple-element.106), channel_id=1, source_target_pairs={{0,16},{16,0},{1,17},{17,1},{2,18},{18,2},{3,19},{19,3},{4,20},{20... | collective-permute-start | bytes 221192 | tf_op jit(solution)/shard_map/ppermute | solution.py:394

commit v6 on v5

--- a/solution.py
+++ b/solution.py
@@ -52,7 +52,7 @@
 
 
 def pack_kernel(
-    axes, q_hbm, k_hbm, v_hbm, o_hbm, g_hbm, x_hbm, pos_hbm, ids_hbm, qg_ref, kv_ref, x_ref, *scratch
+    axes, q_hbm, k_hbm, v_hbm, o_hbm, g_hbm, pos_hbm, ids_hbm, qg_ref, kv_ref, *scratch
 ):
     outs, prod, extra, pos, ids, sems = scratch
     count, width = outs.shape
@@ -67,7 +67,6 @@
                 (q_hbm, qg_ref.at[:count, :width]),
                 (k_hbm, kv_ref.at[:count, :width]),
                 (v_hbm, kv_ref.at[:count, width:]),
-                (x_hbm, x_ref),
             )
         )
     ]
@@ -107,8 +106,11 @@
         copy.wait()
 
 
-def deal_kernel(sizes, x_ref, *refs):
-    *out_refs, dealt = refs
+def deal_kernel(sizes, x_hbm, *refs):
+    *out_refs, dealt, x_ref, sem = refs
+    copy = pltpu.make_async_copy(x_hbm, x_ref, sem)
+    copy.start()
+    copy.wait()
     n_row, n_z, n_y, n_core = sizes
     blk = x_ref.shape[1] // (n_row * n_z * n_y * n_core)
     for a in range(n_row):
@@ -415,18 +417,19 @@
         return xor_permute(value, ("core",), (1,))
 
     packed = jax.ShapeDtypeStruct((count + PAD_ROWS, 2 * width), BF16)
-    qg, kv, x_here = pl.pallas_call(
+    x_here = layer_input
+    qg, kv = pl.pallas_call(
         functools.partial(pack_kernel, axes),
-        out_shape=(packed, packed, jax.ShapeDtypeStruct(layer_input.shape, BF16)),
-        in_specs=[HBM] * 8,
-        out_specs=(VMEM, VMEM, VMEM),
+        out_shape=(packed, packed),
+        in_specs=[HBM] * 7,
+        out_specs=(VMEM, VMEM),
         scratch_shapes=[
             pltpu.VMEM((count, width), BF16),
             pltpu.VMEM((2 * width, width), F32),
             pltpu.VMEM((PAD_ROWS, 2 * width), F32),
             pltpu.VMEM((token_pos.shape[0] // LANES, LANES), jnp.int32),
             pltpu.SMEM(block_sample.shape, jnp.int32),
-            pltpu.SemaphoreType.DMA((8,)),
+            pltpu.SemaphoreType.DMA((7,)),
         ],
         compiler_params=params(8 * MIB),
         name="pack",
@@ -439,7 +442,6 @@
                 values,
                 forward_out,
                 out_grad,
-                layer_input,
                 token_pos.reshape(-1, LANES),
                 block_sample,
             )
@@ -449,16 +451,20 @@
     blk = model_width // (n_z * n_y * n_core * n_row)
     kv_near = [kv] + [over_plane(kv, where) for where in plane[1:]]
     qg_all = [qg] + over_z([qg] * (n_z - 1))
-    x_here, kv_near[1] = lax.optimization_barrier((x_here, kv_near[1]))
+    x_here, kv_near[1:] = lax.optimization_barrier((x_here, kv_near[1:]))
     x_send = pl.pallas_call(
         functools.partial(deal_kernel, (n_row, n_z, n_y, n_core)),
         out_shape=[jax.ShapeDtypeStruct((n_core, count, n_z * blk), BF16)] * n_plane,
-        in_specs=[VMEM],
+        in_specs=[HBM],
         out_specs=[VMEM] * n_plane,
-        scratch_shapes=[pltpu.VMEM((n_plane, n_core, count, n_z * blk), BF16)],
+        scratch_shapes=[
+            pltpu.VMEM((n_plane, n_core, count, n_z * blk), BF16),
+            pltpu.VMEM(layer_input.shape, BF16),
+            pltpu.SemaphoreType.DMA(()),
+        ],
         compiler_params=params(16 * MIB),
         name="deal",
-    )(x_here)
+    )(pltpu.with_memory_space_constraint(x_here, pltpu.HBM))
     stacked = jnp.stack(kv_near)
     kv_all = [piece[None] for piece in kv_near] if n_pieces <= 8 else [stacked]
     kv_all = kv_all + [over_core(stacked)]

time: 64.5 us -> 64.4 us (level)
  waiting for transfers between devices: 21.6 us -> 20.3 us
  Pallas kernels: 8 us -> 9.04 us
    ppermute x30, waiting for transfers between devices: 21.6 us -> 20.3 us  [xor_permute(): return lax.ppermute(value, tuple(names), pairs)]
    pallas_call x1, Pallas kernels: 0.66 us -> 1.87 us  [local(): pl.pallas_call(functools.partial(deal_kernel, (n_row, n_z, n_y, n_core)),...]
  transfers between devices with their start and end apart: 30 -> 30, of which waited for: 9 -> 9; matrix products, arithmetic and copies ran while one was open for 3% -> 3% of each run, Pallas kernels for 8% -> 10%
where the time goes in v6:
time: 64.4 us; the launch traced here: 64.2 us
  starting transfers between devices  31.4 us (49%)
  waiting for transfers between devices  20.3 us (32%)
  Pallas kernels  9.04 us (14%)
  local copies, waits for them, and re-layouts  1.37 us (2%)
  other arithmetic  1.14 us (2%)
  between operations  0.93 us (1%)
    ppermute x30, starting transfers between devices, xor_permute(): return lax.ppermute(value, tuple(names), pairs)  31.4 us
    ppermute x30, waiting for transfers between devices, xor_permute(): return lax.ppermute(value, tuple(names), pairs)  20.3 us
    pallas_call x1, Pallas kernels, local(): pl.pallas_call(functools.partial(forward_kernel, count, width, n_z, len(k...  2.26 us
    pallas_call x1, Pallas kernels, local(): pl.pallas_call(functools.partial(deal_kernel, (n_row, n_z, n_y, n_core)),...  1.87 us
  transfers between devices with their start and end apart: 30, of which 9 were waited for; matrix products, arithmetic and copies ran while one was open for 3% of the time, Pallas kernels for 10%

profile of v6, /device:TPU:0, one launch (start us, length us, event | category | flops | bytes accessed | tf_op | source)
XLA Modules:
  0.0 64.2 jit_solution(2831033588980323411)
XLA Ops:
  0.6 1.2 %pack.1 = (bf16[176,256]{1,0:T(8,128)(2,1)S(1)}, bf16[176,256]{1,0:T(8,128)(2,1)S(1)}) custom-call(bf16[160,128]{1,0:T(8,128)(2,1)} %q_hbm.1, bf16[160,128]{1,0:T(8,128)(2,1)} %k_hbm.1, bf16[160,128]{1,0:T(8,128)(2,1)} %v_hbm.1, bf16[160,128]{1,0:T(8,128)(2,1)} %o_hbm.1, bf16[160,128]{1,0:T(8,128)(2,1)} %g_hbm.1, s32[40,128]{1,0:T(8,128)} %bitcast.41, s32[40]{0:T(128)} %ids_hbm.1), custom_call_target="tpu_custom_call" | custom-call | tf_op jit(solution)/shard_map/pack/pallas_call | solution.py:421
  1.9 3.0 %collective-permute-start = (bf16[176,256]{1,0:T(8,128)(2,1)S(1)}, bf16[176,256]{1,0:T(8,128)(2,1)S(1)}, u32[]{:S(2)}, u32[]{:S(2)}) collective-permute-start(bf16[176,256]{1,0:T(8,128)(2,1)S(1)} %get-tuple-element.56), channel_id=1, source_target_pairs={{0,2},{2,0},{16,18},{18,16},{1,3},{3,1},{17,19},{19,17},{4,6},{6,4... | collective-permute-start | bytes 270344 | tf_op jit(solution)/shard_map/ppermute | solution.py:396
  4.9 1.5 %collective-permute-start.1 = (bf16[176,256]{1,0:T(8,128)(2,1)S(1)}, bf16[176,256]{1,0:T(8,128)(2,1)S(1)}, u32[]{:S(2)}, u32[]{:S(2)}) collective-permute-start(bf16[176,256]{1,0:T(8,128)(2,1)S(1)} %get-tuple-element.56), channel_id=1, source_target_pairs={{0,16},{2,18},{16,0},{18,2},{1,17},{3,19},{17,1},{19,3},{4,20},{6,... | collective-permute-start | bytes 270344 | tf_op jit(solution)/shard_map/ppermute | solution.py:396
  6.5 4.0 %collective-permute-start.3 = (bf16[176,256]{1,0:T(8,128)(2,1)S(1)}, bf16[176,256]{1,0:T(8,128)(2,1)S(1)}, u32[]{:S(2)}, u32[]{:S(2)}) collective-permute-start(bf16[176,256]{1,0:T(8,128)(2,1)S(1)} %get-tuple-element.59.refs_3_), channel_id=1, source_target_pairs={{0,12},{4,8},{8,4},{12,0},{1,13},{5,9},{9,5},{13,1},{2,14},{6,10},... | collective-permute-start | bytes 270344 | tf_op jit(solution)/shard_map/ppermute | solution.py:396
  10.5 0.6 collective-permute-start.5
  11.1 0.8 %collective-permute-done.2 = bf16[176,256]{1,0:T(8,128)(2,1)S(1)} collective-permute-done((bf16[176,256]{1,0:T(8,128)(2,1)S(1)}, bf16[176,256]{1,0:T(8,128)(2,1)S(1)}, u32[]{:S(2)}, u32[]{:S(2)}) %collective-permute-start.2) | collective-permute-done | bytes 90144 | tf_op jit(solution)/shard_map/ppermute | solution.py:396
  11.9 0.1 collective-permute-start.6
  12.0 1.9 %deal.1 = (bf16[2,160,384]{2,1,0:T(8,128)(2,1)S(1)}, bf16[2,160,384]{2,1,0:T(8,128)(2,1)S(1)}, bf16[2,160,384]{2,1,0:T(8,128)(2,1)S(1)}, bf16[2,160,384]{2,1,0:T(8,128)(2,1)S(1)}) custom-call(bf16[160,3072]{1,0:T(8,128)(2,1)} %x_hbm), custom_call_target="tpu_custom_call" | custom-call | tf_op jit(solution)/shard_map/deal/pallas_call | solution.py:455
  13.9 2.0 %collective-permute-start.10 = (bf16[2,160,384]{2,1,0:T(8,128)(2,1)S(1)}, bf16[2,160,384]{2,1,0:T(8,128)(2,1)S(1)}, u32[]{:S(2)}, u32[]{:S(2)}) collective-permute-start(bf16[2,160,384]{2,1,0:T(8,128)(2,1)S(1)} %get-tuple-element.72), channel_id=1, source_target_pairs={{0,18},{2,16},{16,2},{18,0},{1,19},{3,17},{17,3},{19,1},{4,22},{6,... | collective-permute-start | bytes 737288 | tf_op jit(solution)/shard_map/ppermute | solution.py:396
  15.8 1.4 %collective-permute-done.4.refs_1_ = bf16[176,256]{1,0:T(8,128)(2,1)S(1)} collective-permute-done((bf16[176,256]{1,0:T(8,128)(2,1)S(1)}, bf16[176,256]{1,0:T(8,128)(2,1)S(1)}, u32[]{:S(2)}, u32[]{:S(2)}) %collective-permute-start.4) | collective-permute-done | bytes 90144 | tf_op jit(solution)/shard_map/ppermute | solution.py:396
  17.3 0.1 lines.1
  17.4 2.3 %forward.1 = (bf16[8,160,640]{2,1,0:T(8,128)(2,1)S(1)}, bf16[8,160,640]{2,1,0:T(8,128)(2,1)S(1)}, f32[8,640]{1,0:T(8,128)S(1)}, bf16[160,128]{1,0:T(8,128)(2,1)S...) custom-call(bf16[640,128]{1,0:T(8,128)(2,1)S(1)} %get-tuple-element.60.refs_0_.refs_3_, ...), custom_call_target="tpu_custom_call" | custom-call | flops 30000001024 | tf_op jit(solution)/shard_map/forward/pallas_call | solution.py:484
  19.7 0.7 %collective-permute-start.7 = (bf16[192,128]{1,0:T(8,128)(2,1)S(1)}, bf16[192,128]{1,0:T(8,128)(2,1)S(1)}, u32[]{:S(2)}, u32[]{:S(2)}) collective-permute-start(bf16[192,128]{1,0:T(8,128)(2,1)S(1)} %get-tuple-element.69), channel_id=1, source_target_pairs={{0,4},{4,0},{8,12},{12,8},{1,5},{5,1},{9,13},{13,9},{2,6},{6,2},{1... | collective-permute-start | bytes 147464 | tf_op jit(solution)/shard_map/ppermute | solution.py:396
  20.4 2.4 %collective-permute-start.8 = (bf16[192,128]{1,0:T(8,128)(2,1)S(1)}, bf16[192,128]{1,0:T(8,128)(2,1)S(1)}, u32[]{:S(2)}, u32[]{:S(2)}) collective-permute-start(bf16[192,128]{1,0:T(8,128)(2,1)S(1)} %get-tuple-element.70), channel_id=1, source_target_pairs={{0,8},{4,12},{8,0},{12,4},{1,9},{5,13},{9,1},{13,5},{2,10},{6,14},... | collective-permute-start | bytes 147464 | tf_op jit(solution)/shard_map/ppermute | solution.py:396
  22.8 1.3 %collective-permute-start.9 = (bf16[192,128]{1,0:T(8,128)(2,1)S(1)}, bf16[192,128]{1,0:T(8,128)(2,1)S(1)}, u32[]{:S(2)}, u32[]{:S(2)}) collective-permute-start(bf16[192,128]{1,0:T(8,128)(2,1)S(1)} %get-tuple-element.71), channel_id=1, source_target_pairs={{0,12},{4,8},{8,4},{12,0},{1,13},{5,9},{9,5},{13,1},{2,14},{6,10},... | collective-permute-start | bytes 147464 | tf_op jit(solution)/shard_map/ppermute | solution.py:396
  24.1 1.5 %collective-permute-start.11 = (bf16[2,160,384]{2,1,0:T(8,128)(2,1)S(1)}, bf16[2,160,384]{2,1,0:T(8,128)(2,1)S(1)}, u32[]{:S(2)}, u32[]{:S(2)}) collective-permute-start(bf16[2,160,384]{2,1,0:T(8,128)(2,1)S(1)} %get-tuple-element.80), channel_id=1, source_target_pairs={{0,2},{2,0},{16,18},{18,16},{1,3},{3,1},{17,19},{19,17},{4,6},{6,4... | collective-permute-start | bytes 737288 | tf_op jit(solution)/shard_map/ppermute | solution.py:396
  25.7 1.5 %collective-permute-start.12 = (bf16[2,160,384]{2,1,0:T(8,128)(2,1)S(1)}, bf16[2,160,384]{2,1,0:T(8,128)(2,1)S(1)}, u32[]{:S(2)}, u32[]{:S(2)}) collective-permute-start(bf16[2,160,384]{2,1,0:T(8,128)(2,1)S(1)} %get-tuple-element.81), channel_id=1, source_target_pairs={{0,16},{2,18},{16,0},{18,2},{1,17},{3,19},{17,1},{19,3},{4,20},{6,... | collective-permute-start | bytes 737288 | tf_op jit(solution)/shard_map/ppermute | solution.py:396
  27.2 1.5 %collective-permute-done.9.refs_5_.refs_2_ = bf16[192,128]{1,0:T(8,128)(2,1)S(1)} collective-permute-done((bf16[192,128]{1,0:T(8,128)(2,1)S(1)}, bf16[192,128]{1,0:T(8,128)(2,1)S(1)}, u32[]{:S(2)}, u32[]{:S(2)}) %collective-permute-start.9) | collective-permute-done | bytes 49184 | tf_op jit(solution)/shard_map/ppermute | solution.py:396
  28.7 0.9 %away.1 = (bf16[4,160,128]{2,1,0:T(8,128)(2,1)S(1)}, bf16[4,160,128]{2,1,0:T(8,128)(2,1)S(1)}, bf16[640,128]{1,0:T(8,128)(2,1)S(1)}, bf16[640,128]{1,0:T(8,128)(2,1)S(1)}, f32[640,8]{1,0:T(8,128)S(1)}) custom-call(bf16[8,160,640]{2,1,0:T(8,128)(2,1)S(1)} %get-tuple-element.66.refs_0_.w_ref, bf16[8,160,640]{2,1,0:T(8,128)(2,1)S(1)} %get-tuple-element.67.refs_1_.u_ref, ...), custom_call_target="tpu_custom_call" | custom-call | flops 30000001024 | tf_op jit(solution)/shard_map/away/pallas_call | solution.py:522
  29.7 0.5 collective-permute-start.14
  30.2 0.6 home.1
  30.8 1.0 %collective-permute-done.12.refs_2_ = bf16[2,160,384]{2,1,0:T(8,128)(2,1)S(1)} collective-permute-done((bf16[2,160,384]{2,1,0:T(8,128)(2,1)S(1)}, bf16[2,160,384]{2,1,0:T(8,128)(2,1)S(1)}, u32[]{:S(2)}, u32[]{:S(2)}) %collective-permute-start.12) | collective-permute-done | bytes 245792 | tf_op jit(solution)/shard_map/ppermute | solution.py:396
  31.9 0.2 query.1
  32.2 1.6 %collective-permute-start.15 = (bf16[784,128]{1,0:T(8,128)(2,1)S(1)}, bf16[784,128]{1,0:T(8,128)(2,1)S(1)}, u32[]{:S(2)}, u32[]{:S(2)}) collective-permute-start(bf16[784,128]{1,0:T(8,128)(2,1)S(1)} %pad_maximum_fusion.2), channel_id=1, source_target_pairs={{0,16},{2,18},{16,0},{18,2},{1,17},{3,19},{17,1},{19,3},{4,20},{6,... | collective-permute-start | bytes 602120 | tf_op jit(solution)/shard_map/ppermute | solution.py:396
  33.7 0.8 %collective-permute-start.16 = (bf16[656,128]{1,0:T(8,128)(2,1)S(1)}, bf16[656,128]{1,0:T(8,128)(2,1)S(1)}, u32[]{:S(2)}, u32[]{:S(2)}) collective-permute-start(bf16[656,128]{1,0:T(8,128)(2,1)S(1)} %pad_maximum_fusion.4), channel_id=1, source_target_pairs={{0,2},{2,0},{16,18},{18,16},{1,3},{3,1},{17,19},{19,17},{4,6},{6,4... | collective-permute-start | bytes 503816 | tf_op jit(solution)/shard_map/ppermute | solution.py:396
  34.5 4.7 %collective-permute-done.16 = bf16[656,128]{1,0:T(8,128)(2,1)S(1)} collective-permute-done((bf16[656,128]{1,0:T(8,128)(2,1)S(1)}, bf16[656,128]{1,0:T(8,128)(2,1)S(1)}, u32[]{:S(2)}, u32[]{:S(2)}) %collective-permute-start.16) | collective-permute-done | bytes 167968 | tf_op jit(solution)/shard_map/ppermute | solution.py:396
  39.4 1.6 %collective-permute-start.17 = (bf16[928,128]{1,0:T(8,128)(2,1)S(1)}, bf16[928,128]{1,0:T(8,128)(2,1)S(1)}, u32[]{:S(2)}, u32[]{:S(2)}) collective-permute-start(bf16[928,128]{1,0:T(8,128)(2,1)S(1)} %pad_maximum_fusion.1), channel_id=1, source_target_pairs={{0,2},{2,0},{16,18},{18,16},{1,3},{3,1},{17,19},{19,17},{4,6},{6,4... | collective-permute-start | bytes 712712 | tf_op jit(solution)/shard_map/ppermute | solution.py:396
  41.0 1.0 %collective-permute-start.18 = (bf16[672,128]{1,0:T(8,128)(2,1)S(1)}, bf16[672,128]{1,0:T(8,128)(2,1)S(1)}, u32[]{:S(2)}, u32[]{:S(2)}) collective-permute-start(bf16[672,128]{1,0:T(8,128)(2,1)S(1)} %pad_maximum_fusion.3), channel_id=1, source_target_pairs={{0,16},{2,18},{16,0},{18,2},{1,17},{3,19},{17,1},{19,3},{4,20},{6,... | collective-permute-start | bytes 516104 | tf_op jit(solution)/shard_map/ppermute | solution.py:396
  42.0 0.5 collective-permute-start.20
  42.5 3.9 %collective-permute-done.18 = bf16[672,128]{1,0:T(8,128)(2,1)S(1)} collective-permute-done((bf16[672,128]{1,0:T(8,128)(2,1)S(1)}, bf16[672,128]{1,0:T(8,128)(2,1)S(1)}, u32[]{:S(2)}, u32[]{:S(2)}) %collective-permute-start.18) | collective-permute-done | bytes 172064 | tf_op jit(solution)/shard_map/ppermute | solution.py:396
  46.5 0.1 fusion.refs_6_
  46.6 0.6 collective-permute-start.25
  47.2 0.1 fusion.1.refs_5_
  47.3 0.1 collective-permute-start.24
  47.4 0.5 collective-permute-start.23
  47.9 0.5 near.1.near_ref
  48.4 0.6 dynamic-slice_bitcast_fusion
  49.1 0.6 far.1
  49.7 0.1 collective-permute-start.26
  49.8 2.4 %collective-permute-start.27 = (bf16[96,384]{1,0:T(8,128)(2,1)S(1)}, bf16[96,384]{1,0:T(8,128)(2,1)S(1)}, u32[]{:S(2)}, u32[]{:S(2)}) collective-permute-start(bf16[96,384]{1,0:T(8,128)(2,1)S(1)} %get-tuple-element.106), channel_id=1, source_target_pairs={{0,8},{4,12},{8,0},{12,4},{1,9},{5,13},{9,1},{13,5},{2,10},{6,14},... | collective-permute-start | bytes 221192 | tf_op jit(solution)/shard_map/ppermute | solution.py:396
  52.1 2.0 %collective-permute-start.28 = (bf16[96,384]{1,0:T(8,128)(2,1)S(1)}, bf16[96,384]{1,0:T(8,128)(2,1)S(1)}, u32[]{:S(2)}, u32[]{:S(2)}) collective-permute-start(bf16[96,384]{1,0:T(8,128)(2,1)S(1)} %get-tuple-element.107), channel_id=1, source_target_pairs={{0,12},{4,8},{8,4},{12,0},{1,13},{5,9},{9,5},{13,1},{2,14},{6,10},... | collective-permute-start | bytes 221192 | tf_op jit(solution)/shard_map/ppermute | solution.py:396
  54.1 0.6 dynamic-slice_bitcast_fusion.1
  54.7 0.4 collective-permute-done.26
  55.1 3.8 %collective-permute-done.27 = bf16[96,384]{1,0:T(8,128)(2,1)S(1)} collective-permute-done((bf16[96,384]{1,0:T(8,128)(2,1)S(1)}, bf16[96,384]{1,0:T(8,128)(2,1)S(1)}, u32[]{:S(2)}, u32[]{:S(2)}) %collective-permute-start.27) | collective-permute-done | bytes 73760 | tf_op jit(solution)/shard_map/ppermute | solution.py:396
  59.0 1.1 %collective-permute-start.29 = (bf16[96,384]{1,0:T(8,128)(2,1)S(1)}, bf16[96,384]{1,0:T(8,128)(2,1)S(1)}, u32[]{:S(2)}, u32[]{:S(2)}) collective-permute-start(bf16[96,384]{1,0:T(8,128)(2,1)S(1)} %get-tuple-element.108), channel_id=1, source_target_pairs={{0,16},{16,0},{1,17},{17,1},{2,18},{18,2},{3,19},{19,3},{4,20},{20... | collective-permute-start | bytes 221192 | tf_op jit(solution)/shard_map/ppermute | solution.py:396
  60.1 0.6 pad_maximum_fusion.5
  60.8 2.7 %collective-permute-done.29.refs_0_ = bf16[96,384]{1,0:T(8,128)(2,1)S(1)} collective-permute-done((bf16[96,384]{1,0:T(8,128)(2,1)S(1)}, bf16[96,384]{1,0:T(8,128)(2,1)S(1)}, u32[]{:S(2)}, u32[]{:S(2)}) %collective-permute-start.29) | collective-permute-done | bytes 73760 | tf_op jit(solution)/shard_map/ppermute | solution.py:396
  63.5 0.7 %assemble.1 = f32[2,96,384]{2,1,0:T(8,128)} custom-call(f32[96,384]{1,0:T(8,128)S(1)} %get-tuple-element.109.own_ref, bf16[96,384]{1,0:T(8,128)(2,1)S(1)} %collective-permute-done.29.refs_0_), custom_call_target="tpu_custom_call" | custom-call | tf_op jit(solution)/shard_map/assemble/pallas_call | solution.py:614
  (49 shorter events, 0.7 us)
Async XLA Ops:
  1.9 8.6 %collective-permute-start = (bf16[176,256]{1,0:T(8,128)(2,1)S(1)}, bf16[176,256]{1,0:T(8,128)(2,1)S(1)}, u32[]{:S(2)}, u32[]{:S(2)}) collective-permute-start(bf16[176,256]{1,0:T(8,128)(2,1)S(1)} %get-tuple-element.56), channel_id=1, source_target_pairs={{0,2},{2,0},{16,18},{18,16},{1,3},{3,1},{17,19},{19,17},{4,6},{6,4... | collective-permute-start | bytes 270344 | tf_op jit(solution)/shard_map/ppermute | solution.py:396
  4.9 6.1 %collective-permute-start.1 = (bf16[176,256]{1,0:T(8,128)(2,1)S(1)}, bf16[176,256]{1,0:T(8,128)(2,1)S(1)}, u32[]{:S(2)}, u32[]{:S(2)}) collective-permute-start(bf16[176,256]{1,0:T(8,128)(2,1)S(1)} %get-tuple-element.56), channel_id=1, source_target_pairs={{0,16},{2,18},{16,0},{18,2},{1,17},{3,19},{17,1},{19,3},{4,20},{6,... | collective-permute-start | bytes 270344 | tf_op jit(solution)/shard_map/ppermute | solution.py:396
  6.4 5.4 %collective-permute-start.2 = (bf16[176,256]{1,0:T(8,128)(2,1)S(1)}, bf16[176,256]{1,0:T(8,128)(2,1)S(1)}, u32[]{:S(2)}, u32[]{:S(2)}) collective-permute-start(bf16[176,256]{1,0:T(8,128)(2,1)S(1)} %get-tuple-element.56), channel_id=1, source_target_pairs={{0,18},{2,16},{16,2},{18,0},{1,19},{3,17},{17,3},{19,1},{4,22},{6,... | collective-permute-start | bytes 270344 | tf_op jit(solution)/shard_map/ppermute | solution.py:396
  6.5 9.4 %collective-permute-start.3 = (bf16[176,256]{1,0:T(8,128)(2,1)S(1)}, bf16[176,256]{1,0:T(8,128)(2,1)S(1)}, u32[]{:S(2)}, u32[]{:S(2)}) collective-permute-start(bf16[176,256]{1,0:T(8,128)(2,1)S(1)} %get-tuple-element.59.refs_3_), channel_id=1, source_target_pairs={{0,12},{4,8},{8,4},{12,0},{1,13},{5,9},{9,5},{13,1},{2,14},{6,10},... | collective-permute-start | bytes 270344 | tf_op jit(solution)/shard_map/ppermute | solution.py:396
  10.5 6.8 %collective-permute-start.4 = (bf16[176,256]{1,0:T(8,128)(2,1)S(1)}, bf16[176,256]{1,0:T(8,128)(2,1)S(1)}, u32[]{:S(2)}, u32[]{:S(2)}) collective-permute-start(bf16[176,256]{1,0:T(8,128)(2,1)S(1)} %get-tuple-element.59.refs_3_), channel_id=1, source_target_pairs={{0,8},{4,12},{8,0},{12,4},{1,9},{5,13},{9,1},{13,5},{2,10},{6,14},... | collective-permute-start | bytes 270344 | tf_op jit(solution)/shard_map/ppermute | solution.py:396
  10.5 6.8 %collective-permute-start.5 = (bf16[176,256]{1,0:T(8,128)(2,1)S(1)}, bf16[176,256]{1,0:T(8,128)(2,1)S(1)}, u32[]{:S(2)}, u32[]{:S(2)}) collective-permute-start(bf16[176,256]{1,0:T(8,128)(2,1)S(1)} %get-tuple-element.59.refs_3_), channel_id=1, source_target_pairs={{0,4},{4,0},{8,12},{12,8},{1,5},{5,1},{9,13},{13,9},{2,6},{6,2},{1... | collective-permute-start | bytes 270344 | tf_op jit(solution)/shard_map/ppermute | solution.py:396
  11.9 5.5 %collective-permute-start.6 = (bf16[4,176,256]{2,1,0:T(8,128)(2,1)S(1)}, bf16[4,176,256]{2,1,0:T(8,128)(2,1)S(1)}, u32[]{:S(2)}, u32[]{:S(2)}) collective-permute-start(bf16[4,176,256]{2,1,0:T(8,128)(2,1)S(1)} %pad_maximum_fusion), channel_id=1, source_target_pairs={{0,1},{1,0},{2,3},{3,2},{4,5},{5,4},{6,7},{7,6},{8,9},{9,8},{10,11... | collective-permute-start | bytes 1081352 | tf_op jit(solution)/shard_map/ppermute | solution.py:396
  13.9 11.8 %collective-permute-start.10 = (bf16[2,160,384]{2,1,0:T(8,128)(2,1)S(1)}, bf16[2,160,384]{2,1,0:T(8,128)(2,1)S(1)}, u32[]{:S(2)}, u32[]{:S(2)}) collective-permute-start(bf16[2,160,384]{2,1,0:T(8,128)(2,1)S(1)} %get-tuple-element.72), channel_id=1, source_target_pairs={{0,18},{2,16},{16,2},{18,0},{1,19},{3,17},{17,3},{19,1},{4,22},{6,... | collective-permute-start | bytes 737288 | tf_op jit(solution)/shard_map/ppermute | solution.py:396
  19.7 7.5 %collective-permute-start.7 = (bf16[192,128]{1,0:T(8,128)(2,1)S(1)}, bf16[192,128]{1,0:T(8,128)(2,1)S(1)}, u32[]{:S(2)}, u32[]{:S(2)}) collective-permute-start(bf16[192,128]{1,0:T(8,128)(2,1)S(1)} %get-tuple-element.69), channel_id=1, source_target_pairs={{0,4},{4,0},{8,12},{12,8},{1,5},{5,1},{9,13},{13,9},{2,6},{6,2},{1... | collective-permute-start | bytes 147464 | tf_op jit(solution)/shard_map/ppermute | solution.py:396
  20.4 6.8 %collective-permute-start.8 = (bf16[192,128]{1,0:T(8,128)(2,1)S(1)}, bf16[192,128]{1,0:T(8,128)(2,1)S(1)}, u32[]{:S(2)}, u32[]{:S(2)}) collective-permute-start(bf16[192,128]{1,0:T(8,128)(2,1)S(1)} %get-tuple-element.70), channel_id=1, source_target_pairs={{0,8},{4,12},{8,0},{12,4},{1,9},{5,13},{9,1},{13,5},{2,10},{6,14},... | collective-permute-start | bytes 147464 | tf_op jit(solution)/shard_map/ppermute | solution.py:396
  22.8 5.9 %collective-permute-start.9 = (bf16[192,128]{1,0:T(8,128)(2,1)S(1)}, bf16[192,128]{1,0:T(8,128)(2,1)S(1)}, u32[]{:S(2)}, u32[]{:S(2)}) collective-permute-start(bf16[192,128]{1,0:T(8,128)(2,1)S(1)} %get-tuple-element.71), channel_id=1, source_target_pairs={{0,12},{4,8},{8,4},{12,0},{1,13},{5,9},{9,5},{13,1},{2,14},{6,10},... | collective-permute-start | bytes 147464 | tf_op jit(solution)/shard_map/ppermute | solution.py:396
  24.1 6.7 %collective-permute-start.11 = (bf16[2,160,384]{2,1,0:T(8,128)(2,1)S(1)}, bf16[2,160,384]{2,1,0:T(8,128)(2,1)S(1)}, u32[]{:S(2)}, u32[]{:S(2)}) collective-permute-start(bf16[2,160,384]{2,1,0:T(8,128)(2,1)S(1)} %get-tuple-element.80), channel_id=1, source_target_pairs={{0,2},{2,0},{16,18},{18,16},{1,3},{3,1},{17,19},{19,17},{4,6},{6,4... | collective-permute-start | bytes 737288 | tf_op jit(solution)/shard_map/ppermute | solution.py:396
  25.7 6.2 %collective-permute-start.12 = (bf16[2,160,384]{2,1,0:T(8,128)(2,1)S(1)}, bf16[2,160,384]{2,1,0:T(8,128)(2,1)S(1)}, u32[]{:S(2)}, u32[]{:S(2)}) collective-permute-start(bf16[2,160,384]{2,1,0:T(8,128)(2,1)S(1)} %get-tuple-element.81), channel_id=1, source_target_pairs={{0,16},{2,18},{16,0},{18,2},{1,17},{3,19},{17,1},{19,3},{4,20},{6,... | collective-permute-start | bytes 737288 | tf_op jit(solution)/shard_map/ppermute | solution.py:396
  29.6 2.4 %collective-permute-start.13 = (bf16[4,160,128]{2,1,0:T(8,128)(2,1)S(1)}, bf16[4,160,128]{2,1,0:T(8,128)(2,1)S(1)}, u32[]{:S(2)}, u32[]{:S(2)}) collective-permute-start(bf16[4,160,128]{2,1,0:T(8,128)(2,1)S(1)} %get-tuple-element.89), channel_id=1, source_target_pairs={{0,1},{1,0},{2,3},{3,2},{4,5},{5,4},{6,7},{7,6},{8,9},{9,8},{10,11... | collective-permute-start | bytes 491528 | tf_op jit(solution)/shard_map/ppermute | solution.py:396
  29.7 2.3 %collective-permute-start.14 = (bf16[4,160,128]{2,1,0:T(8,128)(2,1)S(1)}, bf16[4,160,128]{2,1,0:T(8,128)(2,1)S(1)}, u32[]{:S(2)}, u32[]{:S(2)}) collective-permute-start(bf16[4,160,128]{2,1,0:T(8,128)(2,1)S(1)} %get-tuple-element.91), channel_id=1, source_target_pairs={{0,1},{1,0},{2,3},{3,2},{4,5},{5,4},{6,7},{7,6},{8,9},{9,8},{10,11... | collective-permute-start | bytes 491528 | tf_op jit(solution)/shard_map/ppermute | solution.py:396
  32.2 7.0 %collective-permute-start.15 = (bf16[784,128]{1,0:T(8,128)(2,1)S(1)}, bf16[784,128]{1,0:T(8,128)(2,1)S(1)}, u32[]{:S(2)}, u32[]{:S(2)}) collective-permute-start(bf16[784,128]{1,0:T(8,128)(2,1)S(1)} %pad_maximum_fusion.2), channel_id=1, source_target_pairs={{0,16},{2,18},{16,0},{18,2},{1,17},{3,19},{17,1},{19,3},{4,20},{6,... | collective-permute-start | bytes 602120 | tf_op jit(solution)/shard_map/ppermute | solution.py:396
  33.7 5.5 %collective-permute-start.16 = (bf16[656,128]{1,0:T(8,128)(2,1)S(1)}, bf16[656,128]{1,0:T(8,128)(2,1)S(1)}, u32[]{:S(2)}, u32[]{:S(2)}) collective-permute-start(bf16[656,128]{1,0:T(8,128)(2,1)S(1)} %pad_maximum_fusion.4), channel_id=1, source_target_pairs={{0,2},{2,0},{16,18},{18,16},{1,3},{3,1},{17,19},{19,17},{4,6},{6,4... | collective-permute-start | bytes 503816 | tf_op jit(solution)/shard_map/ppermute | solution.py:396
  39.4 7.0 %collective-permute-start.17 = (bf16[928,128]{1,0:T(8,128)(2,1)S(1)}, bf16[928,128]{1,0:T(8,128)(2,1)S(1)}, u32[]{:S(2)}, u32[]{:S(2)}) collective-permute-start(bf16[928,128]{1,0:T(8,128)(2,1)S(1)} %pad_maximum_fusion.1), channel_id=1, source_target_pairs={{0,2},{2,0},{16,18},{18,16},{1,3},{3,1},{17,19},{19,17},{4,6},{6,4... | collective-permute-start | bytes 712712 | tf_op jit(solution)/shard_map/ppermute | solution.py:396
  41.0 5.4 %collective-permute-start.18 = (bf16[672,128]{1,0:T(8,128)(2,1)S(1)}, bf16[672,128]{1,0:T(8,128)(2,1)S(1)}, u32[]{:S(2)}, u32[]{:S(2)}) collective-permute-start(bf16[672,128]{1,0:T(8,128)(2,1)S(1)} %pad_maximum_fusion.3), channel_id=1, source_target_pairs={{0,16},{2,18},{16,0},{18,2},{1,17},{3,19},{17,1},{19,3},{4,20},{6,... | collective-permute-start | bytes 516104 | tf_op jit(solution)/shard_map/ppermute | solution.py:396
  42.0 5.3 %collective-permute-start.19 = (bf16[2,160,384]{2,1,0:T(8,128)(2,1)S(1)}, bf16[2,160,384]{2,1,0:T(8,128)(2,1)S(1)}, u32[]{:S(2)}, u32[]{:S(2)}) collective-permute-start(bf16[2,160,384]{2,1,0:T(8,128)(2,1)S(1)} %get-tuple-element.58.refs_0_), channel_id=1, source_target_pairs={{0,1},{1,0},{2,3},{3,2},{4,5},{5,4},{6,7},{7,6},{8,9},{9,8},{10,11... | collective-permute-start | bytes 737288 | tf_op jit(solution)/shard_map/ppermute | solution.py:396
  42.0 5.4 %collective-permute-start.20 = (bf16[2,160,384]{2,1,0:T(8,128)(2,1)S(1)}, bf16[2,160,384]{2,1,0:T(8,128)(2,1)S(1)}, u32[]{:S(2)}, u32[]{:S(2)}) collective-permute-start(bf16[2,160,384]{2,1,0:T(8,128)(2,1)S(1)} %collective-permute-done.11.refs_1_), channel_id=1, source_target_pairs={{0,1},{1,0},{2,3},{3,2},{4,5},{5,4},{6,7},{7,6},{8,9},{9,8},{10,11... | collective-permute-start | bytes 737288 | tf_op jit(solution)/shard_map/ppermute | solution.py:396
  42.5 6.5 %collective-permute-start.21 = (bf16[2,160,384]{2,1,0:T(8,128)(2,1)S(1)}, bf16[2,160,384]{2,1,0:T(8,128)(2,1)S(1)}, u32[]{:S(2)}, u32[]{:S(2)}) collective-permute-start(bf16[2,160,384]{2,1,0:T(8,128)(2,1)S(1)} %collective-permute-done.12.refs_2_), channel_id=1, source_target_pairs={{0,1},{1,0},{2,3},{3,2},{4,5},{5,4},{6,7},{7,6},{8,9},{9,8},{10,11... | collective-permute-start | bytes 737288 | tf_op jit(solution)/shard_map/ppermute | solution.py:396
  46.4 2.6 %collective-permute-start.22 = (bf16[2,160,384]{2,1,0:T(8,128)(2,1)S(1)}, bf16[2,160,384]{2,1,0:T(8,128)(2,1)S(1)}, u32[]{:S(2)}, u32[]{:S(2)}) collective-permute-start(bf16[2,160,384]{2,1,0:T(8,128)(2,1)S(1)} %collective-permute-done.10.refs_3_), channel_id=1, source_target_pairs={{0,1},{1,0},{2,3},{3,2},{4,5},{5,4},{6,7},{7,6},{8,9},{9,8},{10,11... | collective-permute-start | bytes 737288 | tf_op jit(solution)/shard_map/ppermute | solution.py:396
  46.6 2.4 %collective-permute-start.25 = (bf16[4,160,128]{2,1,0:T(8,128)(2,1)S(1)}, bf16[4,160,128]{2,1,0:T(8,128)(2,1)S(1)}, u32[]{:S(2)}, u32[]{:S(2)}) collective-permute-start(bf16[4,160,128]{2,1,0:T(8,128)(2,1)S(1)} %fusion.refs_6_), channel_id=1, source_target_pairs={{0,1},{1,0},{2,3},{3,2},{4,5},{5,4},{6,7},{7,6},{8,9},{9,8},{10,11... | collective-permute-start | bytes 491528 | tf_op jit(solution)/shard_map/ppermute | solution.py:396
  47.3 1.7 %collective-permute-start.24 = (bf16[4,160,128]{2,1,0:T(8,128)(2,1)S(1)}, bf16[4,160,128]{2,1,0:T(8,128)(2,1)S(1)}, u32[]{:S(2)}, u32[]{:S(2)}) collective-permute-start(bf16[4,160,128]{2,1,0:T(8,128)(2,1)S(1)} %fusion.1.refs_5_), channel_id=1, source_target_pairs={{0,1},{1,0},{2,3},{3,2},{4,5},{5,4},{6,7},{7,6},{8,9},{9,8},{10,11... | collective-permute-start | bytes 491528 | tf_op jit(solution)/shard_map/ppermute | solution.py:396
  47.4 1.7 %collective-permute-start.23 = (bf16[640,128]{1,0:T(8,128)(2,1)S(1)}, bf16[640,128]{1,0:T(8,128)(2,1)S(1)}, u32[]{:S(2)}, u32[]{:S(2)}) collective-permute-start(bf16[640,128]{1,0:T(8,128)(2,1)S(1)} %constant_dynamic-update-slice_fusion.refs_4_), channel_id=1, source_target_pairs={{0,1},{1,0},{2,3},{3,2},{4,5},{5,4},{6,7},{7,6},{8,9},{9,8},{10,11... | collective-permute-start | bytes 491528 | tf_op jit(solution)/shard_map/ppermute | solution.py:396
  49.7 5.5 %collective-permute-start.26 = (bf16[96,384]{1,0:T(8,128)(2,1)S(1)}, bf16[96,384]{1,0:T(8,128)(2,1)S(1)}, u32[]{:S(2)}, u32[]{:S(2)}) collective-permute-start(bf16[96,384]{1,0:T(8,128)(2,1)S(1)} %get-tuple-element.105), channel_id=1, source_target_pairs={{0,4},{4,0},{8,12},{12,8},{1,5},{5,1},{9,13},{13,9},{2,6},{6,2},{1... | collective-permute-start | bytes 221192 | tf_op jit(solution)/shard_map/ppermute | solution.py:396
  49.8 9.2 %collective-permute-start.27 = (bf16[96,384]{1,0:T(8,128)(2,1)S(1)}, bf16[96,384]{1,0:T(8,128)(2,1)S(1)}, u32[]{:S(2)}, u32[]{:S(2)}) collective-permute-start(bf16[96,384]{1,0:T(8,128)(2,1)S(1)} %get-tuple-element.106), channel_id=1, source_target_pairs={{0,8},{4,12},{8,0},{12,4},{1,9},{5,13},{9,1},{13,5},{2,10},{6,14},... | collective-permute-start | bytes 221192 | tf_op jit(solution)/shard_map/ppermute | solution.py:396
  52.1 6.8 %collective-permute-start.28 = (bf16[96,384]{1,0:T(8,128)(2,1)S(1)}, bf16[96,384]{1,0:T(8,128)(2,1)S(1)}, u32[]{:S(2)}, u32[]{:S(2)}) collective-permute-start(bf16[96,384]{1,0:T(8,128)(2,1)S(1)} %get-tuple-element.107), channel_id=1, source_target_pairs={{0,12},{4,8},{8,4},{12,0},{1,13},{5,9},{9,5},{13,1},{2,14},{6,10},... | collective-permute-start | bytes 221192 | tf_op jit(solution)/shard_map/ppermute | solution.py:396
  59.0 4.4 %collective-permute-start.29 = (bf16[96,384]{1,0:T(8,128)(2,1)S(1)}, bf16[96,384]{1,0:T(8,128)(2,1)S(1)}, u32[]{:S(2)}, u32[]{:S(2)}) collective-permute-start(bf16[96,384]{1,0:T(8,128)(2,1)S(1)} %get-tuple-element.108), channel_id=1, source_target_pairs={{0,16},{16,0},{1,17},{17,1},{2,18},{18,2},{3,19},{19,3},{4,20},{20... | collective-permute-start | bytes 221192 | tf_op jit(solution)/shard_map/ppermute | solution.py:396

commit v7 on v6

--- a/solution.py
+++ b/solution.py
@@ -478,7 +478,7 @@
         in_specs=[VMEM] * n_z,
         out_specs=[VMEM] * 3,
         compiler_params=params(8 * MIB),
-        cost_estimate=pl.CostEstimate(flops=int(5e9), bytes_accessed=0, transcendentals=0),
+        cost_estimate=pl.CostEstimate(flops=int(3e10), bytes_accessed=0, transcendentals=0),
         name="lines",
     )(*qg_all[::-1])
     w, u, stat, own_part, *send = pl.pallas_call(

time: 64.4 us -> 64.4 us (level)
  no operation moved by 1% of the time
where the time goes in v7:
time: 64.4 us; the launch traced here: 64.2 us
  starting transfers between devices  31.4 us (49%)
  waiting for transfers between devices  20.3 us (32%)
  Pallas kernels  9.04 us (14%)
  local copies, waits for them, and re-layouts  1.37 us (2%)
  other arithmetic  1.14 us (2%)
  between operations  0.93 us (1%)
    ppermute x30, starting transfers between devices, xor_permute(): return lax.ppermute(value, tuple(names), pairs)  31.4 us
    ppermute x30, waiting for transfers between devices, xor_permute(): return lax.ppermute(value, tuple(names), pairs)  20.3 us
    pallas_call x1, Pallas kernels, local(): pl.pallas_call(functools.partial(forward_kernel, count, width, n_z, len(k...  2.26 us
    pallas_call x1, Pallas kernels, local(): pl.pallas_call(functools.partial(deal_kernel, (n_row, n_z, n_y, n_core)),...  1.87 us
  transfers between devices with their start and end apart: 30, of which 9 were waited for; matrix products, arithmetic and copies ran while one was open for 3% of the time, Pallas kernels for 10%

profile of v7, /device:TPU:0, one launch (start us, length us, event | category | flops | bytes accessed | tf_op | source)
XLA Modules:
  0.0 64.2 jit_solution(2831033588980323411)
XLA Ops:
  0.6 1.2 %pack.1 = (bf16[176,256]{1,0:T(8,128)(2,1)S(1)}, bf16[176,256]{1,0:T(8,128)(2,1)S(1)}) custom-call(bf16[160,128]{1,0:T(8,128)(2,1)} %q_hbm.1, bf16[160,128]{1,0:T(8,128)(2,1)} %k_hbm.1, bf16[160,128]{1,0:T(8,128)(2,1)} %v_hbm.1, bf16[160,128]{1,0:T(8,128)(2,1)} %o_hbm.1, bf16[160,128]{1,0:T(8,128)(2,1)} %g_hbm.1, s32[40,128]{1,0:T(8,128)} %bitcast.41, s32[40]{0:T(128)} %ids_hbm.1), custom_call_target="tpu_custom_call" | custom-call | tf_op jit(solution)/shard_map/pack/pallas_call | solution.py:421
  1.9 3.0 %collective-permute-start = (bf16[176,256]{1,0:T(8,128)(2,1)S(1)}, bf16[176,256]{1,0:T(8,128)(2,1)S(1)}, u32[]{:S(2)}, u32[]{:S(2)}) collective-permute-start(bf16[176,256]{1,0:T(8,128)(2,1)S(1)} %get-tuple-element.56), channel_id=1, source_target_pairs={{0,2},{2,0},{16,18},{18,16},{1,3},{3,1},{17,19},{19,17},{4,6},{6,4... | collective-permute-start | bytes 270344 | tf_op jit(solution)/shard_map/ppermute | solution.py:396
  4.9 1.5 %collective-permute-start.1 = (bf16[176,256]{1,0:T(8,128)(2,1)S(1)}, bf16[176,256]{1,0:T(8,128)(2,1)S(1)}, u32[]{:S(2)}, u32[]{:S(2)}) collective-permute-start(bf16[176,256]{1,0:T(8,128)(2,1)S(1)} %get-tuple-element.56), channel_id=1, source_target_pairs={{0,16},{2,18},{16,0},{18,2},{1,17},{3,19},{17,1},{19,3},{4,20},{6,... | collective-permute-start | bytes 270344 | tf_op jit(solution)/shard_map/ppermute | solution.py:396
  6.5 4.0 %collective-permute-start.3 = (bf16[176,256]{1,0:T(8,128)(2,1)S(1)}, bf16[176,256]{1,0:T(8,128)(2,1)S(1)}, u32[]{:S(2)}, u32[]{:S(2)}) collective-permute-start(bf16[176,256]{1,0:T(8,128)(2,1)S(1)} %get-tuple-element.59.refs_3_), channel_id=1, source_target_pairs={{0,12},{4,8},{8,4},{12,0},{1,13},{5,9},{9,5},{13,1},{2,14},{6,10},... | collective-permute-start | bytes 270344 | tf_op jit(solution)/shard_map/ppermute | solution.py:396
  10.5 0.6 collective-permute-start.5
  11.1 0.8 %collective-permute-done.2 = bf16[176,256]{1,0:T(8,128)(2,1)S(1)} collective-permute-done((bf16[176,256]{1,0:T(8,128)(2,1)S(1)}, bf16[176,256]{1,0:T(8,128)(2,1)S(1)}, u32[]{:S(2)}, u32[]{:S(2)}) %collective-permute-start.2) | collective-permute-done | bytes 90144 | tf_op jit(solution)/shard_map/ppermute | solution.py:396
  11.9 0.1 collective-permute-start.6
  12.0 1.9 %deal.1 = (bf16[2,160,384]{2,1,0:T(8,128)(2,1)S(1)}, bf16[2,160,384]{2,1,0:T(8,128)(2,1)S(1)}, bf16[2,160,384]{2,1,0:T(8,128)(2,1)S(1)}, bf16[2,160,384]{2,1,0:T(8,128)(2,1)S(1)}) custom-call(bf16[160,3072]{1,0:T(8,128)(2,1)} %x_hbm), custom_call_target="tpu_custom_call" | custom-call | tf_op jit(solution)/shard_map/deal/pallas_call | solution.py:455
  13.9 2.0 %collective-permute-start.10 = (bf16[2,160,384]{2,1,0:T(8,128)(2,1)S(1)}, bf16[2,160,384]{2,1,0:T(8,128)(2,1)S(1)}, u32[]{:S(2)}, u32[]{:S(2)}) collective-permute-start(bf16[2,160,384]{2,1,0:T(8,128)(2,1)S(1)} %get-tuple-element.72), channel_id=1, source_target_pairs={{0,18},{2,16},{16,2},{18,0},{1,19},{3,17},{17,3},{19,1},{4,22},{6,... | collective-permute-start | bytes 737288 | tf_op jit(solution)/shard_map/ppermute | solution.py:396
  15.8 1.4 %collective-permute-done.4.refs_1_ = bf16[176,256]{1,0:T(8,128)(2,1)S(1)} collective-permute-done((bf16[176,256]{1,0:T(8,128)(2,1)S(1)}, bf16[176,256]{1,0:T(8,128)(2,1)S(1)}, u32[]{:S(2)}, u32[]{:S(2)}) %collective-permute-start.4) | collective-permute-done | bytes 90144 | tf_op jit(solution)/shard_map/ppermute | solution.py:396
  17.3 0.1 lines.1
  17.4 2.3 %forward.1 = (bf16[8,160,640]{2,1,0:T(8,128)(2,1)S(1)}, bf16[8,160,640]{2,1,0:T(8,128)(2,1)S(1)}, f32[8,640]{1,0:T(8,128)S(1)}, bf16[160,128]{1,0:T(8,128)(2,1)S...) custom-call(bf16[640,128]{1,0:T(8,128)(2,1)S(1)} %get-tuple-element.60.refs_0_.refs_3_, ...), custom_call_target="tpu_custom_call" | custom-call | flops 30000001024 | tf_op jit(solution)/shard_map/forward/pallas_call | solution.py:484
  19.7 0.7 %collective-permute-start.7 = (bf16[192,128]{1,0:T(8,128)(2,1)S(1)}, bf16[192,128]{1,0:T(8,128)(2,1)S(1)}, u32[]{:S(2)}, u32[]{:S(2)}) collective-permute-start(bf16[192,128]{1,0:T(8,128)(2,1)S(1)} %get-tuple-element.69), channel_id=1, source_target_pairs={{0,4},{4,0},{8,12},{12,8},{1,5},{5,1},{9,13},{13,9},{2,6},{6,2},{1... | collective-permute-start | bytes 147464 | tf_op jit(solution)/shard_map/ppermute | solution.py:396
  20.4 2.4 %collective-permute-start.8 = (bf16[192,128]{1,0:T(8,128)(2,1)S(1)}, bf16[192,128]{1,0:T(8,128)(2,1)S(1)}, u32[]{:S(2)}, u32[]{:S(2)}) collective-permute-start(bf16[192,128]{1,0:T(8,128)(2,1)S(1)} %get-tuple-element.70), channel_id=1, source_target_pairs={{0,8},{4,12},{8,0},{12,4},{1,9},{5,13},{9,1},{13,5},{2,10},{6,14},... | collective-permute-start | bytes 147464 | tf_op jit(solution)/shard_map/ppermute | solution.py:396
  22.8 1.3 %collective-permute-start.9 = (bf16[192,128]{1,0:T(8,128)(2,1)S(1)}, bf16[192,128]{1,0:T(8,128)(2,1)S(1)}, u32[]{:S(2)}, u32[]{:S(2)}) collective-permute-start(bf16[192,128]{1,0:T(8,128)(2,1)S(1)} %get-tuple-element.71), channel_id=1, source_target_pairs={{0,12},{4,8},{8,4},{12,0},{1,13},{5,9},{9,5},{13,1},{2,14},{6,10},... | collective-permute-start | bytes 147464 | tf_op jit(solution)/shard_map/ppermute | solution.py:396
  24.1 1.5 %collective-permute-start.11 = (bf16[2,160,384]{2,1,0:T(8,128)(2,1)S(1)}, bf16[2,160,384]{2,1,0:T(8,128)(2,1)S(1)}, u32[]{:S(2)}, u32[]{:S(2)}) collective-permute-start(bf16[2,160,384]{2,1,0:T(8,128)(2,1)S(1)} %get-tuple-element.80), channel_id=1, source_target_pairs={{0,2},{2,0},{16,18},{18,16},{1,3},{3,1},{17,19},{19,17},{4,6},{6,4... | collective-permute-start | bytes 737288 | tf_op jit(solution)/shard_map/ppermute | solution.py:396
  25.7 1.5 %collective-permute-start.12 = (bf16[2,160,384]{2,1,0:T(8,128)(2,1)S(1)}, bf16[2,160,384]{2,1,0:T(8,128)(2,1)S(1)}, u32[]{:S(2)}, u32[]{:S(2)}) collective-permute-start(bf16[2,160,384]{2,1,0:T(8,128)(2,1)S(1)} %get-tuple-element.81), channel_id=1, source_target_pairs={{0,16},{2,18},{16,0},{18,2},{1,17},{3,19},{17,1},{19,3},{4,20},{6,... | collective-permute-start | bytes 737288 | tf_op jit(solution)/shard_map/ppermute | solution.py:396
  27.2 1.5 %collective-permute-done.9.refs_5_.refs_2_ = bf16[192,128]{1,0:T(8,128)(2,1)S(1)} collective-permute-done((bf16[192,128]{1,0:T(8,128)(2,1)S(1)}, bf16[192,128]{1,0:T(8,128)(2,1)S(1)}, u32[]{:S(2)}, u32[]{:S(2)}) %collective-permute-start.9) | collective-permute-done | bytes 49184 | tf_op jit(solution)/shard_map/ppermute | solution.py:396
  28.7 0.9 %away.1 = (bf16[4,160,128]{2,1,0:T(8,128)(2,1)S(1)}, bf16[4,160,128]{2,1,0:T(8,128)(2,1)S(1)}, bf16[640,128]{1,0:T(8,128)(2,1)S(1)}, bf16[640,128]{1,0:T(8,128)(2,1)S(1)}, f32[640,8]{1,0:T(8,128)S(1)}) custom-call(bf16[8,160,640]{2,1,0:T(8,128)(2,1)S(1)} %get-tuple-element.66.refs_0_.w_ref, bf16[8,160,640]{2,1,0:T(8,128)(2,1)S(1)} %get-tuple-element.67.refs_1_.u_ref, ...), custom_call_target="tpu_custom_call" | custom-call | flops 30000001024 | tf_op jit(solution)/shard_map/away/pallas_call | solution.py:522
  29.7 0.5 collective-permute-start.14
  30.2 0.6 home.1
  30.8 1.0 %collective-permute-done.12.refs_2_ = bf16[2,160,384]{2,1,0:T(8,128)(2,1)S(1)} collective-permute-done((bf16[2,160,384]{2,1,0:T(8,128)(2,1)S(1)}, bf16[2,160,384]{2,1,0:T(8,128)(2,1)S(1)}, u32[]{:S(2)}, u32[]{:S(2)}) %collective-permute-start.12) | collective-permute-done | bytes 245792 | tf_op jit(solution)/shard_map/ppermute | solution.py:396
  31.9 0.2 query.1
  32.2 1.6 %collective-permute-start.15 = (bf16[784,128]{1,0:T(8,128)(2,1)S(1)}, bf16[784,128]{1,0:T(8,128)(2,1)S(1)}, u32[]{:S(2)}, u32[]{:S(2)}) collective-permute-start(bf16[784,128]{1,0:T(8,128)(2,1)S(1)} %pad_maximum_fusion.2), channel_id=1, source_target_pairs={{0,16},{2,18},{16,0},{18,2},{1,17},{3,19},{17,1},{19,3},{4,20},{6,... | collective-permute-start | bytes 602120 | tf_op jit(solution)/shard_map/ppermute | solution.py:396
  33.7 0.8 %collective-permute-start.16 = (bf16[656,128]{1,0:T(8,128)(2,1)S(1)}, bf16[656,128]{1,0:T(8,128)(2,1)S(1)}, u32[]{:S(2)}, u32[]{:S(2)}) collective-permute-start(bf16[656,128]{1,0:T(8,128)(2,1)S(1)} %pad_maximum_fusion.4), channel_id=1, source_target_pairs={{0,2},{2,0},{16,18},{18,16},{1,3},{3,1},{17,19},{19,17},{4,6},{6,4... | collective-permute-start | bytes 503816 | tf_op jit(solution)/shard_map/ppermute | solution.py:396
  34.5 4.7 %collective-permute-done.16 = bf16[656,128]{1,0:T(8,128)(2,1)S(1)} collective-permute-done((bf16[656,128]{1,0:T(8,128)(2,1)S(1)}, bf16[656,128]{1,0:T(8,128)(2,1)S(1)}, u32[]{:S(2)}, u32[]{:S(2)}) %collective-permute-start.16) | collective-permute-done | bytes 167968 | tf_op jit(solution)/shard_map/ppermute | solution.py:396
  39.4 1.6 %collective-permute-start.17 = (bf16[928,128]{1,0:T(8,128)(2,1)S(1)}, bf16[928,128]{1,0:T(8,128)(2,1)S(1)}, u32[]{:S(2)}, u32[]{:S(2)}) collective-permute-start(bf16[928,128]{1,0:T(8,128)(2,1)S(1)} %pad_maximum_fusion.1), channel_id=1, source_target_pairs={{0,2},{2,0},{16,18},{18,16},{1,3},{3,1},{17,19},{19,17},{4,6},{6,4... | collective-permute-start | bytes 712712 | tf_op jit(solution)/shard_map/ppermute | solution.py:396
  41.0 1.0 %collective-permute-start.18 = (bf16[672,128]{1,0:T(8,128)(2,1)S(1)}, bf16[672,128]{1,0:T(8,128)(2,1)S(1)}, u32[]{:S(2)}, u32[]{:S(2)}) collective-permute-start(bf16[672,128]{1,0:T(8,128)(2,1)S(1)} %pad_maximum_fusion.3), channel_id=1, source_target_pairs={{0,16},{2,18},{16,0},{18,2},{1,17},{3,19},{17,1},{19,3},{4,20},{6,... | collective-permute-start | bytes 516104 | tf_op jit(solution)/shard_map/ppermute | solution.py:396
  42.0 0.5 collective-permute-start.20
  42.5 3.9 %collective-permute-done.18 = bf16[672,128]{1,0:T(8,128)(2,1)S(1)} collective-permute-done((bf16[672,128]{1,0:T(8,128)(2,1)S(1)}, bf16[672,128]{1,0:T(8,128)(2,1)S(1)}, u32[]{:S(2)}, u32[]{:S(2)}) %collective-permute-start.18) | collective-permute-done | bytes 172064 | tf_op jit(solution)/shard_map/ppermute | solution.py:396
  46.5 0.1 fusion.refs_6_
  46.6 0.6 collective-permute-start.25
  47.2 0.1 fusion.1.refs_5_
  47.3 0.1 collective-permute-start.24
  47.4 0.5 collective-permute-start.23
  47.9 0.5 near.1.near_ref
  48.4 0.6 dynamic-slice_bitcast_fusion
  49.1 0.6 far.1
  49.7 0.1 collective-permute-start.26
  49.8 2.4 %collective-permute-start.27 = (bf16[96,384]{1,0:T(8,128)(2,1)S(1)}, bf16[96,384]{1,0:T(8,128)(2,1)S(1)}, u32[]{:S(2)}, u32[]{:S(2)}) collective-permute-start(bf16[96,384]{1,0:T(8,128)(2,1)S(1)} %get-tuple-element.106), channel_id=1, source_target_pairs={{0,8},{4,12},{8,0},{12,4},{1,9},{5,13},{9,1},{13,5},{2,10},{6,14},... | collective-permute-start | bytes 221192 | tf_op jit(solution)/shard_map/ppermute | solution.py:396
  52.1 2.0 %collective-permute-start.28 = (bf16[96,384]{1,0:T(8,128)(2,1)S(1)}, bf16[96,384]{1,0:T(8,128)(2,1)S(1)}, u32[]{:S(2)}, u32[]{:S(2)}) collective-permute-start(bf16[96,384]{1,0:T(8,128)(2,1)S(1)} %get-tuple-element.107), channel_id=1, source_target_pairs={{0,12},{4,8},{8,4},{12,0},{1,13},{5,9},{9,5},{13,1},{2,14},{6,10},... | collective-permute-start | bytes 221192 | tf_op jit(solution)/shard_map/ppermute | solution.py:396
  54.1 0.6 dynamic-slice_bitcast_fusion.1
  54.7 0.4 collective-permute-done.26
  55.1 3.8 %collective-permute-done.27 = bf16[96,384]{1,0:T(8,128)(2,1)S(1)} collective-permute-done((bf16[96,384]{1,0:T(8,128)(2,1)S(1)}, bf16[96,384]{1,0:T(8,128)(2,1)S(1)}, u32[]{:S(2)}, u32[]{:S(2)}) %collective-permute-start.27) | collective-permute-done | bytes 73760 | tf_op jit(solution)/shard_map/ppermute | solution.py:396
  59.0 1.1 %collective-permute-start.29 = (bf16[96,384]{1,0:T(8,128)(2,1)S(1)}, bf16[96,384]{1,0:T(8,128)(2,1)S(1)}, u32[]{:S(2)}, u32[]{:S(2)}) collective-permute-start(bf16[96,384]{1,0:T(8,128)(2,1)S(1)} %get-tuple-element.108), channel_id=1, source_target_pairs={{0,16},{16,0},{1,17},{17,1},{2,18},{18,2},{3,19},{19,3},{4,20},{20... | collective-permute-start | bytes 221192 | tf_op jit(solution)/shard_map/ppermute | solution.py:396
  60.1 0.6 pad_maximum_fusion.5
  60.8 2.7 %collective-permute-done.29.refs_0_ = bf16[96,384]{1,0:T(8,128)(2,1)S(1)} collective-permute-done((bf16[96,384]{1,0:T(8,128)(2,1)S(1)}, bf16[96,384]{1,0:T(8,128)(2,1)S(1)}, u32[]{:S(2)}, u32[]{:S(2)}) %collective-permute-start.29) | collective-permute-done | bytes 73760 | tf_op jit(solution)/shard_map/ppermute | solution.py:396
  63.5 0.7 %assemble.1 = f32[2,96,384]{2,1,0:T(8,128)} custom-call(f32[96,384]{1,0:T(8,128)S(1)} %get-tuple-element.109.own_ref, bf16[96,384]{1,0:T(8,128)(2,1)S(1)} %collective-permute-done.29.refs_0_), custom_call_target="tpu_custom_call" | custom-call | tf_op jit(solution)/shard_map/assemble/pallas_call | solution.py:614
  (49 shorter events, 0.7 us)
Async XLA Ops:
  1.9 8.6 %collective-permute-start = (bf16[176,256]{1,0:T(8,128)(2,1)S(1)}, bf16[176,256]{1,0:T(8,128)(2,1)S(1)}, u32[]{:S(2)}, u32[]{:S(2)}) collective-permute-start(bf16[176,256]{1,0:T(8,128)(2,1)S(1)} %get-tuple-element.56), channel_id=1, source_target_pairs={{0,2},{2,0},{16,18},{18,16},{1,3},{3,1},{17,19},{19,17},{4,6},{6,4... | collective-permute-start | bytes 270344 | tf_op jit(solution)/shard_map/ppermute | solution.py:396
  4.9 6.1 %collective-permute-start.1 = (bf16[176,256]{1,0:T(8,128)(2,1)S(1)}, bf16[176,256]{1,0:T(8,128)(2,1)S(1)}, u32[]{:S(2)}, u32[]{:S(2)}) collective-permute-start(bf16[176,256]{1,0:T(8,128)(2,1)S(1)} %get-tuple-element.56), channel_id=1, source_target_pairs={{0,16},{2,18},{16,0},{18,2},{1,17},{3,19},{17,1},{19,3},{4,20},{6,... | collective-permute-start | bytes 270344 | tf_op jit(solution)/shard_map/ppermute | solution.py:396
  6.4 5.4 %collective-permute-start.2 = (bf16[176,256]{1,0:T(8,128)(2,1)S(1)}, bf16[176,256]{1,0:T(8,128)(2,1)S(1)}, u32[]{:S(2)}, u32[]{:S(2)}) collective-permute-start(bf16[176,256]{1,0:T(8,128)(2,1)S(1)} %get-tuple-element.56), channel_id=1, source_target_pairs={{0,18},{2,16},{16,2},{18,0},{1,19},{3,17},{17,3},{19,1},{4,22},{6,... | collective-permute-start | bytes 270344 | tf_op jit(solution)/shard_map/ppermute | solution.py:396
  6.5 9.4 %collective-permute-start.3 = (bf16[176,256]{1,0:T(8,128)(2,1)S(1)}, bf16[176,256]{1,0:T(8,128)(2,1)S(1)}, u32[]{:S(2)}, u32[]{:S(2)}) collective-permute-start(bf16[176,256]{1,0:T(8,128)(2,1)S(1)} %get-tuple-element.59.refs_3_), channel_id=1, source_target_pairs={{0,12},{4,8},{8,4},{12,0},{1,13},{5,9},{9,5},{13,1},{2,14},{6,10},... | collective-permute-start | bytes 270344 | tf_op jit(solution)/shard_map/ppermute | solution.py:396
  10.5 6.8 %collective-permute-start.4 = (bf16[176,256]{1,0:T(8,128)(2,1)S(1)}, bf16[176,256]{1,0:T(8,128)(2,1)S(1)}, u32[]{:S(2)}, u32[]{:S(2)}) collective-permute-start(bf16[176,256]{1,0:T(8,128)(2,1)S(1)} %get-tuple-element.59.refs_3_), channel_id=1, source_target_pairs={{0,8},{4,12},{8,0},{12,4},{1,9},{5,13},{9,1},{13,5},{2,10},{6,14},... | collective-permute-start | bytes 270344 | tf_op jit(solution)/shard_map/ppermute | solution.py:396
  10.5 6.8 %collective-permute-start.5 = (bf16[176,256]{1,0:T(8,128)(2,1)S(1)}, bf16[176,256]{1,0:T(8,128)(2,1)S(1)}, u32[]{:S(2)}, u32[]{:S(2)}) collective-permute-start(bf16[176,256]{1,0:T(8,128)(2,1)S(1)} %get-tuple-element.59.refs_3_), channel_id=1, source_target_pairs={{0,4},{4,0},{8,12},{12,8},{1,5},{5,1},{9,13},{13,9},{2,6},{6,2},{1... | collective-permute-start | bytes 270344 | tf_op jit(solution)/shard_map/ppermute | solution.py:396
  11.9 5.5 %collective-permute-start.6 = (bf16[4,176,256]{2,1,0:T(8,128)(2,1)S(1)}, bf16[4,176,256]{2,1,0:T(8,128)(2,1)S(1)}, u32[]{:S(2)}, u32[]{:S(2)}) collective-permute-start(bf16[4,176,256]{2,1,0:T(8,128)(2,1)S(1)} %pad_maximum_fusion), channel_id=1, source_target_pairs={{0,1},{1,0},{2,3},{3,2},{4,5},{5,4},{6,7},{7,6},{8,9},{9,8},{10,11... | collective-permute-start | bytes 1081352 | tf_op jit(solution)/shard_map/ppermute | solution.py:396
  13.9 11.8 %collective-permute-start.10 = (bf16[2,160,384]{2,1,0:T(8,128)(2,1)S(1)}, bf16[2,160,384]{2,1,0:T(8,128)(2,1)S(1)}, u32[]{:S(2)}, u32[]{:S(2)}) collective-permute-start(bf16[2,160,384]{2,1,0:T(8,128)(2,1)S(1)} %get-tuple-element.72), channel_id=1, source_target_pairs={{0,18},{2,16},{16,2},{18,0},{1,19},{3,17},{17,3},{19,1},{4,22},{6,... | collective-permute-start | bytes 737288 | tf_op jit(solution)/shard_map/ppermute | solution.py:396
  19.7 7.5 %collective-permute-start.7 = (bf16[192,128]{1,0:T(8,128)(2,1)S(1)}, bf16[192,128]{1,0:T(8,128)(2,1)S(1)}, u32[]{:S(2)}, u32[]{:S(2)}) collective-permute-start(bf16[192,128]{1,0:T(8,128)(2,1)S(1)} %get-tuple-element.69), channel_id=1, source_target_pairs={{0,4},{4,0},{8,12},{12,8},{1,5},{5,1},{9,13},{13,9},{2,6},{6,2},{1... | collective-permute-start | bytes 147464 | tf_op jit(solution)/shard_map/ppermute | solution.py:396
  20.4 6.8 %collective-permute-start.8 = (bf16[192,128]{1,0:T(8,128)(2,1)S(1)}, bf16[192,128]{1,0:T(8,128)(2,1)S(1)}, u32[]{:S(2)}, u32[]{:S(2)}) collective-permute-start(bf16[192,128]{1,0:T(8,128)(2,1)S(1)} %get-tuple-element.70), channel_id=1, source_target_pairs={{0,8},{4,12},{8,0},{12,4},{1,9},{5,13},{9,1},{13,5},{2,10},{6,14},... | collective-permute-start | bytes 147464 | tf_op jit(solution)/shard_map/ppermute | solution.py:396
  22.8 5.9 %collective-permute-start.9 = (bf16[192,128]{1,0:T(8,128)(2,1)S(1)}, bf16[192,128]{1,0:T(8,128)(2,1)S(1)}, u32[]{:S(2)}, u32[]{:S(2)}) collective-permute-start(bf16[192,128]{1,0:T(8,128)(2,1)S(1)} %get-tuple-element.71), channel_id=1, source_target_pairs={{0,12},{4,8},{8,4},{12,0},{1,13},{5,9},{9,5},{13,1},{2,14},{6,10},... | collective-permute-start | bytes 147464 | tf_op jit(solution)/shard_map/ppermute | solution.py:396
  24.1 6.7 %collective-permute-start.11 = (bf16[2,160,384]{2,1,0:T(8,128)(2,1)S(1)}, bf16[2,160,384]{2,1,0:T(8,128)(2,1)S(1)}, u32[]{:S(2)}, u32[]{:S(2)}) collective-permute-start(bf16[2,160,384]{2,1,0:T(8,128)(2,1)S(1)} %get-tuple-element.80), channel_id=1, source_target_pairs={{0,2},{2,0},{16,18},{18,16},{1,3},{3,1},{17,19},{19,17},{4,6},{6,4... | collective-permute-start | bytes 737288 | tf_op jit(solution)/shard_map/ppermute | solution.py:396
  25.7 6.2 %collective-permute-start.12 = (bf16[2,160,384]{2,1,0:T(8,128)(2,1)S(1)}, bf16[2,160,384]{2,1,0:T(8,128)(2,1)S(1)}, u32[]{:S(2)}, u32[]{:S(2)}) collective-permute-start(bf16[2,160,384]{2,1,0:T(8,128)(2,1)S(1)} %get-tuple-element.81), channel_id=1, source_target_pairs={{0,16},{2,18},{16,0},{18,2},{1,17},{3,19},{17,1},{19,3},{4,20},{6,... | collective-permute-start | bytes 737288 | tf_op jit(solution)/shard_map/ppermute | solution.py:396
  29.6 2.4 %collective-permute-start.13 = (bf16[4,160,128]{2,1,0:T(8,128)(2,1)S(1)}, bf16[4,160,128]{2,1,0:T(8,128)(2,1)S(1)}, u32[]{:S(2)}, u32[]{:S(2)}) collective-permute-start(bf16[4,160,128]{2,1,0:T(8,128)(2,1)S(1)} %get-tuple-element.89), channel_id=1, source_target_pairs={{0,1},{1,0},{2,3},{3,2},{4,5},{5,4},{6,7},{7,6},{8,9},{9,8},{10,11... | collective-permute-start | bytes 491528 | tf_op jit(solution)/shard_map/ppermute | solution.py:396
  29.7 2.3 %collective-permute-start.14 = (bf16[4,160,128]{2,1,0:T(8,128)(2,1)S(1)}, bf16[4,160,128]{2,1,0:T(8,128)(2,1)S(1)}, u32[]{:S(2)}, u32[]{:S(2)}) collective-permute-start(bf16[4,160,128]{2,1,0:T(8,128)(2,1)S(1)} %get-tuple-element.91), channel_id=1, source_target_pairs={{0,1},{1,0},{2,3},{3,2},{4,5},{5,4},{6,7},{7,6},{8,9},{9,8},{10,11... | collective-permute-start | bytes 491528 | tf_op jit(solution)/shard_map/ppermute | solution.py:396
  32.2 7.0 %collective-permute-start.15 = (bf16[784,128]{1,0:T(8,128)(2,1)S(1)}, bf16[784,128]{1,0:T(8,128)(2,1)S(1)}, u32[]{:S(2)}, u32[]{:S(2)}) collective-permute-start(bf16[784,128]{1,0:T(8,128)(2,1)S(1)} %pad_maximum_fusion.2), channel_id=1, source_target_pairs={{0,16},{2,18},{16,0},{18,2},{1,17},{3,19},{17,1},{19,3},{4,20},{6,... | collective-permute-start | bytes 602120 | tf_op jit(solution)/shard_map/ppermute | solution.py:396
  33.7 5.5 %collective-permute-start.16 = (bf16[656,128]{1,0:T(8,128)(2,1)S(1)}, bf16[656,128]{1,0:T(8,128)(2,1)S(1)}, u32[]{:S(2)}, u32[]{:S(2)}) collective-permute-start(bf16[656,128]{1,0:T(8,128)(2,1)S(1)} %pad_maximum_fusion.4), channel_id=1, source_target_pairs={{0,2},{2,0},{16,18},{18,16},{1,3},{3,1},{17,19},{19,17},{4,6},{6,4... | collective-permute-start | bytes 503816 | tf_op jit(solution)/shard_map/ppermute | solution.py:396
  39.4 7.0 %collective-permute-start.17 = (bf16[928,128]{1,0:T(8,128)(2,1)S(1)}, bf16[928,128]{1,0:T(8,128)(2,1)S(1)}, u32[]{:S(2)}, u32[]{:S(2)}) collective-permute-start(bf16[928,128]{1,0:T(8,128)(2,1)S(1)} %pad_maximum_fusion.1), channel_id=1, source_target_pairs={{0,2},{2,0},{16,18},{18,16},{1,3},{3,1},{17,19},{19,17},{4,6},{6,4... | collective-permute-start | bytes 712712 | tf_op jit(solution)/shard_map/ppermute | solution.py:396
  41.0 5.4 %collective-permute-start.18 = (bf16[672,128]{1,0:T(8,128)(2,1)S(1)}, bf16[672,128]{1,0:T(8,128)(2,1)S(1)}, u32[]{:S(2)}, u32[]{:S(2)}) collective-permute-start(bf16[672,128]{1,0:T(8,128)(2,1)S(1)} %pad_maximum_fusion.3), channel_id=1, source_target_pairs={{0,16},{2,18},{16,0},{18,2},{1,17},{3,19},{17,1},{19,3},{4,20},{6,... | collective-permute-start | bytes 516104 | tf_op jit(solution)/shard_map/ppermute | solution.py:396
  42.0 5.3 %collective-permute-start.19 = (bf16[2,160,384]{2,1,0:T(8,128)(2,1)S(1)}, bf16[2,160,384]{2,1,0:T(8,128)(2,1)S(1)}, u32[]{:S(2)}, u32[]{:S(2)}) collective-permute-start(bf16[2,160,384]{2,1,0:T(8,128)(2,1)S(1)} %get-tuple-element.58.refs_0_), channel_id=1, source_target_pairs={{0,1},{1,0},{2,3},{3,2},{4,5},{5,4},{6,7},{7,6},{8,9},{9,8},{10,11... | collective-permute-start | bytes 737288 | tf_op jit(solution)/shard_map/ppermute | solution.py:396
  42.0 5.4 %collective-permute-start.20 = (bf16[2,160,384]{2,1,0:T(8,128)(2,1)S(1)}, bf16[2,160,384]{2,1,0:T(8,128)(2,1)S(1)}, u32[]{:S(2)}, u32[]{:S(2)}) collective-permute-start(bf16[2,160,384]{2,1,0:T(8,128)(2,1)S(1)} %collective-permute-done.11.refs_1_), channel_id=1, source_target_pairs={{0,1},{1,0},{2,3},{3,2},{4,5},{5,4},{6,7},{7,6},{8,9},{9,8},{10,11... | collective-permute-start | bytes 737288 | tf_op jit(solution)/shard_map/ppermute | solution.py:396
  42.5 6.5 %collective-permute-start.21 = (bf16[2,160,384]{2,1,0:T(8,128)(2,1)S(1)}, bf16[2,160,384]{2,1,0:T(8,128)(2,1)S(1)}, u32[]{:S(2)}, u32[]{:S(2)}) collective-permute-start(bf16[2,160,384]{2,1,0:T(8,128)(2,1)S(1)} %collective-permute-done.12.refs_2_), channel_id=1, source_target_pairs={{0,1},{1,0},{2,3},{3,2},{4,5},{5,4},{6,7},{7,6},{8,9},{9,8},{10,11... | collective-permute-start | bytes 737288 | tf_op jit(solution)/shard_map/ppermute | solution.py:396
  46.4 2.6 %collective-permute-start.22 = (bf16[2,160,384]{2,1,0:T(8,128)(2,1)S(1)}, bf16[2,160,384]{2,1,0:T(8,128)(2,1)S(1)}, u32[]{:S(2)}, u32[]{:S(2)}) collective-permute-start(bf16[2,160,384]{2,1,0:T(8,128)(2,1)S(1)} %collective-permute-done.10.refs_3_), channel_id=1, source_target_pairs={{0,1},{1,0},{2,3},{3,2},{4,5},{5,4},{6,7},{7,6},{8,9},{9,8},{10,11... | collective-permute-start | bytes 737288 | tf_op jit(solution)/shard_map/ppermute | solution.py:396
  46.6 2.4 %collective-permute-start.25 = (bf16[4,160,128]{2,1,0:T(8,128)(2,1)S(1)}, bf16[4,160,128]{2,1,0:T(8,128)(2,1)S(1)}, u32[]{:S(2)}, u32[]{:S(2)}) collective-permute-start(bf16[4,160,128]{2,1,0:T(8,128)(2,1)S(1)} %fusion.refs_6_), channel_id=1, source_target_pairs={{0,1},{1,0},{2,3},{3,2},{4,5},{5,4},{6,7},{7,6},{8,9},{9,8},{10,11... | collective-permute-start | bytes 491528 | tf_op jit(solution)/shard_map/ppermute | solution.py:396
  47.3 1.7 %collective-permute-start.24 = (bf16[4,160,128]{2,1,0:T(8,128)(2,1)S(1)}, bf16[4,160,128]{2,1,0:T(8,128)(2,1)S(1)}, u32[]{:S(2)}, u32[]{:S(2)}) collective-permute-start(bf16[4,160,128]{2,1,0:T(8,128)(2,1)S(1)} %fusion.1.refs_5_), channel_id=1, source_target_pairs={{0,1},{1,0},{2,3},{3,2},{4,5},{5,4},{6,7},{7,6},{8,9},{9,8},{10,11... | collective-permute-start | bytes 491528 | tf_op jit(solution)/shard_map/ppermute | solution.py:396
  47.4 1.7 %collective-permute-start.23 = (bf16[640,128]{1,0:T(8,128)(2,1)S(1)}, bf16[640,128]{1,0:T(8,128)(2,1)S(1)}, u32[]{:S(2)}, u32[]{:S(2)}) collective-permute-start(bf16[640,128]{1,0:T(8,128)(2,1)S(1)} %constant_dynamic-update-slice_fusion.refs_4_), channel_id=1, source_target_pairs={{0,1},{1,0},{2,3},{3,2},{4,5},{5,4},{6,7},{7,6},{8,9},{9,8},{10,11... | collective-permute-start | bytes 491528 | tf_op jit(solution)/shard_map/ppermute | solution.py:396
  49.7 5.5 %collective-permute-start.26 = (bf16[96,384]{1,0:T(8,128)(2,1)S(1)}, bf16[96,384]{1,0:T(8,128)(2,1)S(1)}, u32[]{:S(2)}, u32[]{:S(2)}) collective-permute-start(bf16[96,384]{1,0:T(8,128)(2,1)S(1)} %get-tuple-element.105), channel_id=1, source_target_pairs={{0,4},{4,0},{8,12},{12,8},{1,5},{5,1},{9,13},{13,9},{2,6},{6,2},{1... | collective-permute-start | bytes 221192 | tf_op jit(solution)/shard_map/ppermute | solution.py:396
  49.8 9.2 %collective-permute-start.27 = (bf16[96,384]{1,0:T(8,128)(2,1)S(1)}, bf16[96,384]{1,0:T(8,128)(2,1)S(1)}, u32[]{:S(2)}, u32[]{:S(2)}) collective-permute-start(bf16[96,384]{1,0:T(8,128)(2,1)S(1)} %get-tuple-element.106), channel_id=1, source_target_pairs={{0,8},{4,12},{8,0},{12,4},{1,9},{5,13},{9,1},{13,5},{2,10},{6,14},... | collective-permute-start | bytes 221192 | tf_op jit(solution)/shard_map/ppermute | solution.py:396
  52.1 6.8 %collective-permute-start.28 = (bf16[96,384]{1,0:T(8,128)(2,1)S(1)}, bf16[96,384]{1,0:T(8,128)(2,1)S(1)}, u32[]{:S(2)}, u32[]{:S(2)}) collective-permute-start(bf16[96,384]{1,0:T(8,128)(2,1)S(1)} %get-tuple-element.107), channel_id=1, source_target_pairs={{0,12},{4,8},{8,4},{12,0},{1,13},{5,9},{9,5},{13,1},{2,14},{6,10},... | collective-permute-start | bytes 221192 | tf_op jit(solution)/shard_map/ppermute | solution.py:396
  59.0 4.4 %collective-permute-start.29 = (bf16[96,384]{1,0:T(8,128)(2,1)S(1)}, bf16[96,384]{1,0:T(8,128)(2,1)S(1)}, u32[]{:S(2)}, u32[]{:S(2)}) collective-permute-start(bf16[96,384]{1,0:T(8,128)(2,1)S(1)} %get-tuple-element.108), channel_id=1, source_target_pairs={{0,16},{16,0},{1,17},{17,1},{2,18},{18,2},{3,19},{19,3},{4,20},{20... | collective-permute-start | bytes 221192 | tf_op jit(solution)/shard_map/ppermute | solution.py:396
